TPU v7x, 32 devices: a whole 2x2x4 slice. The times are simulated.
32 devices in a mesh: cuts: 2 (over x), brick: 16 (over z, y, core).
Axes of the slice: x: 2, y: 2, z: 4, core: 2. Of those that a mesh axis runs over, the one named last changes fastest.
Arguments:
- eigen_vectors: float32 [64, 2, 3, 64, 512], P(None, None, None, ('cuts', 'brick')), parts along dimension 3, may hold values from -6 to 6
- link_field: float32 [3, 2, 3, 3, 64, 512], P(None, None, None, None, ('cuts', 'brick')), parts along dimension 4, may hold values from -3 to 3
- block_slot: int32 [63], replicated, may hold values from 0 to 63, as said below
Outputs:
- elementals: float32 [128, 32, 128], P(('cuts', 'brick')), parts along dimension 0
There are 2 independent parts, one for each index of `cuts`. A program takes and returns all parts, laid end to end along the dimension named above; an argument that names none is the same for every part. Nothing has to cross between parts.
Inputs may be any that keep to these rules, and one draw needn't show every extreme that they name: block_slot names distinct slots; slot s belongs to device s // 4 of the brick axis; in every draw some device has all 4 of its slots named.
All inputs are finite; a program needn't handle non-finite values.
Results may differ from a plain program's by a relative error of at most 0.0044.
Values sent between devices are 32-bit elements; how exact they have to be, the bound alone decides.
No kernel may reach another device: no remote copies, remote signals or barrier semaphores. Data moves between devices by JAX's collectives and lax.ppermute only.
A program may use at most 64 MiB of HBM per device.

v0:
```python
import functools
import math

import jax
import jax.numpy as jnp
import numpy as np
from jax import lax
from jax.experimental import pallas as pl
from jax.experimental.pallas import tpu as pltpu
from jax.sharding import PartitionSpec as P

PB = 32
CAP = 4
LX = 8
LANES = 128
ROWS = 8
VMEM = pl.BlockSpec(memory_space=pltpu.VMEM)
SMEM = pl.BlockSpec(memory_space=pltpu.SMEM)


def params(limit_mib):
    return pltpu.CompilerParams(vmem_limit_bytes=limit_mib * 1024 * 1024)


def cost(flops, bytes_accessed):
    return pl.CostEstimate(
        flops=int(flops), bytes_accessed=int(bytes_accessed), transcendentals=0
    )


def tile_rows(array):
    planes, sites = array.shape[-2:]
    tiles = sites // LANES
    lead = math.prod(array.shape[:-2])
    array = array.reshape(lead, planes, tiles, LANES).transpose(0, 2, 1, 3)
    return array.reshape(lead * tiles * planes, LANES)


def times(link, field, total):
    total = list(total)
    for out_row in range(3):
        for in_row in range(3):
            real, imag = link(0, out_row, in_row), link(1, out_row, in_row)
            f_real, f_imag = field[in_row], field[3 + in_row]
            total[out_row] = total[out_row] + real * f_real - imag * f_imag
            total[3 + out_row] = total[3 + out_row] + real * f_imag + imag * f_real
    return total


def adjoint(link, field, total):
    total = list(total)
    for out_row in range(3):
        for in_row in range(3):
            real, imag = link(0, in_row, out_row), link(1, in_row, out_row)
            f_real, f_imag = field[in_row], field[3 + in_row]
            total[out_row] = total[out_row] + real * f_real + imag * f_imag
            total[3 + out_row] = total[3 + out_row] + real * f_imag - imag * f_real
    return total


def link_row(part, row, column):
    return (part * 3 + row) * 3 + column


def split_kernel(tiles, chunk_tiles, place_ref, x_ref, *refs):
    outer, inner = refs[:-1], refs[-1]
    vectors = inner.shape[1]
    lower_core = place_ref[1] == 0
    for chunk, (first_tile, count) in enumerate(chunk_tiles):
        for part in range(6):
            for tile in range(first_tile, first_tile + count):
                start = (part * tiles + tile) * 2
                plane_0, plane_1 = (
                    x_ref[pl.ds(start + plane, vectors, stride=6 * tiles * 2), :]
                    for plane in range(2)
                )
                at = (tile - first_tile) * LANES
                outer[chunk][part, :, at : at + LANES] = jnp.where(lower_core, plane_0, plane_1)
                at = tile * LANES
                inner[part, :, at : at + LANES] = jnp.where(lower_core, plane_1, plane_0)


def link_kernel(tiles, place_ref, link_ref, plane_links, cross_links, top_links):
    lower_core = place_ref[1] == 0
    for index in range(36 * tiles):
        plane_0, plane_1 = (
            link_ref[index * 2 + plane : index * 2 + plane + 1, :] for plane in range(2)
        )
        plane_links[index : index + 1, :] = jnp.where(lower_core, plane_1, plane_0)
        index += 36 * tiles
        plane_links[index : index + 1, :] = jnp.where(lower_core, plane_0, plane_1)
    for part in range(2):
        for row in range(3):
            for column in range(3):
                for tile in range(tiles):
                    straight = ((36 + link_row(part, row, column)) * tiles + tile) * 2
                    turned = ((36 + link_row(part, column, row)) * tiles + tile) * 2
                    index = link_row(part, row, column) * tiles + tile
                    sign = -1.0 if part else 1.0
                    cross_links[index : index + 1, :] = jnp.where(
                        lower_core,
                        link_ref[straight : straight + 1, :],
                        sign * link_ref[turned : turned + 1, :],
                    )
                    top_links[index : index + 1, :] = link_ref[straight + 1 : straight + 2, :]


def z_link(top_links, low_links, tiles, tile, use_low):
    found = {}
    for part in range(2):
        for row in range(3):
            for column in range(3):
                straight = link_row(part, row, column) * tiles + tile
                turned = link_row(part, column, row) * tiles + tile
                sign = -1.0 if part else 1.0
                found[part, row, column] = jnp.where(
                    use_low,
                    sign * low_links[turned : turned + 1, :],
                    top_links[straight : straight + 1, :],
                )
    return lambda *index: found[index]


def local_kernel(tiles, chunk_tiles, plane_links, cross_links, inner, *refs):
    outer, (inner_out, outer_out) = refs[: len(chunk_tiles)], refs[len(chunk_tiles) :]
    vectors = inner.shape[1]
    lane = lax.broadcasted_iota(jnp.int32, (ROWS, LANES), 1)
    column = lane % LX
    first_column, last_column = column == 0, column == LX - 1
    below, above = lane < LX, lane >= LANES - LX
    zeros = [jnp.zeros((ROWS, LANES), jnp.float32)] * 6

    def step(group, carry):
        rows = pl.ds(pl.multiple_of(group * ROWS, ROWS), ROWS)

        def get(plane, tile):
            if plane == 0:
                ref, at = inner, tile * LANES
            else:
                for chunk, (first_tile, count) in enumerate(chunk_tiles):
                    if first_tile <= tile < first_tile + count:
                        ref, at = outer[chunk], (tile - first_tile) * LANES
            return [ref[part, rows, at : at + LANES] for part in range(6)]

        def link_of(direction, plane, tile):
            def link(part, row, column_at):
                index = plane * 36 + direction * 18 + link_row(part, row, column_at)
                index = index * tiles + tile
                return plane_links[index : index + 1, :]

            return link

        def cross_of(tile):
            def link(part, row, column_at):
                index = link_row(part, row, column_at) * tiles + tile
                return cross_links[index : index + 1, :]

            return link

        for plane in range(2):
            sums = []
            rolled_in = []
            rolled_out = []
            for tile in range(tiles):
                field = get(plane, tile)
                ahead = [
                    jnp.where(
                        last_column, pltpu.roll(f, LX - 1, 1), pltpu.roll(f, LANES - 1, 1)
                    )
                    for f in field
                ]
                behind = adjoint(link_of(0, plane, tile), field, zeros)
                total = [
                    jnp.where(
                        first_column, pltpu.roll(f, LANES - LX + 1, 1), pltpu.roll(f, 1, 1)
                    )
                    for f in behind
                ]
                total = times(link_of(0, plane, tile), ahead, total)
                if plane == 0:
                    total = adjoint(cross_of(tile), get(1, tile), total)
                else:
                    total = times(cross_of(tile), get(0, tile), total)
                sums.append(total)
                rolled_in.append([pltpu.roll(f, LANES - LX, 1) for f in field])
                rolled_out.append(
                    [
                        pltpu.roll(f, LX, 1)
                        for f in adjoint(link_of(1, plane, tile), field, zeros)
                    ]
                )
            for tile in range(tiles):
                after, before = (tile + 1) % tiles, (tile - 1) % tiles
                ahead = [
                    jnp.where(above, b, a) for a, b in zip(rolled_in[tile], rolled_in[after])
                ]
                total = times(link_of(1, plane, tile), ahead, sums[tile])
                lanes = slice(tile * LANES, (tile + 1) * LANES)
                for part in range(6):
                    back = jnp.where(below, rolled_out[before][part], rolled_out[tile][part])
                    out = outer_out if plane else inner_out
                    out[part, rows, lanes] = total[part] + back
        return carry

    lax.fori_loop(0, vectors // ROWS, step, 0)


def finish_hop(tiles, chunk, use_low, top_links, low_links, beyond, sums, out, finish):
    first_tile, count = chunk
    vectors = beyond.shape[1]
    for tile in range(count):
        link = z_link(top_links, low_links, tiles, first_tile + tile, use_low)
        lanes = slice(tile * LANES, (tile + 1) * LANES)
        at = (first_tile + tile) * LANES

        def step(group, carry):
            rows = pl.ds(pl.multiple_of(group * ROWS, ROWS), ROWS)
            field = [beyond[part, rows, lanes] for part in range(6)]
            total = [sums[part, rows, at : at + LANES] for part in range(6)]
            total = times(link, field, total)
            for part in range(6):
                out[part, rows, lanes] = finish(total[part], (part, rows, lanes))
            return carry

        lax.fori_loop(0, vectors // ROWS, step, 0, unroll=2)


def edge_kernel(tiles, chunk, low_core, place_ref, top_links, low_links, beyond, sums, *refs):
    finish_hop(
        tiles, chunk, place_ref[1] == low_core, top_links, low_links, beyond, sums, refs[-1],
        lambda total, index: total * (1.0 / 6.0),
    )


def pair_tiles(vectors):
    half = vectors // ROWS // 2
    return [
        (base + left, base + right)
        for base in (0, half)
        for left in range(half)
        for right in range(left, half)
    ]


def add_pairs(field, low, quarks, sums):
    vectors, width = field.shape[1:]
    for colour in range(3):
        real = field[colour].astype(jnp.bfloat16)
        imag = field[3 + colour].astype(jnp.bfloat16)
        for part, (top, bottom) in enumerate(((real, imag), (-imag, real))):
            at = (part * 3 + colour) * width
            low[:vectors, at : at + width] = top
            low[vectors:, at : at + width] = bottom

    combos = pair_tiles(vectors)
    block = ROWS * ROWS
    lefts = sorted({left for left, _ in combos})
    half = len(lefts) // 2
    steps = [lefts[:1], lefts[1:half], lefts[half : half + 1], lefts[half + 1 :]]

    def form(left):
        numbers = [number for number, combo in enumerate(combos) if combo[0] == left]
        for tile in range(width // LANES):
            at = tile * LANES
            lanes = slice(at, at + LANES)
            rights = [
                [
                    field[part, right * ROWS : (right + 1) * ROWS, lanes]
                    for part in range(6)
                ]
                for right in (combos[number][1] for number in numbers)
            ]
            for row in range(0, ROWS, 2):
                pair = [
                    [field[part, index : index + 1, lanes] for part in range(6)]
                    for index in (left * ROWS + row, left * ROWS + row + 1)
                ]
                for number, b in zip(numbers, rights):
                    made = [[] for _ in range(6)]
                    for a in pair:
                        for colour in range(3):
                            x, y = (colour + 1) % 3, (colour + 2) % 3
                            made[colour].append(
                                (a[x] * b[y] - a[3 + x] * b[3 + y])
                                - (a[y] * b[x] - a[3 + y] * b[3 + x])
                            )
                            made[3 + colour].append(
                                (a[x] * b[3 + y] + a[3 + x] * b[y])
                                - (a[y] * b[3 + x] + a[3 + y] * b[x])
                            )
                    start = number * block + row * ROWS
                    for part in range(6):
                        quarks[
                            start : start + 2 * ROWS,
                            part * width + at : part * width + at + LANES,
                        ] = jnp.concatenate(made[part], 0).astype(jnp.bfloat16)

    def multiply(step):
        numbers = [number for number, combo in enumerate(combos) if combo[0] in step]
        rows = slice(numbers[0] * block, (numbers[-1] + 1) * block)
        sums[rows, :] += lax.dot_general(
            quarks[rows, :],
            low[...],
            (((1,), (1,)), ((), ())),
            preferred_element_type=jnp.float32,
        )

    for left in steps[0]:
        form(left)
    for now, later in zip(steps, steps[1:] + [[]]):
        for left in later:
            form(left)
        multiply(now)


def inner_pairs_kernel(
    tiles, place_ref, top_links, low_links, partner, partial, own, sums, field, low, quarks
):
    finish_hop(
        tiles, (0, tiles), place_ref[1] == 1, top_links, low_links, partner, partial, field,
        lambda total, index: total * (2.0 / 6.0) - own[index],
    )
    sums[...] = jnp.zeros_like(sums)
    width = low.shape[1] // 6
    for start in range(0, field.shape[2], width):
        add_pairs(field.at[:, :, start : start + width], low, quarks, sums)


def outer_pairs_kernel(
    tiles, chunk, place_ref, top_links, low_links, far, partial, own, before, sums, field, low, quarks
):
    finish_hop(
        tiles, chunk, place_ref[1] == 0, top_links, low_links, far, partial, field,
        lambda total, index: total * (2.0 / 6.0) - own[index],
    )
    sums[...] = before[...]
    add_pairs(field, low, quarks, sums)


def arrange(sums, grid, crossed, ordered, factor):
    half = grid.shape[0] // 2
    side = math.isqrt(half)
    vectors = 2 * side
    block = ROWS * ROWS
    for number, (left, right) in enumerate(pair_tiles(vectors)):
        for row in range(ROWS):
            start = number * block + row * ROWS
            at = (left * ROWS + row) * side + right * ROWS % side
            grid[at : at + ROWS, :] = sums[start : start + ROWS, :] * factor
            if left != right:
                at = (right * ROWS + row) * side + left * ROWS % side
                grid[at : at + ROWS, :] = (
                    sums[pl.ds(number * block + row, ROWS, stride=ROWS), :] * -factor
                )
    lane = lax.broadcasted_iota(jnp.int32, (side, 2 * vectors), 1)
    own_half = lane % vectors < side
    per = 2 * vectors // side
    for start in range(0, half, 2 * vectors):
        turned = grid[half + start : half + start + 2 * vectors, :].T
        real, imag = turned[:side], turned[vectors : vectors + side]
        for index in range(per):
            second = start // side + index
            turn = (side - index * side) % (2 * vectors)
            value = jnp.where(
                lane < vectors,
                pltpu.roll(real, turn, 1) if turn else real,
                pltpu.roll(imag, (turn + vectors) % (2 * vectors), 1)
                if (turn + vectors) % (2 * vectors)
                else imag,
            )
            crossed[pl.ds(second, side, stride=side), :] = value
    for start in range(0, half, 2 * vectors):
        turned = grid[start : start + 2 * vectors, :].T
        real, imag = turned[side:vectors], turned[vectors + side :]
        for index in range(per):
            first = start // side + index
            turn = (-index * side) % (2 * vectors)
            value = jnp.where(
                lane < vectors,
                pltpu.roll(real, turn, 1) if turn else real,
                pltpu.roll(imag, (turn + vectors) % (2 * vectors), 1)
                if (turn + vectors) % (2 * vectors)
                else imag,
            )
            value = jnp.where(own_half, -value, crossed[first * side : (first + 1) * side, :])
            pair = first * vectors - first * (first + 1) // 2 + side - first - 1
            ordered[pair : pair + side, :] = value
    for first in range(vectors):
        skip = first % side + 1
        if skip < side:
            pair = first * vectors - first * (first + 1) // 2
            ordered[pair : pair + side - skip, :] = grid[
                first * side + skip : (first + 1) * side, :
            ]


def last_pairs_kernel(
    tiles, chunk, factor, slot_ref, place_ref, top_links, low_links, far, partial, own, before,
    keep, send, sums, field, low, quarks, grid, crossed, ordered,
):
    outer_pairs_kernel(
        tiles, chunk, place_ref, top_links, low_links, far, partial, own, before, sums, field, low,
        quarks,
    )
    arrange(sums, grid, crossed, ordered, factor)
    keep[...] = jnp.zeros_like(keep)
    send[...] = jnp.zeros_like(send)
    my_core = place_ref[1]

    def place(block, carry):
        slot = slot_ref[block]
        owner = slot // CAP
        chip = owner // 2
        value = ordered[pl.ds(pl.multiple_of(block * PB, PB), PB), :]

        @pl.when(owner % 2 == my_core)
        def _():
            keep[chip, slot % CAP] = value

        @pl.when(owner % 2 != my_core)
        def _():
            send[chip, slot % CAP] = value

        return carry

    lax.fori_loop(0, slot_ref.shape[0], place, 0)


def combine_kernel(keep, received, out):
    out[...] = keep[...] + received[...]


def total_kernel(arrived, out):
    total = arrived[0]
    for chip in range(1, arrived.shape[0]):
        total = total + arrived[chip]
    out[...] = total


def on_device(eigen_vectors, link_field, block_slot):
    count = lax.axis_size("brick")
    vectors, sites = eigen_vectors.shape[0], eigen_vectors.shape[-1]
    planes = eigen_vectors.shape[-2]
    tiles = sites // LANES
    half_tiles = tiles // 2
    chunk_tiles = ((0, half_tiles), (half_tiles, tiles - half_tiles))

    def plane_of(width):
        return jax.ShapeDtypeStruct((6, vectors, width), jnp.float32)

    plane = plane_of(sites)
    pieces = [plane_of(size * LANES) for _, size in chunk_tiles]
    plane_bytes = 6 * vectors * sites * 4
    pair_rows = len(pair_tiles(vectors)) * ROWS * ROWS
    up = [(i, (i + 1) % count) for i in range(count)]
    on_chip = [(i, i ^ 1) for i in range(count)]
    off_chip = [(i, (i + 2 * (i % 2) - 1) % count) for i in range(count)]
    me = lax.axis_index("brick")
    place = jnp.stack([me // 2, me % 2]).astype(jnp.int32)
    z_links = jax.ShapeDtypeStruct((18 * tiles, LANES), jnp.float32)

    plane_links, cross_links, top_links = pl.pallas_call(
        functools.partial(link_kernel, tiles),
        out_shape=[jax.ShapeDtypeStruct((72 * tiles, LANES), jnp.float32), z_links, z_links],
        in_specs=[SMEM, VMEM],
        out_specs=[VMEM] * 3,
        compiler_params=params(32),
        name="links",
    )(place, tile_rows(link_field))
    *outer, inner = pl.pallas_call(
        functools.partial(split_kernel, tiles, chunk_tiles),
        out_shape=pieces + [plane],
        in_specs=[SMEM, VMEM],
        out_specs=[VMEM] * (len(pieces) + 1),
        compiler_params=params(32),
        name="split",
    )(place, tile_rows(eigen_vectors))

    def off(fields):
        return [lax.ppermute(field, "brick", off_chip) for field in fields]

    def local_hops(inner, outer):
        return pl.pallas_call(
            functools.partial(local_kernel, tiles, chunk_tiles),
            out_shape=[plane] * 2,
            in_specs=[VMEM] * (3 + len(pieces)),
            out_specs=[VMEM] * 2,
            compiler_params=params(48),
            cost_estimate=cost(5e9, 4 * plane_bytes),
            name="local",
        )(plane_links, cross_links, inner, *outer)

    def edge(chunk, low_core, shape, *args):
        return pl.pallas_call(
            functools.partial(edge_kernel, tiles, chunk, low_core),
            out_shape=shape,
            in_specs=[SMEM] + [VMEM] * (2 + len(args)),
            out_specs=VMEM,
            compiler_params=params(32),
            name="edge",
        )(place, top_links, low_links, *args)

    far = off(outer)
    low_links = lax.ppermute(top_links, "brick", up)
    partner = lax.ppermute(inner, "brick", on_chip)
    inner_sums, outer_sums = local_hops(inner, outer)
    first_inner = edge((0, tiles), 1, plane, partner, inner_sums)
    partner = lax.ppermute(first_inner, "brick", on_chip)
    token = sum(field[0, :ROWS, :LANES] for field in far)
    token = lax.ppermute(token, "brick", on_chip)
    first_outer = [
        edge(chunk, 0, piece, field, outer_sums, token)
        for chunk, piece, field in zip(chunk_tiles, pieces, far)
    ]
    far = off(first_outer)
    inner_sums, sums = local_hops(first_inner, first_outer)

    def scratch(width):
        return [
            pltpu.VMEM((2 * vectors, 6 * width), jnp.bfloat16),
            pltpu.VMEM((pair_rows, 6 * width), jnp.bfloat16),
        ]

    partial_sums = jax.ShapeDtypeStruct((pair_rows, 2 * vectors), jnp.float32)
    before = pl.pallas_call(
        functools.partial(inner_pairs_kernel, tiles),
        out_shape=partial_sums,
        in_specs=[SMEM] + [VMEM] * 5,
        out_specs=VMEM,
        scratch_shapes=[pltpu.VMEM(plane.shape, jnp.float32)] + scratch(2 * LANES),
        compiler_params=params(48),
        cost_estimate=cost(8e9, 6 * plane_bytes),
        name="inner_pairs",
    )(place, top_links, low_links, partner, inner_sums, inner)
    for chunk, piece, field, own in zip(chunk_tiles[:-1], pieces, far, outer):
        before = pl.pallas_call(
            functools.partial(outer_pairs_kernel, tiles, chunk),
            out_shape=partial_sums,
            in_specs=[SMEM] + [VMEM] * 6,
            out_specs=VMEM,
            scratch_shapes=[pltpu.VMEM(piece.shape, jnp.float32)] + scratch(piece.shape[2]),
            compiler_params=params(48),
            cost_estimate=cost(4e9, 3 * plane_bytes),
            name="outer_pairs",
        )(place, top_links, low_links, field, sums, own, before)
    factor = 1.0 / math.sqrt(3.0 * sites * planes * count)
    chips = count // 2
    half = jax.ShapeDtypeStruct((chips, CAP, PB, 2 * vectors), jnp.float32)
    blocks = vectors * (vectors - 1) // 2
    keep, send = pl.pallas_call(
        functools.partial(last_pairs_kernel, tiles, chunk_tiles[-1], factor),
        out_shape=[half] * 2,
        in_specs=[SMEM] * 2 + [VMEM] * 6,
        out_specs=[VMEM] * 2,
        scratch_shapes=[
            pltpu.VMEM(partial_sums.shape, jnp.float32),
            pltpu.VMEM(pieces[-1].shape, jnp.float32),
        ]
        + scratch(pieces[-1].shape[2])
        + [
            pltpu.VMEM((vectors * vectors // 2, 2 * vectors), jnp.float32),
            pltpu.VMEM((vectors * vectors // 4, 2 * vectors), jnp.float32),
            pltpu.VMEM((blocks, 2 * vectors), jnp.float32),
        ],
        compiler_params=params(48),
        cost_estimate=cost(4e9, 3 * plane_bytes),
        name="last_pairs",
    )(block_slot, place, top_links, low_links, far[-1], sums, outer[-1], before)
    received = lax.ppermute(send, "brick", on_chip)
    share = jax.ShapeDtypeStruct((CAP, PB, 2 * vectors), jnp.float32)
    shares = pl.pallas_call(
        combine_kernel,
        out_shape=half,
        in_specs=[VMEM] * 2,
        out_specs=VMEM,
        compiler_params=params(32),
        name="combine",
    )(keep, received)
    arrived = lax.all_to_all(
        shares,
        "brick",
        0,
        0,
        axis_index_groups=[list(range(core, count, 2)) for core in range(2)],
        tiled=True,
    )
    return pl.pallas_call(
        total_kernel,
        out_shape=share,
        in_specs=[VMEM],
        out_specs=VMEM,
        compiler_params=params(32),
        name="total",
    )(arrived)


def solution(mesh):
    return jax.shard_map(
        on_device,
        mesh=mesh,
        in_specs=(
            P(None, None, None, ("cuts", "brick"), None),
            P(None, None, None, None, ("cuts", "brick"), None),
            P(),
        ),
        out_specs=P(("cuts", "brick"), None, None),
        check_vma=False,
    )
```

profile of v0, /device:TPU:0, one launch (start us, length us, event | category | flops | bytes accessed | tf_op | source)
XLA Modules:
  0.0 80.9 jit_solution(13042693884771832648)
XLA Ops:
  0.0 0.1 pad_add_fusion.place_ref
  0.1 0.0 copy-start
  0.1 1.4 %copy-done = f32[64,2,3,2,512]{4,3,2,1,0:T(2,128)S(1)} copy-done((f32[64,2,3,2,512]{4,3,2,1,0:T(2,128)S(1)}, f32[64,2,3,2,512]{4,3,2,1,0:T(2,128)}, u32[]{:S(2)}) %copy-start) | copy-done | bytes 1572888
  1.5 0.0 copy-start.1
  1.5 1.0 %split.1 = (f32[6,64,256]{2,1,0:T(8,128)S(1)}, f32[6,64,256]{2,1,0:T(8,128)S(1)}, f32[6,64,512]{2,1,0:T(8,128)S(1)}) custom-call(s32[2]{0:T(128)S(1)} %pad_add_fusion.place_ref, f32[3072,128]{1,0:T(8,128)S(1)} %bitcast.14), custom_call_target="tpu_custom_call" | custom-call | tf_op jit(solution)/shard_map/split/pallas_call | solution.py:470
  2.5 0.5 collective-permute-start.5
  3.0 5.7 %collective-permute-start.1 = (f32[6,64,256]{2,1,0:T(8,128)S(1)}, f32[6,64,256]{2,1,0:T(8,128)S(1)}, u32[]{:S(2)}, u32[]{:S(2)}) collective-permute-start(f32[6,64,256]{2,1,0:T(8,128)S(1)} %get-tuple-element.18.refs_1_.own), channel_id=1, source_target_pairs={{0,15},{1,2},{2,1},{3,4},{4,3},{5,6},{6,5},{7,8},{8,7},{9,10},{10,... | collective-permute-start | bytes 1179656 | tf_op jit(solution)/shard_map/ppermute | solution.py:480
  8.7 0.0 collective-permute-start.2
  8.7 0.0 copy-done.1
  8.7 0.7 links.1
  9.4 0.1 collective-permute-start
  9.5 4.0 %local.2 = (f32[6,64,512]{2,1,0:T(8,128)S(1)}, f32[6,64,512]{2,1,0:T(8,128)S(1)}) custom-call(f32[288,128]{1,0:T(8,128)S(1)} %get-tuple-element.19.plane_links, f32[72,128]{1,0:T(8,128)S(1)} %get-tuple-element.20.cross_links, f32[6,64,512]{2,1,0:T(8,128)S(1)} %get-tuple-element.21.inner.own, f32[6,64,256]{2,1,0:T(8,128)S(1)} %get-tuple-element.22.refs_0_.own, ...), custom_call_target="tpu_custom_call" | custom-call | flops 5000000000 | bytes 3145728 | tf_op jit(solution)/shard_map/local/pallas_call | solution.py:483
  13.5 5.5 %collective-permute-done.low_links = f32[72,128]{1,0:T(8,128)S(1)} collective-permute-done((f32[72,128]{1,0:T(8,128)S(1)}, f32[72,128]{1,0:T(8,128)S(1)}, u32[]{:S(2)}, u32[]{:S(2)}) %collective-permute-start) | collective-permute-done | bytes 36896 | tf_op jit(solution)/shard_map/ppermute | solution.py:504
  19.0 0.0 collective-permute-done.5.beyond
  19.0 1.1 %edge.4.inner = f32[6,64,512]{2,1,0:T(8,128)S(1)} custom-call(s32[2]{0:T(128)S(1)} %pad_add_fusion.place_ref, f32[72,128]{1,0:T(8,128)S(1)} %get-tuple-element.17.top_links, f32[72,128]{1,0:T(8,128)S(1)} %collective-permute-done.low_links, f32[6,64,512]{2,1,0:T(8,128)S(1)} %collective-permute-done.5.beyond, f32[6,64,512]{2,1,0:T(8,128)S(1)} %get-tuple-element.24.sums), custom_call_target="tpu_custom_call" | custom-call | tf_op jit(solution)/shard_map/edge/pallas_call | solution.py:494
  20.2 4.5 %collective-permute-start.7 = (f32[6,64,512]{2,1,0:T(8,128)S(1)}, f32[6,64,512]{2,1,0:T(8,128)S(1)}, u32[]{:S(2)}, u32[]{:S(2)}) collective-permute-start(f32[6,64,512]{2,1,0:T(8,128)S(1)} %edge.4.inner), channel_id=1, source_target_pairs={{0,1},{1,0},{2,3},{3,2},{4,5},{5,4},{6,7},{7,6},{8,9},{9,8},{10,11... | collective-permute-start | bytes 2359304 | tf_op jit(solution)/shard_map/ppermute | solution.py:508
  24.7 0.0 collective-permute-done.1.beyond
  24.7 0.0 collective-permute-done.2.beyond
  24.7 0.1 collective-permute-start.3
  24.8 1.8 %collective-permute-done.3.refs_0_ = f32[8,128]{1,0:T(8,128)S(1)} collective-permute-done((f32[8,128]{1,0:T(8,128)S(1)}, f32[8,128]{1,0:T(8,128)S(1)}, u32[]{:S(2)}, u32[]{:S(2)}) %collective-permute-start.3) | collective-permute-done | bytes 4128 | tf_op jit(solution)/shard_map/ppermute | solution.py:510
  26.6 0.8 %edge.5.refs_0_ = f32[6,64,256]{2,1,0:T(8,128)S(1)} custom-call(s32[2]{0:T(128)S(1)} %pad_add_fusion.place_ref, f32[72,128]{1,0:T(8,128)S(1)} %get-tuple-element.17.top_links, f32[72,128]{1,0:T(8,128)S(1)} %collective-permute-done.low_links, f32[6,64,256]{2,1,0:T(8,128)S(1)} %collective-permute-done.2.beyond, f32[6,64,512]{2,1,0:T(8,128)S(1)} %get-tuple-element.23.sums, ...), custom_call_target="tpu_custom_call" | custom-call | tf_op jit(solution)/shard_map/edge/pallas_call | solution.py:494
  27.4 5.6 %collective-permute-start.6 = (f32[6,64,256]{2,1,0:T(8,128)S(1)}, f32[6,64,256]{2,1,0:T(8,128)S(1)}, u32[]{:S(2)}, u32[]{:S(2)}) collective-permute-start(f32[6,64,256]{2,1,0:T(8,128)S(1)} %edge.5.refs_0_), channel_id=1, source_target_pairs={{0,15},{1,2},{2,1},{3,4},{4,3},{5,6},{6,5},{7,8},{8,7},{9,10},{10,... | collective-permute-start | bytes 1179656 | tf_op jit(solution)/shard_map/ppermute | solution.py:480
  33.0 0.8 %edge.3.refs_1_ = f32[6,64,256]{2,1,0:T(8,128)S(1)} custom-call(s32[2]{0:T(128)S(1)} %pad_add_fusion.place_ref, f32[72,128]{1,0:T(8,128)S(1)} %get-tuple-element.17.top_links, f32[72,128]{1,0:T(8,128)S(1)} %collective-permute-done.low_links, f32[6,64,256]{2,1,0:T(8,128)S(1)} %collective-permute-done.1.beyond, f32[6,64,512]{2,1,0:T(8,128)S(1)} %get-tuple-element.23.sums, ...), custom_call_target="tpu_custom_call" | custom-call | tf_op jit(solution)/shard_map/edge/pallas_call | solution.py:494
  33.8 0.1 collective-permute-start.4
  33.9 4.1 %local.3 = (f32[6,64,512]{2,1,0:T(8,128)S(1)}, f32[6,64,512]{2,1,0:T(8,128)S(1)}) custom-call(f32[288,128]{1,0:T(8,128)S(1)} %get-tuple-element.19.plane_links, f32[72,128]{1,0:T(8,128)S(1)} %get-tuple-element.20.cross_links, f32[6,64,512]{2,1,0:T(8,128)S(1)} %edge.4.inner, f32[6,64,256]{2,1,0:T(8,128)S(1)} %edge.5.refs_0_, f32[6,64,256]{2,1,0:T(8,128)S(1)} %edge.3.refs_1_), custom_call_target="tpu_custom_call" | custom-call | flops 5000000000 | bytes 3145728 | tf_op jit(solution)/shard_map/local/pallas_call | solution.py:483
  38.0 0.0 collective-permute-done.7.partner
  38.0 8.2 %inner_pairs.1.before = f32[1280,128]{1,0:T(8,128)S(1)} custom-call(s32[2]{0:T(128)S(1)} %pad_add_fusion.place_ref, f32[72,128]{1,0:T(8,128)S(1)} %get-tuple-element.17.top_links, f32[72,128]{1,0:T(8,128)S(1)} %collective-permute-done.low_links, f32[6,64,512]{2,1,0:T(8,128)S(1)} %collective-permute-done.7.partner, ...), custom_call_target="tpu_custom_call" | custom-call | flops 8000000000 | bytes 4718592 | tf_op jit(solution)/shard_map/inner_pairs/pallas_call | solution.py:525
  46.2 0.0 collective-permute-done.6.far
  46.2 0.0 copy-start.2
  46.2 4.2 %outer_pairs.1.before = f32[1280,128]{1,0:T(8,128)S(1)} custom-call(s32[2]{0:T(128)S(1)} %pad_add_fusion.place_ref, f32[72,128]{1,0:T(8,128)S(1)} %get-tuple-element.17.top_links, f32[72,128]{1,0:T(8,128)S(1)} %collective-permute-done.low_links, f32[6,64,256]{2,1,0:T(8,128)S(1)} %collective-permute-done.6.far, f32[6,64,512]{2,1,0:T(8,128)S(1)} %get-tuple-element.25.partial, ...), custom_call_target="tpu_custom_call" | custom-call | flops 4000000000 | bytes 2359296 | tf_op jit(solution)/shard_map/outer_pairs/pallas_call | solution.py:536
  50.4 0.0 collective-permute-done.4.far
  50.5 0.0 copy-done.2
  50.5 7.2 %last_pairs.1 = (f32[8,4,32,128]{3,2,1,0:T(8,128)S(1)}, f32[8,4,32,128]{3,2,1,0:T(8,128)S(1)}) custom-call(s32[63]{0:T(128)S(1)} %copy-done.2, s32[2]{0:T(128)S(1)} %pad_add_fusion.place_ref, f32[72,128]{1,0:T(8,128)S(1)} %get-tuple-element.17.top_links, f32[72,128]{1,0:T(8,128)S(1)} %collective-permute-done.low_links, ...), custom_call_target="tpu_custom_call" | custom-call | flops 4000000000 | bytes 2359296 | tf_op jit(solution)/shard_map/last_pairs/pallas_call | solution.py:550
  57.6 0.1 collective-permute-start.8
  57.7 1.9 %collective-permute-done.8.received = f32[8,4,32,128]{3,2,1,0:T(8,128)S(1)} collective-permute-done((f32[8,4,32,128]{3,2,1,0:T(8,128)S(1)}, f32[8,4,32,128]{3,2,1,0:T(8,128)S(1)}, u32[]{:S(2)}, u32[]{:S(2)}) %collective-permute-start.8) | collective-permute-done | bytes 524320 | tf_op jit(solution)/shard_map/ppermute | solution.py:569
  59.6 0.1 combine.1
  59.7 20.5 %all_to_all.5.arrived = f32[8,4,32,128]{3,2,1,0:T(8,128)S(1)} all-to-all(f32[8,4,32,128]{3,2,1,0:T(8,128)S(1)} %combine.1), channel_id=1, replica_groups={{0,2,4,6,8,10,12,14},{1,3,5,7,9,11,13,15},{16,18,20,22,24,26,28,30},{17..., dimensions={0} | all-to-all | bytes 1048576 | tf_op jit(solution)/shard_map/all_to_all | solution.py:579
  80.2 0.7 total.1
  (1 shorter events, 0.0 us)
Async XLA Ops:
  0.1 1.4 %copy-start = (f32[64,2,3,2,512]{4,3,2,1,0:T(2,128)S(1)}, f32[64,2,3,2,512]{4,3,2,1,0:T(2,128)}, u32[]{:S(2)}) copy-start(f32[64,2,3,2,512]{4,3,2,1,0:T(2,128)} %param.3) | copy-start | bytes 4718596
  1.5 7.2 %copy-start.1 = (f32[3,2,3,3,2,512]{5,4,3,2,1,0:T(2,128)S(1)}, f32[3,2,3,3,2,512]{5,4,3,2,1,0:T(2,128)}, u32[]{:S(2)}) copy-start(f32[3,2,3,3,2,512]{5,4,3,2,1,0:T(2,128)} %param.4) | copy-start | bytes 663556
  2.5 16.5 %collective-permute-start.5 = (f32[6,64,512]{2,1,0:T(8,128)S(1)}, f32[6,64,512]{2,1,0:T(8,128)S(1)}, u32[]{:S(2)}, u32[]{:S(2)}) collective-permute-start(f32[6,64,512]{2,1,0:T(8,128)S(1)} %get-tuple-element.21.inner.own), channel_id=1, source_target_pairs={{0,1},{1,0},{2,3},{3,2},{4,5},{5,4},{6,7},{7,6},{8,9},{9,8},{10,11... | collective-permute-start | bytes 2359304 | tf_op jit(solution)/shard_map/ppermute | solution.py:505
  3.0 21.7 %collective-permute-start.1 = (f32[6,64,256]{2,1,0:T(8,128)S(1)}, f32[6,64,256]{2,1,0:T(8,128)S(1)}, u32[]{:S(2)}, u32[]{:S(2)}) collective-permute-start(f32[6,64,256]{2,1,0:T(8,128)S(1)} %get-tuple-element.18.refs_1_.own), channel_id=1, source_target_pairs={{0,15},{1,2},{2,1},{3,4},{4,3},{5,6},{6,5},{7,8},{8,7},{9,10},{10,... | collective-permute-start | bytes 1179656 | tf_op jit(solution)/shard_map/ppermute | solution.py:480
  8.7 16.0 %collective-permute-start.2 = (f32[6,64,256]{2,1,0:T(8,128)S(1)}, f32[6,64,256]{2,1,0:T(8,128)S(1)}, u32[]{:S(2)}, u32[]{:S(2)}) collective-permute-start(f32[6,64,256]{2,1,0:T(8,128)S(1)} %get-tuple-element.22.refs_0_.own), channel_id=1, source_target_pairs={{0,15},{1,2},{2,1},{3,4},{4,3},{5,6},{6,5},{7,8},{8,7},{9,10},{10,... | collective-permute-start | bytes 1179656 | tf_op jit(solution)/shard_map/ppermute | solution.py:480
  9.4 9.6 %collective-permute-start = (f32[72,128]{1,0:T(8,128)S(1)}, f32[72,128]{1,0:T(8,128)S(1)}, u32[]{:S(2)}, u32[]{:S(2)}) collective-permute-start(f32[72,128]{1,0:T(8,128)S(1)} %get-tuple-element.17.top_links), channel_id=1, source_target_pairs={{0,1},{1,2},{2,3},{3,4},{4,5},{5,6},{6,7},{7,8},{8,9},{9,10},{10,1... | collective-permute-start | bytes 110600 | tf_op jit(solution)/shard_map/ppermute | solution.py:504
  20.2 17.8 %collective-permute-start.7 = (f32[6,64,512]{2,1,0:T(8,128)S(1)}, f32[6,64,512]{2,1,0:T(8,128)S(1)}, u32[]{:S(2)}, u32[]{:S(2)}) collective-permute-start(f32[6,64,512]{2,1,0:T(8,128)S(1)} %edge.4.inner), channel_id=1, source_target_pairs={{0,1},{1,0},{2,3},{3,2},{4,5},{5,4},{6,7},{7,6},{8,9},{9,8},{10,11... | collective-permute-start | bytes 2359304 | tf_op jit(solution)/shard_map/ppermute | solution.py:508
  24.7 1.9 %collective-permute-start.3 = (f32[8,128]{1,0:T(8,128)S(1)}, f32[8,128]{1,0:T(8,128)S(1)}, u32[]{:S(2)}, u32[]{:S(2)}) collective-permute-start(f32[8,128]{1,0:T(8,128)S(1)} %fusion), channel_id=1, source_target_pairs={{0,1},{1,0},{2,3},{3,2},{4,5},{5,4},{6,7},{7,6},{8,9},{9,8},{10,11... | collective-permute-start | bytes 12296 | tf_op jit(solution)/shard_map/ppermute | solution.py:510
  27.4 18.8 %collective-permute-start.6 = (f32[6,64,256]{2,1,0:T(8,128)S(1)}, f32[6,64,256]{2,1,0:T(8,128)S(1)}, u32[]{:S(2)}, u32[]{:S(2)}) collective-permute-start(f32[6,64,256]{2,1,0:T(8,128)S(1)} %edge.5.refs_0_), channel_id=1, source_target_pairs={{0,15},{1,2},{2,1},{3,4},{4,3},{5,6},{6,5},{7,8},{8,7},{9,10},{10,... | collective-permute-start | bytes 1179656 | tf_op jit(solution)/shard_map/ppermute | solution.py:480
  33.8 16.6 %collective-permute-start.4 = (f32[6,64,256]{2,1,0:T(8,128)S(1)}, f32[6,64,256]{2,1,0:T(8,128)S(1)}, u32[]{:S(2)}, u32[]{:S(2)}) collective-permute-start(f32[6,64,256]{2,1,0:T(8,128)S(1)} %edge.3.refs_1_), channel_id=1, source_target_pairs={{0,15},{1,2},{2,1},{3,4},{4,3},{5,6},{6,5},{7,8},{8,7},{9,10},{10,... | collective-permute-start | bytes 1179656 | tf_op jit(solution)/shard_map/ppermute | solution.py:480
  46.2 4.2 %copy-start.2 = (s32[63]{0:T(128)S(1)}, s32[63]{0:T(128)}, u32[]{:S(2)}) copy-start(s32[63]{0:T(128)} %slot_ref.1) | copy-start | bytes 760
  57.6 2.0 %collective-permute-start.8 = (f32[8,4,32,128]{3,2,1,0:T(8,128)S(1)}, f32[8,4,32,128]{3,2,1,0:T(8,128)S(1)}, u32[]{:S(2)}, u32[]{:S(2)}) collective-permute-start(f32[8,4,32,128]{3,2,1,0:T(8,128)S(1)} %get-tuple-element.28), channel_id=1, source_target_pairs={{0,1},{1,0},{2,3},{3,2},{4,5},{5,4},{6,7},{7,6},{8,9},{9,8},{10,11... | collective-permute-start | bytes 1572872 | tf_op jit(solution)/shard_map/ppermute | solution.py:569
where the time goes:
time: 81 us; the launch traced here: 80.9 us
  Pallas kernels  32.8 us (40%)
  blocking collectives  20.5 us (25%)
  starting transfers between devices  16.6 us (20%)
  waiting for transfers between devices  9.23 us (11%)
  local copies, waits for them, and re-layouts  1.42 us (2%)
    all_to_all x1, blocking collectives, on_device(): lax.all_to_all(shares, 'brick', 0, 0, axis_index_groups=[list(range(core,...  20.5 us
    ppermute x4, starting transfers between devices, off(): return [lax.ppermute(field, 'brick', off_chip) for field in fields]  11.4 us
    pallas_call x1, Pallas kernels, on_device(): pl.pallas_call(functools.partial(inner_pairs_kernel, tiles), out_shape=pa...  8.2 us
    pallas_call x2, Pallas kernels, local_hops(): pl.pallas_call(functools.partial(local_kernel, tiles, chunk_tiles), out_s...  8.1 us
    pallas_call x1, Pallas kernels, on_device(): pl.pallas_call(functools.partial(last_pairs_kernel, tiles, chunk_tiles[-1...  7.16 us
    ppermute x1, waiting for transfers between devices, on_device(): low_links = lax.ppermute(top_links, 'brick', up)  5.51 us
    ppermute x1, starting transfers between devices, on_device(): partner = lax.ppermute(first_inner, 'brick', on_chip)  4.51 us
    pallas_call x1, Pallas kernels, on_device(): pl.pallas_call(functools.partial(outer_pairs_kernel, tiles, chunk), out_s...  4.2 us
  transfers between devices with their start and end apart: 9, of which 3 were waited for; matrix products, arithmetic and copies ran while one was open for 0% of the time, Pallas kernels for 30%

commit v1 on v0

--- a/solution.py
+++ b/solution.py
@@ -62,26 +62,38 @@
     return (part * 3 + row) * 3 + column
 
 
-def split_kernel(tiles, chunk_tiles, place_ref, x_ref, *refs):
-    outer, inner = refs[:-1], refs[-1]
-    vectors = inner.shape[1]
+def plane_rows(x_ref, part, tile, tiles, vectors, lower_core, inner):
+    start = (part * tiles + tile) * 2
+    plane_0, plane_1 = (
+        x_ref[pl.ds(start + plane, vectors, stride=6 * tiles * 2), :] for plane in range(2)
+    )
+    if inner:
+        return jnp.where(lower_core, plane_1, plane_0)
+    return jnp.where(lower_core, plane_0, plane_1)
+
+
+def outer_kernel(tiles, chunk_tiles, place_ref, x_ref, *outer):
     lower_core = place_ref[1] == 0
-    for chunk, (first_tile, count) in enumerate(chunk_tiles):
+    for (first_tile, count), out in zip(chunk_tiles, outer):
         for part in range(6):
-            for tile in range(first_tile, first_tile + count):
-                start = (part * tiles + tile) * 2
-                plane_0, plane_1 = (
-                    x_ref[pl.ds(start + plane, vectors, stride=6 * tiles * 2), :]
-                    for plane in range(2)
+            for tile in range(count):
+                at = tile * LANES
+                out[part, :, at : at + LANES] = plane_rows(
+                    x_ref, part, first_tile + tile, tiles, out.shape[1], lower_core, False
                 )
-                at = (tile - first_tile) * LANES
-                outer[chunk][part, :, at : at + LANES] = jnp.where(lower_core, plane_0, plane_1)
-                at = tile * LANES
-                inner[part, :, at : at + LANES] = jnp.where(lower_core, plane_1, plane_0)
-
-
-def link_kernel(tiles, place_ref, link_ref, plane_links, cross_links, top_links):
+
+
+def inner_kernel(
+    tiles, vectors, place_ref, x_ref, link_ref, after, inner, plane_links, cross_links, top_links
+):
+    del after
     lower_core = place_ref[1] == 0
+    for part in range(6):
+        for tile in range(tiles):
+            inner[part, :vectors, tile * LANES : (tile + 1) * LANES] = plane_rows(
+                x_ref, part, tile, tiles, vectors, lower_core, True
+            )
+    inner[:, vectors:, :] = jnp.zeros_like(inner[:, vectors:, :])
     for index in range(36 * tiles):
         plane_0, plane_1 = (
             link_ref[index * 2 + plane : index * 2 + plane + 1, :] for plane in range(2)
@@ -95,139 +107,211 @@
                 for tile in range(tiles):
                     straight = ((36 + link_row(part, row, column)) * tiles + tile) * 2
                     turned = ((36 + link_row(part, column, row)) * tiles + tile) * 2
-                    index = link_row(part, row, column) * tiles + tile
+                    number = link_row(part, row, column)
+                    index = number * tiles + tile
                     sign = -1.0 if part else 1.0
                     cross_links[index : index + 1, :] = jnp.where(
                         lower_core,
                         link_ref[straight : straight + 1, :],
                         sign * link_ref[turned : turned + 1, :],
                     )
-                    top_links[index : index + 1, :] = link_ref[straight + 1 : straight + 2, :]
-
-
-def z_link(top_links, low_links, tiles, tile, use_low):
+                    top = link_ref[straight + 1 : straight + 2, :]
+                    top_links[index : index + 1, :] = top
+                    inner[
+                        number // 3,
+                        vectors + number % 3 : vectors + number % 3 + 1,
+                        tile * LANES : (tile + 1) * LANES,
+                    ] = top
+
+
+def z_link(tiles, tile, top_links, low_link, use_low):
     found = {}
     for part in range(2):
         for row in range(3):
             for column in range(3):
                 straight = link_row(part, row, column) * tiles + tile
-                turned = link_row(part, column, row) * tiles + tile
                 sign = -1.0 if part else 1.0
-                found[part, row, column] = jnp.where(
+                value = jnp.where(
                     use_low,
-                    sign * low_links[turned : turned + 1, :],
+                    sign * low_link(part, column, row, tile),
                     top_links[straight : straight + 1, :],
                 )
+                found[part, row, column] = jnp.broadcast_to(value, (ROWS, LANES))
     return lambda *index: found[index]
 
 
-def local_kernel(tiles, chunk_tiles, plane_links, cross_links, inner, *refs):
-    outer, (inner_out, outer_out) = refs[: len(chunk_tiles)], refs[len(chunk_tiles) :]
-    vectors = inner.shape[1]
+def low_rows(low_links, tiles):
+    def low_link(part, row, column, tile):
+        index = link_row(part, row, column) * tiles + tile
+        return low_links[index : index + 1, :]
+
+    return low_link
+
+
+def partner_rows(partner, vectors):
+    def low_link(part, row, column, tile):
+        number = link_row(part, row, column)
+        at = vectors + number % 3
+        return partner[number // 3, at : at + 1, tile * LANES : (tile + 1) * LANES]
+
+    return low_link
+
+
+def tile_of(chunk_tiles, refs, tile):
+    for (first_tile, count), ref in zip(chunk_tiles, refs):
+        if first_tile <= tile < first_tile + count:
+            return ref, slice((tile - first_tile) * LANES, (tile - first_tile + 1) * LANES)
+
+
+def cross_of(cross_links, tiles, tile):
+    def link(part, row, column):
+        index = link_row(part, row, column) * tiles + tile
+        return cross_links[index : index + 1, :]
+
+    return link
+
+
+def plane_hops(tiles, plane, plane_links, get, extra, put):
     lane = lax.broadcasted_iota(jnp.int32, (ROWS, LANES), 1)
     column = lane % LX
     first_column, last_column = column == 0, column == LX - 1
     below, above = lane < LX, lane >= LANES - LX
     zeros = [jnp.zeros((ROWS, LANES), jnp.float32)] * 6
 
-    def step(group, carry):
-        rows = pl.ds(pl.multiple_of(group * ROWS, ROWS), ROWS)
-
+    def link_of(direction, tile):
+        def link(part, row, column_at):
+            index = plane * 36 + direction * 18 + link_row(part, row, column_at)
+            index = index * tiles + tile
+            return plane_links[index : index + 1, :]
+
+        return link
+
+    sums = []
+    rolled_in = []
+    rolled_out = []
+    for tile in range(tiles):
+        field = get(tile)
+        ahead = [
+            jnp.where(last_column, pltpu.roll(f, LX - 1, 1), pltpu.roll(f, LANES - 1, 1))
+            for f in field
+        ]
+        total = [
+            jnp.where(first_column, pltpu.roll(f, LANES - LX + 1, 1), pltpu.roll(f, 1, 1))
+            for f in adjoint(link_of(0, tile), field, zeros)
+        ]
+        sums.append(extra(tile, times(link_of(0, tile), ahead, total)))
+        rolled_in.append([pltpu.roll(f, LANES - LX, 1) for f in field])
+        rolled_out.append(
+            [pltpu.roll(f, LX, 1) for f in adjoint(link_of(1, tile), field, zeros)]
+        )
+    for tile in range(tiles):
+        after, before = (tile + 1) % tiles, (tile - 1) % tiles
+        ahead = [jnp.where(above, b, a) for a, b in zip(rolled_in[tile], rolled_in[after])]
+        total = times(link_of(1, tile), ahead, sums[tile])
+        put(
+            tile,
+            [
+                t + jnp.where(below, b, o)
+                for t, b, o in zip(total, rolled_out[before], rolled_out[tile])
+            ],
+        )
+
+
+def groups_loop(vectors, step, unroll=1):
+    def body(group, carry):
+        step(pl.ds(pl.multiple_of(group * ROWS, ROWS), ROWS))
+        return carry
+
+    lax.fori_loop(0, vectors // ROWS, body, 0, unroll=unroll)
+
+
+def local_kernel(tiles, chunk_tiles, planes, plane_links, cross_links, inner, *refs):
+    outer, outs = refs[: len(chunk_tiles)], refs[-len(planes) :]
+
+    def step(rows):
         def get(plane, tile):
             if plane == 0:
-                ref, at = inner, tile * LANES
+                ref, lanes = inner, slice(tile * LANES, (tile + 1) * LANES)
             else:
-                for chunk, (first_tile, count) in enumerate(chunk_tiles):
-                    if first_tile <= tile < first_tile + count:
-                        ref, at = outer[chunk], (tile - first_tile) * LANES
-            return [ref[part, rows, at : at + LANES] for part in range(6)]
-
-        def link_of(direction, plane, tile):
-            def link(part, row, column_at):
-                index = plane * 36 + direction * 18 + link_row(part, row, column_at)
-                index = index * tiles + tile
-                return plane_links[index : index + 1, :]
-
-            return link
-
-        def cross_of(tile):
-            def link(part, row, column_at):
-                index = link_row(part, row, column_at) * tiles + tile
-                return cross_links[index : index + 1, :]
-
-            return link
-
-        for plane in range(2):
-            sums = []
-            rolled_in = []
-            rolled_out = []
-            for tile in range(tiles):
-                field = get(plane, tile)
-                ahead = [
-                    jnp.where(
-                        last_column, pltpu.roll(f, LX - 1, 1), pltpu.roll(f, LANES - 1, 1)
-                    )
-                    for f in field
-                ]
-                behind = adjoint(link_of(0, plane, tile), field, zeros)
-                total = [
-                    jnp.where(
-                        first_column, pltpu.roll(f, LANES - LX + 1, 1), pltpu.roll(f, 1, 1)
-                    )
-                    for f in behind
-                ]
-                total = times(link_of(0, plane, tile), ahead, total)
-                if plane == 0:
-                    total = adjoint(cross_of(tile), get(1, tile), total)
-                else:
-                    total = times(cross_of(tile), get(0, tile), total)
-                sums.append(total)
-                rolled_in.append([pltpu.roll(f, LANES - LX, 1) for f in field])
-                rolled_out.append(
-                    [
-                        pltpu.roll(f, LX, 1)
-                        for f in adjoint(link_of(1, plane, tile), field, zeros)
-                    ]
-                )
-            for tile in range(tiles):
-                after, before = (tile + 1) % tiles, (tile - 1) % tiles
-                ahead = [
-                    jnp.where(above, b, a) for a, b in zip(rolled_in[tile], rolled_in[after])
-                ]
-                total = times(link_of(1, plane, tile), ahead, sums[tile])
-                lanes = slice(tile * LANES, (tile + 1) * LANES)
+                ref, lanes = tile_of(chunk_tiles, outer, tile)
+            return [ref[part, rows, lanes] for part in range(6)]
+
+        for plane, out in zip(planes, outs):
+            hop = times if plane else adjoint
+
+            def put(tile, total):
                 for part in range(6):
-                    back = jnp.where(below, rolled_out[before][part], rolled_out[tile][part])
-                    out = outer_out if plane else inner_out
-                    out[part, rows, lanes] = total[part] + back
-        return carry
-
-    lax.fori_loop(0, vectors // ROWS, step, 0)
-
-
-def finish_hop(tiles, chunk, use_low, top_links, low_links, beyond, sums, out, finish):
+                    out[part, rows, tile * LANES : (tile + 1) * LANES] = total[part]
+
+            plane_hops(
+                tiles,
+                plane,
+                plane_links,
+                lambda tile: get(plane, tile),
+                lambda tile, total: hop(
+                    cross_of(cross_links, tiles, tile), get(1 - plane, tile), total
+                ),
+                put,
+            )
+
+    groups_loop(outer[0].shape[1], step)
+
+
+def inner_hop_kernel(tiles, plane_links, first, out):
+    def step(rows):
+        def put(tile, total):
+            for part in range(6):
+                out[part, rows, tile * LANES : (tile + 1) * LANES] = total[part]
+
+        plane_hops(
+            tiles,
+            0,
+            plane_links,
+            lambda tile: [
+                first[part, rows, tile * LANES : (tile + 1) * LANES] for part in range(6)
+            ],
+            lambda tile, total: total,
+            put,
+        )
+
+    groups_loop(out.shape[1], step)
+
+
+def finish_hop(tiles, chunk, use_low, top_links, low_link, beyond, sums, out, finish):
     first_tile, count = chunk
-    vectors = beyond.shape[1]
     for tile in range(count):
-        link = z_link(top_links, low_links, tiles, first_tile + tile, use_low)
+        link = z_link(tiles, first_tile + tile, top_links, low_link, use_low)
         lanes = slice(tile * LANES, (tile + 1) * LANES)
         at = (first_tile + tile) * LANES
 
-        def step(group, carry):
-            rows = pl.ds(pl.multiple_of(group * ROWS, ROWS), ROWS)
+        def step(rows):
             field = [beyond[part, rows, lanes] for part in range(6)]
             total = [sums[part, rows, at : at + LANES] for part in range(6)]
             total = times(link, field, total)
             for part in range(6):
                 out[part, rows, lanes] = finish(total[part], (part, rows, lanes))
-            return carry
-
-        lax.fori_loop(0, vectors // ROWS, step, 0, unroll=2)
-
-
-def edge_kernel(tiles, chunk, low_core, place_ref, top_links, low_links, beyond, sums, *refs):
+
+        groups_loop(out.shape[1], step, 2)
+
+
+def inner_edge_kernel(tiles, place_ref, top_links, partner, sums, out):
     finish_hop(
-        tiles, chunk, place_ref[1] == low_core, top_links, low_links, beyond, sums, refs[-1],
+        tiles, (0, tiles), place_ref[1] == 1, top_links, partner_rows(partner, out.shape[1]),
+        partner, sums, out, lambda total, index: total * (1.0 / 6.0),
+    )
+
+
+def inner_rest_kernel(tiles, place_ref, top_links, linked, partner, sums, own, out):
+    finish_hop(
+        tiles, (0, tiles), place_ref[1] == 1, top_links, partner_rows(linked, out.shape[1]),
+        partner, sums, out, lambda total, index: total * (2.0 / 6.0) - own[index],
+    )
+
+
+def edge_kernel(tiles, chunk, place_ref, top_links, low_links, beyond, sums, token, out):
+    del token
+    finish_hop(
+        tiles, chunk, place_ref[1] == 0, top_links, low_rows(low_links, tiles), beyond, sums, out,
         lambda total, index: total * (1.0 / 6.0),
     )
 
@@ -313,13 +397,27 @@
         multiply(now)
 
 
-def inner_pairs_kernel(
-    tiles, place_ref, top_links, low_links, partner, partial, own, sums, field, low, quarks
-):
-    finish_hop(
-        tiles, (0, tiles), place_ref[1] == 1, top_links, low_links, partner, partial, field,
-        lambda total, index: total * (2.0 / 6.0) - own[index],
-    )
+def inner_pairs_kernel(tiles, chunk_tiles, cross_links, rest, *refs):
+    outer, (sums, field, low, quarks) = refs[: len(chunk_tiles)], refs[len(chunk_tiles) :]
+    for tile in range(tiles):
+        ref, from_lanes = tile_of(chunk_tiles, outer, tile)
+        lanes = slice(tile * LANES, (tile + 1) * LANES)
+        link = cross_of(cross_links, tiles, tile)
+        found = {
+            (part, row, column): jnp.broadcast_to(link(part, row, column), (ROWS, LANES))
+            for part in range(2)
+            for row in range(3)
+            for column in range(3)
+        }
+
+        def step(rows):
+            source = [ref[part, rows, from_lanes] for part in range(6)]
+            zeros = [jnp.zeros((ROWS, LANES), jnp.float32)] * 6
+            total = adjoint(lambda *index: found[index], source, zeros)
+            for part in range(6):
+                field[part, rows, lanes] = rest[part, rows, lanes] + total[part] * (2.0 / 6.0)
+
+        groups_loop(field.shape[1], step, 2)
     sums[...] = jnp.zeros_like(sums)
     width = low.shape[1] // 6
     for start in range(0, field.shape[2], width):
@@ -330,7 +428,7 @@
     tiles, chunk, place_ref, top_links, low_links, far, partial, own, before, sums, field, low, quarks
 ):
     finish_hop(
-        tiles, chunk, place_ref[1] == 0, top_links, low_links, far, partial, field,
+        tiles, chunk, place_ref[1] == 0, top_links, low_rows(low_links, tiles), far, partial, field,
         lambda total, index: total * (2.0 / 6.0) - own[index],
     )
     sums[...] = before[...]
@@ -426,15 +524,24 @@
     lax.fori_loop(0, slot_ref.shape[0], place, 0)
 
 
-def combine_kernel(keep, received, out):
-    out[...] = keep[...] + received[...]
-
-
-def total_kernel(arrived, out):
-    total = arrived[0]
-    for chip in range(1, arrived.shape[0]):
-        total = total + arrived[chip]
-    out[...] = total
+def fold_kernel(parts, place_ref, *refs):
+    ins, outs = refs[: -2 * len(parts)], refs[-2 * len(parts) :]
+    for number, (rows, bit, position) in enumerate(parts):
+        kept, received = ins[:2] if len(ins) == 2 else ins[2 * number : 2 * number + 2]
+        stay, leave = outs[2 * number : 2 * number + 2]
+        mine = lax.rem(lax.div(place_ref[0], 1 << bit), 2)
+        for index in range(stay.shape[0]):
+            low = index % (1 << position)
+            base = (index - low) * 2 + low
+            for out, value in ((stay, mine), (leave, 1 - mine)):
+                at = base + value * (1 << position)
+                out[index] = kept[at, :, rows, :] + received[at, :, rows, :]
+
+
+def total_kernel(cut, *refs):
+    out = refs[-1]
+    for number, rows in enumerate(cut):
+        out[:, rows, :] = refs[2 * number][0] + refs[2 * number + 1][0]
 
 
 def on_device(eigen_vectors, link_field, block_slot):
@@ -459,62 +566,63 @@
     place = jnp.stack([me // 2, me % 2]).astype(jnp.int32)
     z_links = jax.ShapeDtypeStruct((18 * tiles, LANES), jnp.float32)
 
-    plane_links, cross_links, top_links = pl.pallas_call(
-        functools.partial(link_kernel, tiles),
-        out_shape=[jax.ShapeDtypeStruct((72 * tiles, LANES), jnp.float32), z_links, z_links],
-        in_specs=[SMEM, VMEM],
-        out_specs=[VMEM] * 3,
-        compiler_params=params(32),
-        name="links",
-    )(place, tile_rows(link_field))
-    *outer, inner = pl.pallas_call(
-        functools.partial(split_kernel, tiles, chunk_tiles),
-        out_shape=pieces + [plane],
-        in_specs=[SMEM, VMEM],
-        out_specs=[VMEM] * (len(pieces) + 1),
-        compiler_params=params(32),
-        name="split",
-    )(place, tile_rows(eigen_vectors))
+    def call(kernel, shapes, name, smem, *args, limit=32, flops=0, scratch=()):
+        many = isinstance(shapes, list)
+        return pl.pallas_call(
+            kernel,
+            out_shape=shapes,
+            in_specs=[SMEM] * smem + [VMEM] * (len(args) - smem),
+            out_specs=[VMEM] * len(shapes) if many else VMEM,
+            scratch_shapes=list(scratch),
+            compiler_params=params(limit),
+            cost_estimate=cost(flops, 2 * plane_bytes) if flops else None,
+            name=name,
+        )(*args)
+
+    rows = tile_rows(eigen_vectors)
+    outer = call(
+        functools.partial(outer_kernel, tiles, chunk_tiles), pieces, "outer", 1, place, rows
+    )
+    with_links = jax.ShapeDtypeStruct((6, vectors + ROWS, sites), jnp.float32)
+    inner, plane_links, cross_links, top_links = call(
+        functools.partial(inner_kernel, tiles, vectors),
+        [with_links, jax.ShapeDtypeStruct((72 * tiles, LANES), jnp.float32), z_links, z_links],
+        "inner", 1, place, rows, tile_rows(link_field), outer[-1],
+    )
 
     def off(fields):
         return [lax.ppermute(field, "brick", off_chip) for field in fields]
 
-    def local_hops(inner, outer):
-        return pl.pallas_call(
-            functools.partial(local_kernel, tiles, chunk_tiles),
-            out_shape=[plane] * 2,
-            in_specs=[VMEM] * (3 + len(pieces)),
-            out_specs=[VMEM] * 2,
-            compiler_params=params(48),
-            cost_estimate=cost(5e9, 4 * plane_bytes),
-            name="local",
-        )(plane_links, cross_links, inner, *outer)
-
-    def edge(chunk, low_core, shape, *args):
-        return pl.pallas_call(
-            functools.partial(edge_kernel, tiles, chunk, low_core),
-            out_shape=shape,
-            in_specs=[SMEM] + [VMEM] * (2 + len(args)),
-            out_specs=VMEM,
-            compiler_params=params(32),
-            name="edge",
-        )(place, top_links, low_links, *args)
-
     far = off(outer)
+    linked = lax.ppermute(inner, "brick", on_chip)
     low_links = lax.ppermute(top_links, "brick", up)
-    partner = lax.ppermute(inner, "brick", on_chip)
-    inner_sums, outer_sums = local_hops(inner, outer)
-    first_inner = edge((0, tiles), 1, plane, partner, inner_sums)
+    inner_sums, outer_sums = call(
+        functools.partial(local_kernel, tiles, chunk_tiles, (0, 1)), [plane] * 2, "local", 0,
+        plane_links, cross_links, inner, *outer, limit=48, flops=4e9,
+    )
+    first_inner = call(
+        functools.partial(inner_edge_kernel, tiles), plane, "inner_edge", 1,
+        place, top_links, linked, inner_sums,
+    )
     partner = lax.ppermute(first_inner, "brick", on_chip)
-    token = sum(field[0, :ROWS, :LANES] for field in far)
-    token = lax.ppermute(token, "brick", on_chip)
+    inner_sums = call(
+        functools.partial(inner_hop_kernel, tiles), plane, "inner_hop", 0,
+        plane_links, first_inner, flops=2e9,
+    )
+    rest = call(
+        functools.partial(inner_rest_kernel, tiles), plane, "inner_rest", 1,
+        place, top_links, linked, partner, inner_sums, inner, flops=1e9,
+    )
+    token = sum(field[0, :ROWS, :LANES] for field in [rest, *far])
+    token = lax.ppermute(token, "brick", [(i, i ^ 1) for i in range(count) if i % 4 in (1, 2)])
     first_outer = [
-        edge(chunk, 0, piece, field, outer_sums, token)
+        call(
+            functools.partial(edge_kernel, tiles, chunk), piece, "edge", 1,
+            place, top_links, low_links, field, outer_sums, token,
+        )
         for chunk, piece, field in zip(chunk_tiles, pieces, far)
     ]
     far = off(first_outer)
-    inner_sums, sums = local_hops(first_inner, first_outer)
-
     def scratch(width):
         return [
             pltpu.VMEM((2 * vectors, 6 * width), jnp.bfloat16),
@@ -522,16 +630,15 @@
         ]
 
     partial_sums = jax.ShapeDtypeStruct((pair_rows, 2 * vectors), jnp.float32)
-    before = pl.pallas_call(
-        functools.partial(inner_pairs_kernel, tiles),
-        out_shape=partial_sums,
-        in_specs=[SMEM] + [VMEM] * 5,
-        out_specs=VMEM,
-        scratch_shapes=[pltpu.VMEM(plane.shape, jnp.float32)] + scratch(2 * LANES),
-        compiler_params=params(48),
-        cost_estimate=cost(8e9, 6 * plane_bytes),
-        name="inner_pairs",
-    )(place, top_links, low_links, partner, inner_sums, inner)
+    before = call(
+        functools.partial(inner_pairs_kernel, tiles, chunk_tiles), partial_sums, "inner_pairs", 0,
+        cross_links, rest, *first_outer, limit=48, flops=8e9,
+        scratch=[pltpu.VMEM(plane.shape, jnp.float32)] + scratch(2 * LANES),
+    )
+    (sums,) = call(
+        functools.partial(local_kernel, tiles, chunk_tiles, (1,)), [plane], "outer_hop", 0,
+        plane_links, cross_links, first_inner, *first_outer, before, limit=48, flops=2e9,
+    )
     for chunk, piece, field, own in zip(chunk_tiles[:-1], pieces, far, outer):
         before = pl.pallas_call(
             functools.partial(outer_pairs_kernel, tiles, chunk),
@@ -567,31 +674,39 @@
         name="last_pairs",
     )(block_slot, place, top_links, low_links, far[-1], sums, outer[-1], before)
     received = lax.ppermute(send, "brick", on_chip)
+    bits = chips.bit_length() - 1
+    cut = (slice(0, PB // 2), slice(PB // 2, PB))
+    orders = [list(range(bits)), list(range(bits))]
+    if bits > 1:
+        orders[1][:2] = [1, 0]
+    remaining = [list(range(bits)), list(range(bits))]
+
+    def fold(halves, stage, rows_of, *pairs):
+        parts, shapes = [], []
+        for half_at in halves:
+            bit = orders[half_at][stage]
+            parts.append((rows_of[half_at], bit, remaining[half_at].index(bit)))
+            remaining[half_at].remove(bit)
+            shape = (2 ** len(remaining[half_at]), CAP, PB // 2, 2 * vectors)
+            shapes += [jax.ShapeDtypeStruct(shape, jnp.float32)] * 2
+        outs = call(
+            functools.partial(fold_kernel, parts), shapes, "fold", 1, place, *pairs
+        )
+        found = []
+        for number, half_at in enumerate(halves):
+            bit = orders[half_at][stage]
+            route = [(i, i ^ (2 << bit)) for i in range(count)]
+            found.append((outs[2 * number], lax.ppermute(outs[2 * number + 1], "brick", route)))
+        return found
+
+    whole = (slice(None), slice(None))
+    pairs = fold((0, 1), 0, cut, keep, received)
+    for stage in range(1, bits):
+        pairs = [fold((half_at,), stage, whole, *pairs[half_at])[0] for half_at in range(2)]
     share = jax.ShapeDtypeStruct((CAP, PB, 2 * vectors), jnp.float32)
-    shares = pl.pallas_call(
-        combine_kernel,
-        out_shape=half,
-        in_specs=[VMEM] * 2,
-        out_specs=VMEM,
-        compiler_params=params(32),
-        name="combine",
-    )(keep, received)
-    arrived = lax.all_to_all(
-        shares,
-        "brick",
-        0,
-        0,
-        axis_index_groups=[list(range(core, count, 2)) for core in range(2)],
-        tiled=True,
-    )
-    return pl.pallas_call(
-        total_kernel,
-        out_shape=share,
-        in_specs=[VMEM],
-        out_specs=VMEM,
-        compiler_params=params(32),
-        name="total",
-    )(arrived)
+    return call(
+        functools.partial(total_kernel, cut), share, "total", 0, *(ref for pair in pairs for ref in pair)
+    )
 
 
 def solution(mesh):

time: 81 us -> 84.9 us (1.048)
  blocking collectives: 20.5 us -> 0 us
  waiting for transfers between devices: 9.23 us -> 28.7 us
  Pallas kernels: 32.8 us -> 36.7 us
  starting transfers between devices: 16.6 us -> 17.5 us
    all_to_all x1 -> x0, blocking collectives: 20.5 us -> none  [on_device(): lax.all_to_all(shares, 'brick', 0, 0, axis_index_groups=[list(range(core,...]
    ppermute x2 -> x8, waiting for transfers between devices: 1.81 us -> 16.7 us  [the longest x6 10.4 us: fold(): lax.ppermute(outs[2 * number + 1], 'brick', route)]
    ppermute x4, waiting for transfers between devices: 0.01 us -> 10.1 us  [off(): return [lax.ppermute(field, 'brick', off_chip) for field in fields]]
    ppermute x2 -> x8, starting transfers between devices: 0.62 us -> 7 us  [the longest x6 5.02 us: fold(): lax.ppermute(outs[2 * number + 1], 'brick', route)]
    ppermute x1, waiting for transfers between devices: 5.51 us -> 0.01 us  [on_device(): low_links = lax.ppermute(top_links, 'brick', up)]
    ppermute x1, starting transfers between devices: 4.51 us -> 0.12 us  [on_device(): partner = lax.ppermute(first_inner, 'brick', on_chip)]
    pallas_call x10 -> x16, Pallas kernels: 21.5 us -> 25.3 us  [call(): pl.pallas_call(kernel, out_shape=shapes, in_specs=[SMEM] * smem + [VMEM]...]
    ppermute x4, starting transfers between devices: 11.4 us -> 10.3 us  [off(): return [lax.ppermute(field, 'brick', off_chip) for field in fields]]
  transfers between devices with their start and end apart: 9 -> 15, of which waited for: 3 -> 9; matrix products, arithmetic and copies ran while one was open for 0% -> 0% of each run, Pallas kernels for 30% -> 29%
where the time goes in v1:
time: 84.9 us; the launch traced here: 84.7 us
  Pallas kernels  36.7 us (43%)
  waiting for transfers between devices  28.7 us (34%)
  starting transfers between devices  17.5 us (21%)
  local copies, waits for them, and re-layouts  1.42 us (2%)
    pallas_call x16, Pallas kernels, call(): pl.pallas_call(kernel, out_shape=shapes, in_specs=[SMEM] * smem + [VMEM]...  25.3 us
    ppermute x6, waiting for transfers between devices, fold(): lax.ppermute(outs[2 * number + 1], 'brick', route)  10.4 us
    ppermute x4, starting transfers between devices, off(): return [lax.ppermute(field, 'brick', off_chip) for field in fields]  10.3 us
    ppermute x4, waiting for transfers between devices, off(): return [lax.ppermute(field, 'brick', off_chip) for field in fields]  10.1 us
    pallas_call x1, Pallas kernels, on_device(): pl.pallas_call(functools.partial(last_pairs_kernel, tiles, chunk_tiles[-1...  7.19 us
    ppermute x1, waiting for transfers between devices, on_device(): lax.ppermute(token, 'brick', [(i, i ^ 1) for i in range(count) if i % 4 i...  6.38 us
    ppermute x6, starting transfers between devices, fold(): lax.ppermute(outs[2 * number + 1], 'brick', route)  5.02 us
    pallas_call x1, Pallas kernels, on_device(): pl.pallas_call(functools.partial(outer_pairs_kernel, tiles, chunk), out_s...  4.19 us
  transfers between devices with their start and end apart: 15, of which 9 were waited for; matrix products, arithmetic and copies ran while one was open for 0% of the time, Pallas kernels for 29%

profile of v1, /device:TPU:0, one launch (start us, length us, event | category | flops | bytes accessed | tf_op | source)
XLA Modules:
  0.0 84.7 jit_solution(15875345611289788293)
XLA Ops:
  0.0 0.1 pad_add_fusion.place_ref
  0.1 0.0 copy-start
  0.1 1.4 %copy-done = f32[64,2,3,2,512]{4,3,2,1,0:T(2,128)S(1)} copy-done((f32[64,2,3,2,512]{4,3,2,1,0:T(2,128)S(1)}, f32[64,2,3,2,512]{4,3,2,1,0:T(2,128)}, u32[]{:S(2)}) %copy-start) | copy-done | bytes 1572888
  1.5 0.0 copy-start.1
  1.5 1.0 %outer.1 = (f32[6,64,256]{2,1,0:T(8,128)S(1)}, f32[6,64,256]{2,1,0:T(8,128)S(1)}) custom-call(s32[2]{0:T(128)S(1)} %pad_add_fusion.place_ref, f32[3072,128]{1,0:T(8,128)S(1)} %bitcast.14), custom_call_target="tpu_custom_call" | custom-call | tf_op jit(solution)/shard_map/outer/pallas_call | solution.py:571
  2.5 0.0 copy-done.1
  2.5 1.2 %inner.1 = (f32[6,72,512]{2,1,0:T(8,128)S(1)}, f32[288,128]{1,0:T(8,128)S(1)}, f32[72,128]{1,0:T(8,128)S(1)}, f32[72,128]{1,0:T(8,128)S(1)}) custom-call(s32[2]{0:T(128)S(1)} %pad_add_fusion.place_ref, f32[3072,128]{1,0:T(8,128)S(1)} %bitcast.15, f32[432,128]{1,0:T(8,128)S(1)} %bitcast.16, f32[6,64,256]{2,1,0:T(8,128)S(1)} %get-tuple-element.27.after.refs_1_.own), custom_call_target="tpu_custom_call" | custom-call | tf_op jit(solution)/shard_map/inner/pallas_call | solution.py:571
  3.7 0.5 collective-permute-start.2
  4.2 4.1 %local.1 = (f32[6,64,512]{2,1,0:T(8,128)S(1)}, f32[6,64,512]{2,1,0:T(8,128)S(1)}) custom-call(f32[288,128]{1,0:T(8,128)S(1)} %get-tuple-element.29.plane_links, f32[72,128]{1,0:T(8,128)S(1)} %get-tuple-element.30.cross_links, f32[6,72,512]{2,1,0:T(8,128)S(1)} %get-tuple-element.31.inner.own, f32[6,64,256]{2,1,0:T(8,128)S(1)} %get-tuple-element.32.refs_0_.own, ...), custom_call_target="tpu_custom_call" | custom-call | flops 4000000000 | bytes 1572864 | tf_op jit(solution)/shard_map/local/pallas_call | solution.py:571
  8.3 0.0 collective-permute-done.2.partner.linked
  8.3 1.1 %inner_edge.1.first.inner = f32[6,64,512]{2,1,0:T(8,128)S(1)} custom-call(s32[2]{0:T(128)S(1)} %pad_add_fusion.place_ref, f32[72,128]{1,0:T(8,128)S(1)} %get-tuple-element.28.top_links, f32[6,72,512]{2,1,0:T(8,128)S(1)} %collective-permute-done.2.partner.linked, f32[6,64,512]{2,1,0:T(8,128)S(1)} %get-tuple-element.34.sums), custom_call_target="tpu_custom_call" | custom-call | tf_op jit(solution)/shard_map/inner_edge/pallas_call | solution.py:571
  9.4 0.1 collective-permute-start.3
  9.5 5.7 %collective-permute-start.1 = (f32[6,64,256]{2,1,0:T(8,128)S(1)}, f32[6,64,256]{2,1,0:T(8,128)S(1)}, u32[]{:S(2)}, u32[]{:S(2)}) collective-permute-start(f32[6,64,256]{2,1,0:T(8,128)S(1)} %get-tuple-element.27.after.refs_1_.own), channel_id=1, source_target_pairs={{0,15},{1,2},{2,1},{3,4},{4,3},{5,6},{6,5},{7,8},{8,7},{9,10},{10,... | collective-permute-start | bytes 1179656 | tf_op jit(solution)/shard_map/ppermute | solution.py:594
  15.2 0.1 collective-permute-start.4
  15.3 0.0 collective-permute-start
  15.3 2.0 %inner_hop.1.sums = f32[6,64,512]{2,1,0:T(8,128)S(1)} custom-call(f32[288,128]{1,0:T(8,128)S(1)} %get-tuple-element.29.plane_links, f32[6,64,512]{2,1,0:T(8,128)S(1)} %inner_edge.1.first.inner), custom_call_target="tpu_custom_call" | custom-call | flops 2000000000 | bytes 1572864 | tf_op jit(solution)/shard_map/inner_hop/pallas_call | solution.py:571
  17.3 0.0 collective-permute-done.3.partner
  17.3 1.1 %inner_rest.1.rest = f32[6,64,512]{2,1,0:T(8,128)S(1)} custom-call(s32[2]{0:T(128)S(1)} %pad_add_fusion.place_ref, f32[72,128]{1,0:T(8,128)S(1)} %get-tuple-element.28.top_links, f32[6,72,512]{2,1,0:T(8,128)S(1)} %collective-permute-done.2.partner.linked, f32[6,64,512]{2,1,0:T(8,128)S(1)} %collective-permute-done.3.partner, ...), custom_call_target="tpu_custom_call" | custom-call | flops 1000000000 | bytes 1572864 | tf_op jit(solution)/shard_map/inner_rest/pallas_call | solution.py:571
  18.4 2.4 %collective-permute-done.1.beyond = f32[6,64,256]{2,1,0:T(8,128)S(1)} collective-permute-done((f32[6,64,256]{2,1,0:T(8,128)S(1)}, f32[6,64,256]{2,1,0:T(8,128)S(1)}, u32[]{:S(2)}, u32[]{:S(2)}) %collective-permute-start.1) | collective-permute-done | bytes 393248 | tf_op jit(solution)/shard_map/ppermute | solution.py:594
  20.8 4.4 %collective-permute-done.4.beyond = f32[6,64,256]{2,1,0:T(8,128)S(1)} collective-permute-done((f32[6,64,256]{2,1,0:T(8,128)S(1)}, f32[6,64,256]{2,1,0:T(8,128)S(1)}, u32[]{:S(2)}, u32[]{:S(2)}) %collective-permute-start.4) | collective-permute-done | bytes 393248 | tf_op jit(solution)/shard_map/ppermute | solution.py:594
  25.2 1.5 %collective-permute-start.5 = (f32[8,128]{1,0:T(8,128)S(1)}, f32[8,128]{1,0:T(8,128)S(1)}, u32[]{:S(2)}, u32[]{:S(2)}) collective-permute-start(f32[8,128]{1,0:T(8,128)S(1)} %fusion), channel_id=1, source_target_pairs={{1,0},{2,3},{5,4},{6,7},{9,8},{10,11},{13,12},{14,15},{17,16},{18,... | collective-permute-start | bytes 12296 | tf_op jit(solution)/shard_map/ppermute | solution.py:617
  26.6 0.0 collective-permute-done.low_links
  26.6 6.4 %collective-permute-done.5.token = f32[8,128]{1,0:T(8,128)S(1)} collective-permute-done((f32[8,128]{1,0:T(8,128)S(1)}, f32[8,128]{1,0:T(8,128)S(1)}, u32[]{:S(2)}, u32[]{:S(2)}) %collective-permute-start.5) | collective-permute-done | bytes 4128 | tf_op jit(solution)/shard_map/ppermute | solution.py:617
  33.0 0.8 edge.3.refs_0_
  33.8 4.5 %collective-permute-start.7 = (f32[6,64,256]{2,1,0:T(8,128)S(1)}, f32[6,64,256]{2,1,0:T(8,128)S(1)}, u32[]{:S(2)}, u32[]{:S(2)}) collective-permute-start(f32[6,64,256]{2,1,0:T(8,128)S(1)} %edge.3.refs_0_), channel_id=1, source_target_pairs={{0,15},{1,2},{2,1},{3,4},{4,3},{5,6},{6,5},{7,8},{8,7},{9,10},{10,... | collective-permute-start | bytes 1179656 | tf_op jit(solution)/shard_map/ppermute | solution.py:594
  38.3 0.8 edge.2.refs_1_
  39.1 7.6 %inner_pairs.1.refs_2_.before = f32[1280,128]{1,0:T(8,128)S(1)} custom-call(f32[72,128]{1,0:T(8,128)S(1)} %get-tuple-element.30.cross_links, f32[6,64,512]{2,1,0:T(8,128)S(1)} %inner_rest.1.rest, f32[6,64,256]{2,1,0:T(8,128)S(1)} %edge.3.refs_0_, f32[6,64,256]{2,1,0:T(8,128)S(1)} %edge.2.refs_1_), custom_call_target="tpu_custom_call" | custom-call | flops 8000000000 | bytes 1572864 | tf_op jit(solution)/shard_map/inner_pairs/pallas_call | solution.py:571
  46.7 0.1 collective-permute-start.6
  46.8 2.3 %outer_hop.1.partial = f32[6,64,512]{2,1,0:T(8,128)S(1)} custom-call(f32[288,128]{1,0:T(8,128)S(1)} %get-tuple-element.29.plane_links, f32[72,128]{1,0:T(8,128)S(1)} %get-tuple-element.30.cross_links, f32[6,64,512]{2,1,0:T(8,128)S(1)} %inner_edge.1.first.inner, f32[6,64,256]{2,1,0:T(8,128)S(1)} %edge.3.refs_0_, f32[6,64,256]{2,1,0:T(8,128)S(1)} %edge.2.refs_1_, ...), custom_call_target="tpu_custom_call" | custom-call | flops 2000000000 | bytes 1572864 | tf_op jit(solution)/shard_map/outer_hop/pallas_call | solution.py:571
  49.0 0.0 copy-start.2
  49.1 0.0 collective-permute-done.7.far
  49.1 4.2 %outer_pairs.1.before = f32[1280,128]{1,0:T(8,128)S(1)} custom-call(s32[2]{0:T(128)S(1)} %pad_add_fusion.place_ref, f32[72,128]{1,0:T(8,128)S(1)} %get-tuple-element.28.top_links, f32[72,128]{1,0:T(8,128)S(1)} %collective-permute-done.low_links, f32[6,64,256]{2,1,0:T(8,128)S(1)} %collective-permute-done.7.far, f32[6,64,512]{2,1,0:T(8,128)S(1)} %outer_hop.1.partial, ...), custom_call_target="tpu_custom_call" | custom-call | flops 4000000000 | bytes 2359296 | tf_op jit(solution)/shard_map/outer_pairs/pallas_call | solution.py:643
  53.3 3.4 %collective-permute-done.6.far = f32[6,64,256]{2,1,0:T(8,128)S(1)} collective-permute-done((f32[6,64,256]{2,1,0:T(8,128)S(1)}, f32[6,64,256]{2,1,0:T(8,128)S(1)}, u32[]{:S(2)}, u32[]{:S(2)}) %collective-permute-start.6) | collective-permute-done | bytes 393248 | tf_op jit(solution)/shard_map/ppermute | solution.py:594
  56.6 0.0 copy-done.2
  56.6 7.2 %last_pairs.1 = (f32[8,4,32,128]{3,2,1,0:T(8,128)S(1)}, f32[8,4,32,128]{3,2,1,0:T(8,128)S(1)}) custom-call(s32[63]{0:T(128)S(1)} %copy-done.2, s32[2]{0:T(128)S(1)} %pad_add_fusion.place_ref, f32[72,128]{1,0:T(8,128)S(1)} %get-tuple-element.28.top_links, f32[72,128]{1,0:T(8,128)S(1)} %collective-permute-done.low_links, ...), custom_call_target="tpu_custom_call" | custom-call | flops 4000000000 | bytes 2359296 | tf_op jit(solution)/shard_map/last_pairs/pallas_call | solution.py:657
  63.8 0.1 collective-permute-start.8
  63.9 1.9 %collective-permute-done.8.refs_1_ = f32[8,4,32,128]{3,2,1,0:T(8,128)S(1)} collective-permute-done((f32[8,4,32,128]{3,2,1,0:T(8,128)S(1)}, f32[8,4,32,128]{3,2,1,0:T(8,128)S(1)}, u32[]{:S(2)}, u32[]{:S(2)}) %collective-permute-start.8) | collective-permute-done | bytes 524320 | tf_op jit(solution)/shard_map/ppermute | solution.py:676
  65.8 0.6 fold.5
  66.4 0.1 collective-permute-start.12
  66.5 0.7 collective-permute-start.9
  67.2 4.8 %collective-permute-done.12.refs_1_ = f32[4,4,16,128]{3,2,1,0:T(8,128)S(1)} collective-permute-done((f32[4,4,16,128]{3,2,1,0:T(8,128)S(1)}, f32[4,4,16,128]{3,2,1,0:T(8,128)S(1)}, u32[]{:S(2)}, u32[]{:S(2)}) %collective-permute-start.12) | collective-permute-done | bytes 131104 | tf_op jit(solution)/shard_map/ppermute | solution.py:699
  72.0 0.6 fold.8
  72.6 0.1 collective-permute-start.13
  72.7 0.0 collective-permute-done.9.refs_1_
  72.7 0.6 fold.6
  73.2 1.2 %collective-permute-start.10 = (f32[2,4,16,128]{3,2,1,0:T(8,128)S(1)}, f32[2,4,16,128]{3,2,1,0:T(8,128)S(1)}, u32[]{:S(2)}, u32[]{:S(2)}) collective-permute-start(f32[2,4,16,128]{3,2,1,0:T(8,128)S(1)} %get-tuple-element.40), channel_id=1, source_target_pairs={{0,4},{1,5},{2,6},{3,7},{4,0},{5,1},{6,2},{7,3},{8,12},{9,13},{10,... | collective-permute-start | bytes 196616 | tf_op jit(solution)/shard_map/ppermute | solution.py:699
  74.4 2.5 %collective-permute-done.13.refs_1_ = f32[2,4,16,128]{3,2,1,0:T(8,128)S(1)} collective-permute-done((f32[2,4,16,128]{3,2,1,0:T(8,128)S(1)}, f32[2,4,16,128]{3,2,1,0:T(8,128)S(1)}, u32[]{:S(2)}, u32[]{:S(2)}) %collective-permute-start.13) | collective-permute-done | bytes 65568 | tf_op jit(solution)/shard_map/ppermute | solution.py:699
  76.9 0.6 fold.9
  77.5 1.2 %collective-permute-start.14 = (f32[1,4,16,128]{3,2,1,0:T(8,128)S(1)}, f32[1,4,16,128]{3,2,1,0:T(8,128)S(1)}, u32[]{:S(2)}, u32[]{:S(2)}) collective-permute-start(f32[1,4,16,128]{3,2,1,0:T(8,128)S(1)} %get-tuple-element.48), channel_id=1, source_target_pairs={{0,8},{1,9},{2,10},{3,11},{4,12},{5,13},{6,14},{7,15},{8,0},{9,1},... | collective-permute-start | bytes 98312 | tf_op jit(solution)/shard_map/ppermute | solution.py:699
  78.6 0.0 collective-permute-done.10.refs_1_
  78.6 0.6 fold.7
  79.2 1.9 %collective-permute-start.11 = (f32[1,4,16,128]{3,2,1,0:T(8,128)S(1)}, f32[1,4,16,128]{3,2,1,0:T(8,128)S(1)}, u32[]{:S(2)}, u32[]{:S(2)}) collective-permute-start(f32[1,4,16,128]{3,2,1,0:T(8,128)S(1)} %get-tuple-element.42), channel_id=1, source_target_pairs={{0,8},{1,9},{2,10},{3,11},{4,12},{5,13},{6,14},{7,15},{8,0},{9,1},... | collective-permute-start | bytes 98312 | tf_op jit(solution)/shard_map/ppermute | solution.py:699
  81.1 1.7 %collective-permute-done.14.refs_3_ = f32[1,4,16,128]{3,2,1,0:T(8,128)S(1)} collective-permute-done((f32[1,4,16,128]{3,2,1,0:T(8,128)S(1)}, f32[1,4,16,128]{3,2,1,0:T(8,128)S(1)}, u32[]{:S(2)}, u32[]{:S(2)}) %collective-permute-start.14) | collective-permute-done | bytes 32800 | tf_op jit(solution)/shard_map/ppermute | solution.py:699
  82.8 1.3 %collective-permute-done.11.refs_1_ = f32[1,4,16,128]{3,2,1,0:T(8,128)S(1)} collective-permute-done((f32[1,4,16,128]{3,2,1,0:T(8,128)S(1)}, f32[1,4,16,128]{3,2,1,0:T(8,128)S(1)}, u32[]{:S(2)}, u32[]{:S(2)}) %collective-permute-start.11) | collective-permute-done | bytes 32800 | tf_op jit(solution)/shard_map/ppermute | solution.py:699
  84.1 0.6 total.1
  (1 shorter events, 0.0 us)
Async XLA Ops:
  0.1 1.4 %copy-start = (f32[64,2,3,2,512]{4,3,2,1,0:T(2,128)S(1)}, f32[64,2,3,2,512]{4,3,2,1,0:T(2,128)}, u32[]{:S(2)}) copy-start(f32[64,2,3,2,512]{4,3,2,1,0:T(2,128)} %param.3) | copy-start | bytes 4718596
  1.5 1.0 %copy-start.1 = (f32[3,2,3,3,2,512]{5,4,3,2,1,0:T(2,128)S(1)}, f32[3,2,3,3,2,512]{5,4,3,2,1,0:T(2,128)}, u32[]{:S(2)}) copy-start(f32[3,2,3,3,2,512]{5,4,3,2,1,0:T(2,128)} %param.4) | copy-start | bytes 663556
  3.7 4.6 %collective-permute-start.2 = (f32[6,72,512]{2,1,0:T(8,128)S(1)}, f32[6,72,512]{2,1,0:T(8,128)S(1)}, u32[]{:S(2)}, u32[]{:S(2)}) collective-permute-start(f32[6,72,512]{2,1,0:T(8,128)S(1)} %get-tuple-element.31.inner.own), channel_id=1, source_target_pairs={{0,1},{1,0},{2,3},{3,2},{4,5},{5,4},{6,7},{7,6},{8,9},{9,8},{10,11... | collective-permute-start | bytes 2654216 | tf_op jit(solution)/shard_map/ppermute | solution.py:597
  9.4 7.9 %collective-permute-start.3 = (f32[6,64,512]{2,1,0:T(8,128)S(1)}, f32[6,64,512]{2,1,0:T(8,128)S(1)}, u32[]{:S(2)}, u32[]{:S(2)}) collective-permute-start(f32[6,64,512]{2,1,0:T(8,128)S(1)} %inner_edge.1.first.inner), channel_id=1, source_target_pairs={{0,1},{1,0},{2,3},{3,2},{4,5},{5,4},{6,7},{7,6},{8,9},{9,8},{10,11... | collective-permute-start | bytes 2359304 | tf_op jit(solution)/shard_map/ppermute | solution.py:607
  9.5 11.3 %collective-permute-start.1 = (f32[6,64,256]{2,1,0:T(8,128)S(1)}, f32[6,64,256]{2,1,0:T(8,128)S(1)}, u32[]{:S(2)}, u32[]{:S(2)}) collective-permute-start(f32[6,64,256]{2,1,0:T(8,128)S(1)} %get-tuple-element.27.after.refs_1_.own), channel_id=1, source_target_pairs={{0,15},{1,2},{2,1},{3,4},{4,3},{5,6},{6,5},{7,8},{8,7},{9,10},{10,... | collective-permute-start | bytes 1179656 | tf_op jit(solution)/shard_map/ppermute | solution.py:594
  15.2 9.9 %collective-permute-start.4 = (f32[6,64,256]{2,1,0:T(8,128)S(1)}, f32[6,64,256]{2,1,0:T(8,128)S(1)}, u32[]{:S(2)}, u32[]{:S(2)}) collective-permute-start(f32[6,64,256]{2,1,0:T(8,128)S(1)} %get-tuple-element.32.refs_0_.own), channel_id=1, source_target_pairs={{0,15},{1,2},{2,1},{3,4},{4,3},{5,6},{6,5},{7,8},{8,7},{9,10},{10,... | collective-permute-start | bytes 1179656 | tf_op jit(solution)/shard_map/ppermute | solution.py:594
  15.3 11.3 %collective-permute-start = (f32[72,128]{1,0:T(8,128)S(1)}, f32[72,128]{1,0:T(8,128)S(1)}, u32[]{:S(2)}, u32[]{:S(2)}) collective-permute-start(f32[72,128]{1,0:T(8,128)S(1)} %get-tuple-element.28.top_links), channel_id=1, source_target_pairs={{0,1},{1,2},{2,3},{3,4},{4,5},{5,6},{6,7},{7,8},{8,9},{9,10},{10,1... | collective-permute-start | bytes 110600 | tf_op jit(solution)/shard_map/ppermute | solution.py:598
  25.2 7.9 %collective-permute-start.5 = (f32[8,128]{1,0:T(8,128)S(1)}, f32[8,128]{1,0:T(8,128)S(1)}, u32[]{:S(2)}, u32[]{:S(2)}) collective-permute-start(f32[8,128]{1,0:T(8,128)S(1)} %fusion), channel_id=1, source_target_pairs={{1,0},{2,3},{5,4},{6,7},{9,8},{10,11},{13,12},{14,15},{17,16},{18,... | collective-permute-start | bytes 12296 | tf_op jit(solution)/shard_map/ppermute | solution.py:617
  33.8 15.2 %collective-permute-start.7 = (f32[6,64,256]{2,1,0:T(8,128)S(1)}, f32[6,64,256]{2,1,0:T(8,128)S(1)}, u32[]{:S(2)}, u32[]{:S(2)}) collective-permute-start(f32[6,64,256]{2,1,0:T(8,128)S(1)} %edge.3.refs_0_), channel_id=1, source_target_pairs={{0,15},{1,2},{2,1},{3,4},{4,3},{5,6},{6,5},{7,8},{8,7},{9,10},{10,... | collective-permute-start | bytes 1179656 | tf_op jit(solution)/shard_map/ppermute | solution.py:594
  46.7 10.0 %collective-permute-start.6 = (f32[6,64,256]{2,1,0:T(8,128)S(1)}, f32[6,64,256]{2,1,0:T(8,128)S(1)}, u32[]{:S(2)}, u32[]{:S(2)}) collective-permute-start(f32[6,64,256]{2,1,0:T(8,128)S(1)} %edge.2.refs_1_), channel_id=1, source_target_pairs={{0,15},{1,2},{2,1},{3,4},{4,3},{5,6},{6,5},{7,8},{8,7},{9,10},{10,... | collective-permute-start | bytes 1179656 | tf_op jit(solution)/shard_map/ppermute | solution.py:594
  49.0 7.6 %copy-start.2 = (s32[63]{0:T(128)S(1)}, s32[63]{0:T(128)}, u32[]{:S(2)}) copy-start(s32[63]{0:T(128)} %slot_ref.1) | copy-start | bytes 760
  63.8 2.0 %collective-permute-start.8 = (f32[8,4,32,128]{3,2,1,0:T(8,128)S(1)}, f32[8,4,32,128]{3,2,1,0:T(8,128)S(1)}, u32[]{:S(2)}, u32[]{:S(2)}) collective-permute-start(f32[8,4,32,128]{3,2,1,0:T(8,128)S(1)} %get-tuple-element.36), channel_id=1, source_target_pairs={{0,1},{1,0},{2,3},{3,2},{4,5},{5,4},{6,7},{7,6},{8,9},{9,8},{10,11... | collective-permute-start | bytes 1572872 | tf_op jit(solution)/shard_map/ppermute | solution.py:676
  66.4 5.6 %collective-permute-start.12 = (f32[4,4,16,128]{3,2,1,0:T(8,128)S(1)}, f32[4,4,16,128]{3,2,1,0:T(8,128)S(1)}, u32[]{:S(2)}, u32[]{:S(2)}) collective-permute-start(f32[4,4,16,128]{3,2,1,0:T(8,128)S(1)} %get-tuple-element.44), channel_id=1, source_target_pairs={{0,4},{1,5},{2,6},{3,7},{4,0},{5,1},{6,2},{7,3},{8,12},{9,13},{10,... | collective-permute-start | bytes 393224 | tf_op jit(solution)/shard_map/ppermute | solution.py:699
  66.5 6.2 %collective-permute-start.9 = (f32[4,4,16,128]{3,2,1,0:T(8,128)S(1)}, f32[4,4,16,128]{3,2,1,0:T(8,128)S(1)}, u32[]{:S(2)}, u32[]{:S(2)}) collective-permute-start(f32[4,4,16,128]{3,2,1,0:T(8,128)S(1)} %get-tuple-element.38), channel_id=1, source_target_pairs={{0,2},{1,3},{2,0},{3,1},{4,6},{5,7},{6,4},{7,5},{8,10},{9,11},{10,... | collective-permute-start | bytes 393224 | tf_op jit(solution)/shard_map/ppermute | solution.py:699
  72.6 4.3 %collective-permute-start.13 = (f32[2,4,16,128]{3,2,1,0:T(8,128)S(1)}, f32[2,4,16,128]{3,2,1,0:T(8,128)S(1)}, u32[]{:S(2)}, u32[]{:S(2)}) collective-permute-start(f32[2,4,16,128]{3,2,1,0:T(8,128)S(1)} %get-tuple-element.46), channel_id=1, source_target_pairs={{0,2},{1,3},{2,0},{3,1},{4,6},{5,7},{6,4},{7,5},{8,10},{9,11},{10,... | collective-permute-start | bytes 196616 | tf_op jit(solution)/shard_map/ppermute | solution.py:699
  73.2 5.4 %collective-permute-start.10 = (f32[2,4,16,128]{3,2,1,0:T(8,128)S(1)}, f32[2,4,16,128]{3,2,1,0:T(8,128)S(1)}, u32[]{:S(2)}, u32[]{:S(2)}) collective-permute-start(f32[2,4,16,128]{3,2,1,0:T(8,128)S(1)} %get-tuple-element.40), channel_id=1, source_target_pairs={{0,4},{1,5},{2,6},{3,7},{4,0},{5,1},{6,2},{7,3},{8,12},{9,13},{10,... | collective-permute-start | bytes 196616 | tf_op jit(solution)/shard_map/ppermute | solution.py:699
  77.5 5.3 %collective-permute-start.14 = (f32[1,4,16,128]{3,2,1,0:T(8,128)S(1)}, f32[1,4,16,128]{3,2,1,0:T(8,128)S(1)}, u32[]{:S(2)}, u32[]{:S(2)}) collective-permute-start(f32[1,4,16,128]{3,2,1,0:T(8,128)S(1)} %get-tuple-element.48), channel_id=1, source_target_pairs={{0,8},{1,9},{2,10},{3,11},{4,12},{5,13},{6,14},{7,15},{8,0},{9,1},... | collective-permute-start | bytes 98312 | tf_op jit(solution)/shard_map/ppermute | solution.py:699
  79.2 4.9 %collective-permute-start.11 = (f32[1,4,16,128]{3,2,1,0:T(8,128)S(1)}, f32[1,4,16,128]{3,2,1,0:T(8,128)S(1)}, u32[]{:S(2)}, u32[]{:S(2)}) collective-permute-start(f32[1,4,16,128]{3,2,1,0:T(8,128)S(1)} %get-tuple-element.42), channel_id=1, source_target_pairs={{0,8},{1,9},{2,10},{3,11},{4,12},{5,13},{6,14},{7,15},{8,0},{9,1},... | collective-permute-start | bytes 98312 | tf_op jit(solution)/shard_map/ppermute | solution.py:699

commit v2 on v1

--- a/solution.py
+++ b/solution.py
@@ -257,7 +257,29 @@
     groups_loop(outer[0].shape[1], step)
 
 
-def inner_hop_kernel(tiles, plane_links, first, out):
+def finish_hop(tiles, chunk, use_low, top_links, low_link, beyond, sums, out, finish):
+    first_tile, count = chunk
+    for tile in range(count):
+        link = z_link(tiles, first_tile + tile, top_links, low_link, use_low)
+        lanes = slice(tile * LANES, (tile + 1) * LANES)
+        at = (first_tile + tile) * LANES
+
+        def step(rows):
+            field = [beyond[part, rows, lanes] for part in range(6)]
+            total = [sums[part, rows, at : at + LANES] for part in range(6)]
+            total = times(link, field, total)
+            for part in range(6):
+                out[part, rows, lanes] = finish(total[part], (part, rows, lanes))
+
+        groups_loop(out.shape[1], step, 2)
+
+
+def inner_step_kernel(tiles, place_ref, top_links, plane_links, partner, sums, first, out):
+    finish_hop(
+        tiles, (0, tiles), place_ref[1] == 1, top_links, partner_rows(partner, first.shape[1]),
+        partner, sums, first, lambda total, index: total * (1.0 / 6.0),
+    )
+
     def step(rows):
         def put(tile, total):
             for part in range(6):
@@ -277,39 +299,11 @@
     groups_loop(out.shape[1], step)
 
 
-def finish_hop(tiles, chunk, use_low, top_links, low_link, beyond, sums, out, finish):
-    first_tile, count = chunk
-    for tile in range(count):
-        link = z_link(tiles, first_tile + tile, top_links, low_link, use_low)
-        lanes = slice(tile * LANES, (tile + 1) * LANES)
-        at = (first_tile + tile) * LANES
-
-        def step(rows):
-            field = [beyond[part, rows, lanes] for part in range(6)]
-            total = [sums[part, rows, at : at + LANES] for part in range(6)]
-            total = times(link, field, total)
-            for part in range(6):
-                out[part, rows, lanes] = finish(total[part], (part, rows, lanes))
-
-        groups_loop(out.shape[1], step, 2)
-
-
-def inner_edge_kernel(tiles, place_ref, top_links, partner, sums, out):
-    finish_hop(
-        tiles, (0, tiles), place_ref[1] == 1, top_links, partner_rows(partner, out.shape[1]),
-        partner, sums, out, lambda total, index: total * (1.0 / 6.0),
-    )
-
-
-def inner_rest_kernel(tiles, place_ref, top_links, linked, partner, sums, own, out):
-    finish_hop(
-        tiles, (0, tiles), place_ref[1] == 1, top_links, partner_rows(linked, out.shape[1]),
-        partner, sums, out, lambda total, index: total * (2.0 / 6.0) - own[index],
-    )
-
-
-def edge_kernel(tiles, chunk, place_ref, top_links, low_links, beyond, sums, token, out):
-    del token
+def edge_kernel(
+    tiles, chunk, place_ref, top_links, low_links, beyond, sums, token, *refs
+):
+    out = refs[1 if len(refs) > 1 else 0]
+    del token, refs
     finish_hop(
         tiles, chunk, place_ref[1] == 0, top_links, low_rows(low_links, tiles), beyond, sums, out,
         lambda total, index: total * (1.0 / 6.0),
@@ -397,27 +391,27 @@
         multiply(now)
 
 
-def inner_pairs_kernel(tiles, chunk_tiles, cross_links, rest, *refs):
+def inner_pairs_kernel(
+    tiles, chunk_tiles, place_ref, top_links, cross_links, linked, partner, partial, own, *refs
+):
     outer, (sums, field, low, quarks) = refs[: len(chunk_tiles)], refs[len(chunk_tiles) :]
+    vectors = field.shape[1]
     for tile in range(tiles):
         ref, from_lanes = tile_of(chunk_tiles, outer, tile)
         lanes = slice(tile * LANES, (tile + 1) * LANES)
-        link = cross_of(cross_links, tiles, tile)
-        found = {
-            (part, row, column): jnp.broadcast_to(link(part, row, column), (ROWS, LANES))
-            for part in range(2)
-            for row in range(3)
-            for column in range(3)
-        }
+        link = z_link(
+            tiles, tile, top_links, partner_rows(linked, vectors), place_ref[1] == 1
+        )
+        cross = cross_of(cross_links, tiles, tile)
 
         def step(rows):
-            source = [ref[part, rows, from_lanes] for part in range(6)]
-            zeros = [jnp.zeros((ROWS, LANES), jnp.float32)] * 6
-            total = adjoint(lambda *index: found[index], source, zeros)
+            total = [partial[part, rows, lanes] for part in range(6)]
+            total = adjoint(cross, [ref[part, rows, from_lanes] for part in range(6)], total)
+            total = times(link, [partner[part, rows, lanes] for part in range(6)], total)
             for part in range(6):
-                field[part, rows, lanes] = rest[part, rows, lanes] + total[part] * (2.0 / 6.0)
-
-        groups_loop(field.shape[1], step, 2)
+                field[part, rows, lanes] = total[part] * (2.0 / 6.0) - own[part, rows, lanes]
+
+        groups_loop(vectors, step, 2)
     sums[...] = jnp.zeros_like(sums)
     width = low.shape[1] // 6
     for start in range(0, field.shape[2], width):
@@ -508,40 +502,32 @@
     def place(block, carry):
         slot = slot_ref[block]
         owner = slot // CAP
-        chip = owner // 2
+        away = jnp.bitwise_xor(owner // 2, place_ref[0])
         value = ordered[pl.ds(pl.multiple_of(block * PB, PB), PB), :]
 
         @pl.when(owner % 2 == my_core)
         def _():
-            keep[chip, slot % CAP] = value
+            keep[away, slot % CAP] = value
 
         @pl.when(owner % 2 != my_core)
         def _():
-            send[chip, slot % CAP] = value
+            send[away, slot % CAP] = value
 
         return carry
 
     lax.fori_loop(0, slot_ref.shape[0], place, 0)
 
 
-def fold_kernel(parts, place_ref, *refs):
-    ins, outs = refs[: -2 * len(parts)], refs[-2 * len(parts) :]
-    for number, (rows, bit, position) in enumerate(parts):
-        kept, received = ins[:2] if len(ins) == 2 else ins[2 * number : 2 * number + 2]
-        stay, leave = outs[2 * number : 2 * number + 2]
-        mine = lax.rem(lax.div(place_ref[0], 1 << bit), 2)
-        for index in range(stay.shape[0]):
-            low = index % (1 << position)
-            base = (index - low) * 2 + low
-            for out, value in ((stay, mine), (leave, 1 - mine)):
-                at = base + value * (1 << position)
-                out[index] = kept[at, :, rows, :] + received[at, :, rows, :]
-
-
-def total_kernel(cut, *refs):
-    out = refs[-1]
-    for number, rows in enumerate(cut):
-        out[:, rows, :] = refs[2 * number][0] + refs[2 * number + 1][0]
+def combine_kernel(kept, received, *outs):
+    for away, out in enumerate(outs):
+        out[...] = kept[away] + received[away]
+
+
+def total_kernel(*refs):
+    total = refs[0][...]
+    for ref in refs[1:-1]:
+        total = total + ref[...]
+    refs[-1][...] = total
 
 
 def on_device(eigen_vectors, link_field, block_slot):
@@ -600,28 +586,31 @@
         functools.partial(local_kernel, tiles, chunk_tiles, (0, 1)), [plane] * 2, "local", 0,
         plane_links, cross_links, inner, *outer, limit=48, flops=4e9,
     )
-    first_inner = call(
-        functools.partial(inner_edge_kernel, tiles), plane, "inner_edge", 1,
-        place, top_links, linked, inner_sums,
-    )
+    first_inner, inner_sums = call(
+        functools.partial(inner_step_kernel, tiles), [plane] * 2, "inner_step", 1,
+        place, top_links, plane_links, linked, inner_sums,
+    )
+    token = sum(field[0, :ROWS, :LANES] for field in [inner_sums, *far])
+    token = lax.ppermute(token, "brick", [(i, i ^ 1) for i in range(count) if i % 4 in (1, 2)])
+    first_outer = []
+    for chunk, piece, field in zip(chunk_tiles, pieces, far):
+        args = (place, top_links, low_links, field, outer_sums, token)
+        if first_outer:
+            first_outer.append(
+                call(functools.partial(edge_kernel, tiles, chunk), piece, "edge", 1, *args)
+            )
+            continue
+        first, first_inner = pl.pallas_call(
+            functools.partial(edge_kernel, tiles, chunk),
+            out_shape=[piece, plane],
+            in_specs=[SMEM] + [VMEM] * 5 + [pl.BlockSpec(memory_space=pl.ANY)],
+            out_specs=[VMEM, pl.BlockSpec(memory_space=pl.ANY)],
+            input_output_aliases={6: 1},
+            compiler_params=params(32),
+            name="edge",
+        )(*args, first_inner)
+        first_outer.append(first)
     partner = lax.ppermute(first_inner, "brick", on_chip)
-    inner_sums = call(
-        functools.partial(inner_hop_kernel, tiles), plane, "inner_hop", 0,
-        plane_links, first_inner, flops=2e9,
-    )
-    rest = call(
-        functools.partial(inner_rest_kernel, tiles), plane, "inner_rest", 1,
-        place, top_links, linked, partner, inner_sums, inner, flops=1e9,
-    )
-    token = sum(field[0, :ROWS, :LANES] for field in [rest, *far])
-    token = lax.ppermute(token, "brick", [(i, i ^ 1) for i in range(count) if i % 4 in (1, 2)])
-    first_outer = [
-        call(
-            functools.partial(edge_kernel, tiles, chunk), piece, "edge", 1,
-            place, top_links, low_links, field, outer_sums, token,
-        )
-        for chunk, piece, field in zip(chunk_tiles, pieces, far)
-    ]
     far = off(first_outer)
     def scratch(width):
         return [
@@ -631,8 +620,8 @@
 
     partial_sums = jax.ShapeDtypeStruct((pair_rows, 2 * vectors), jnp.float32)
     before = call(
-        functools.partial(inner_pairs_kernel, tiles, chunk_tiles), partial_sums, "inner_pairs", 0,
-        cross_links, rest, *first_outer, limit=48, flops=8e9,
+        functools.partial(inner_pairs_kernel, tiles, chunk_tiles), partial_sums, "inner_pairs", 1,
+        place, top_links, cross_links, linked, partner, inner_sums, inner, *first_outer, limit=48, flops=8e9,
         scratch=[pltpu.VMEM(plane.shape, jnp.float32)] + scratch(2 * LANES),
     )
     (sums,) = call(
@@ -674,39 +663,13 @@
         name="last_pairs",
     )(block_slot, place, top_links, low_links, far[-1], sums, outer[-1], before)
     received = lax.ppermute(send, "brick", on_chip)
-    bits = chips.bit_length() - 1
-    cut = (slice(0, PB // 2), slice(PB // 2, PB))
-    orders = [list(range(bits)), list(range(bits))]
-    if bits > 1:
-        orders[1][:2] = [1, 0]
-    remaining = [list(range(bits)), list(range(bits))]
-
-    def fold(halves, stage, rows_of, *pairs):
-        parts, shapes = [], []
-        for half_at in halves:
-            bit = orders[half_at][stage]
-            parts.append((rows_of[half_at], bit, remaining[half_at].index(bit)))
-            remaining[half_at].remove(bit)
-            shape = (2 ** len(remaining[half_at]), CAP, PB // 2, 2 * vectors)
-            shapes += [jax.ShapeDtypeStruct(shape, jnp.float32)] * 2
-        outs = call(
-            functools.partial(fold_kernel, parts), shapes, "fold", 1, place, *pairs
-        )
-        found = []
-        for number, half_at in enumerate(halves):
-            bit = orders[half_at][stage]
-            route = [(i, i ^ (2 << bit)) for i in range(count)]
-            found.append((outs[2 * number], lax.ppermute(outs[2 * number + 1], "brick", route)))
-        return found
-
-    whole = (slice(None), slice(None))
-    pairs = fold((0, 1), 0, cut, keep, received)
-    for stage in range(1, bits):
-        pairs = [fold((half_at,), stage, whole, *pairs[half_at])[0] for half_at in range(2)]
     share = jax.ShapeDtypeStruct((CAP, PB, 2 * vectors), jnp.float32)
-    return call(
-        functools.partial(total_kernel, cut), share, "total", 0, *(ref for pair in pairs for ref in pair)
-    )
+    shares = call(combine_kernel, [share] * chips, "combine", 0, keep, received)
+    arrived = [
+        lax.ppermute(shares[away], "brick", [(i, i ^ (2 * away)) for i in range(count)])
+        for away in reversed(range(1, chips))
+    ]
+    return call(total_kernel, share, "total", 0, shares[0], *arrived)
 
 
 def solution(mesh):

time: 84.9 us -> 77.4 us (0.912)
  waiting for transfers between devices: 28.7 us -> 15.4 us
  starting transfers between devices: 17.5 us -> 26.7 us
  Pallas kernels: 36.7 us -> 33.5 us
    ppermute x6 -> x7, starting transfers between devices: 5.02 us -> 14.2 us  [on_device(): lax.ppermute(shares[away], 'brick', [(i, i ^ 2 * away) for i in range(cou...]
    ppermute x4, waiting for transfers between devices: 10.1 us -> 3.04 us  [off(): return [lax.ppermute(field, 'brick', off_chip) for field in fields]]
    ppermute x6 -> x7, waiting for transfers between devices: 10.4 us -> 4.45 us  [on_device(): lax.ppermute(shares[away], 'brick', [(i, i ^ 2 * away) for i in range(cou...]
    pallas_call x16 -> x9, Pallas kernels: 25.3 us -> 21.3 us  [call(): pl.pallas_call(kernel, out_shape=shapes, in_specs=[SMEM] * smem + [VMEM]...]
  transfers between devices with their start and end apart: 15 -> 16, of which waited for: 9 -> 6; matrix products, arithmetic and copies ran while one was open for 0% -> 0% of each run, Pallas kernels for 29% -> 29%
where the time goes in v2:
time: 77.4 us; the launch traced here: 77.3 us
  Pallas kernels  33.5 us (43%)
  starting transfers between devices  26.7 us (34%)
  waiting for transfers between devices  15.4 us (20%)
  local copies, waits for them, and re-layouts  1.42 us (2%)
    pallas_call x9, Pallas kernels, call(): pl.pallas_call(kernel, out_shape=shapes, in_specs=[SMEM] * smem + [VMEM]...  21.3 us
    ppermute x7, starting transfers between devices, on_device(): lax.ppermute(shares[away], 'brick', [(i, i ^ 2 * away) for i in range(cou...  14.2 us
    ppermute x4, starting transfers between devices, off(): return [lax.ppermute(field, 'brick', off_chip) for field in fields]  10.2 us
    pallas_call x1, Pallas kernels, on_device(): pl.pallas_call(functools.partial(last_pairs_kernel, tiles, chunk_tiles[-1...  7.19 us
    ppermute x1, waiting for transfers between devices, on_device(): lax.ppermute(token, 'brick', [(i, i ^ 1) for i in range(count) if i % 4 i...  6.03 us
    ppermute x7, waiting for transfers between devices, on_device(): lax.ppermute(shares[away], 'brick', [(i, i ^ 2 * away) for i in range(cou...  4.45 us
    pallas_call x1, Pallas kernels, on_device(): pl.pallas_call(functools.partial(outer_pairs_kernel, tiles, chunk), out_s...  4.18 us
    ppermute x4, waiting for transfers between devices, off(): return [lax.ppermute(field, 'brick', off_chip) for field in fields]  3.04 us
  transfers between devices with their start and end apart: 16, of which 6 were waited for; matrix products, arithmetic and copies ran while one was open for 0% of the time, Pallas kernels for 29%

profile of v2, /device:TPU:0, one launch (start us, length us, event | category | flops | bytes accessed | tf_op | source)
XLA Modules:
  0.0 77.3 jit_solution(5537444941983083836)
XLA Ops:
  0.0 0.1 pad_add_fusion.place_ref
  0.1 0.0 copy-start
  0.1 1.4 %copy-done = f32[64,2,3,2,512]{4,3,2,1,0:T(2,128)S(1)} copy-done((f32[64,2,3,2,512]{4,3,2,1,0:T(2,128)S(1)}, f32[64,2,3,2,512]{4,3,2,1,0:T(2,128)}, u32[]{:S(2)}) %copy-start) | copy-done | bytes 1572888
  1.5 0.0 copy-start.1
  1.5 1.0 %outer.1 = (f32[6,64,256]{2,1,0:T(8,128)S(1)}, f32[6,64,256]{2,1,0:T(8,128)S(1)}) custom-call(s32[2]{0:T(128)S(1)} %pad_add_fusion.place_ref, f32[3072,128]{1,0:T(8,128)S(1)} %bitcast.14), custom_call_target="tpu_custom_call" | custom-call | tf_op jit(solution)/shard_map/outer/pallas_call | solution.py:557
  2.5 0.0 copy-done.1
  2.5 1.2 %inner.1 = (f32[6,72,512]{2,1,0:T(8,128)S(1)}, f32[288,128]{1,0:T(8,128)S(1)}, f32[72,128]{1,0:T(8,128)S(1)}, f32[72,128]{1,0:T(8,128)S(1)}) custom-call(s32[2]{0:T(128)S(1)} %pad_add_fusion.place_ref, f32[3072,128]{1,0:T(8,128)S(1)} %bitcast.15, f32[432,128]{1,0:T(8,128)S(1)} %bitcast.16, f32[6,64,256]{2,1,0:T(8,128)S(1)} %get-tuple-element.27.after.refs_1_.own), custom_call_target="tpu_custom_call" | custom-call | tf_op jit(solution)/shard_map/inner/pallas_call | solution.py:557
  3.7 0.5 collective-permute-start.2
  4.2 5.7 %collective-permute-start.1 = (f32[6,64,256]{2,1,0:T(8,128)S(1)}, f32[6,64,256]{2,1,0:T(8,128)S(1)}, u32[]{:S(2)}, u32[]{:S(2)}) collective-permute-start(f32[6,64,256]{2,1,0:T(8,128)S(1)} %get-tuple-element.27.after.refs_1_.own), channel_id=1, source_target_pairs={{0,15},{1,2},{2,1},{3,4},{4,3},{5,6},{6,5},{7,8},{8,7},{9,10},{10,... | collective-permute-start | bytes 1179656 | tf_op jit(solution)/shard_map/ppermute | solution.py:580
  9.9 0.0 collective-permute-start.3
  9.9 0.0 collective-permute-start
  9.9 3.8 %local.1 = (f32[6,64,512]{2,1,0:T(8,128)S(1)}, f32[6,64,512]{2,1,0:T(8,128)S(1)}) custom-call(f32[288,128]{1,0:T(8,128)S(1)} %get-tuple-element.29.plane_links, f32[72,128]{1,0:T(8,128)S(1)} %get-tuple-element.30.cross_links, f32[6,72,512]{2,1,0:T(8,128)S(1)} %get-tuple-element.31.inner.own, f32[6,64,256]{2,1,0:T(8,128)S(1)} %get-tuple-element.32.refs_0_.own, ...), custom_call_target="tpu_custom_call" | custom-call | flops 4000000000 | bytes 1572864 | tf_op jit(solution)/shard_map/local/pallas_call | solution.py:557
  13.7 0.0 collective-permute-done.2.partner.linked
  13.7 3.0 %inner_step.1 = (f32[6,64,512]{2,1,0:T(8,128)S(1)}, f32[6,64,512]{2,1,0:T(8,128)S(1)}) custom-call(s32[2]{0:T(128)S(1)} %pad_add_fusion.place_ref, f32[72,128]{1,0:T(8,128)S(1)} %get-tuple-element.28.top_links, f32[288,128]{1,0:T(8,128)S(1)} %get-tuple-element.29.plane_links, f32[6,72,512]{2,1,0:T(8,128)S(1)} %collective-permute-done.2.partner.linked, ...), custom_call_target="tpu_custom_call" | custom-call | tf_op jit(solution)/shard_map/inner_step/pallas_call | solution.py:557
  16.8 0.0 collective-permute-done.1.beyond
  16.8 3.0 %collective-permute-done.3.beyond = f32[6,64,256]{2,1,0:T(8,128)S(1)} collective-permute-done((f32[6,64,256]{2,1,0:T(8,128)S(1)}, f32[6,64,256]{2,1,0:T(8,128)S(1)}, u32[]{:S(2)}, u32[]{:S(2)}) %collective-permute-start.3) | collective-permute-done | bytes 393248 | tf_op jit(solution)/shard_map/ppermute | solution.py:580
  19.8 1.5 %collective-permute-start.4 = (f32[8,128]{1,0:T(8,128)S(1)}, f32[8,128]{1,0:T(8,128)S(1)}, u32[]{:S(2)}, u32[]{:S(2)}) collective-permute-start(f32[8,128]{1,0:T(8,128)S(1)} %fusion), channel_id=1, source_target_pairs={{1,0},{2,3},{5,4},{6,7},{9,8},{10,11},{13,12},{14,15},{17,16},{18,... | collective-permute-start | bytes 12296 | tf_op jit(solution)/shard_map/ppermute | solution.py:594
  21.3 0.0 collective-permute-done.low_links
  21.3 6.0 %collective-permute-done.4.token = f32[8,128]{1,0:T(8,128)S(1)} collective-permute-done((f32[8,128]{1,0:T(8,128)S(1)}, f32[8,128]{1,0:T(8,128)S(1)}, u32[]{:S(2)}, u32[]{:S(2)}) %collective-permute-start.4) | collective-permute-done | bytes 4128 | tf_op jit(solution)/shard_map/ppermute | solution.py:594
  27.3 0.8 %edge.3 = (f32[6,64,256]{2,1,0:T(8,128)S(1)}, f32[6,64,512]{2,1,0:T(8,128)S(1)}) custom-call(s32[2]{0:T(128)S(1)} %pad_add_fusion.place_ref, f32[72,128]{1,0:T(8,128)S(1)} %get-tuple-element.28.top_links, f32[72,128]{1,0:T(8,128)S(1)} %collective-permute-done.low_links, ...), custom_call_target="tpu_custom_call", output_to_operand_aliasing={{1}: (6, {})} | custom-call | tf_op jit(solution)/shard_map/edge/pallas_call | solution.py:603
  28.1 0.2 collective-permute-start.6
  28.4 4.4 %collective-permute-start.7 = (f32[6,64,256]{2,1,0:T(8,128)S(1)}, f32[6,64,256]{2,1,0:T(8,128)S(1)}, u32[]{:S(2)}, u32[]{:S(2)}) collective-permute-start(f32[6,64,256]{2,1,0:T(8,128)S(1)} %get-tuple-element.38.refs_0_), channel_id=1, source_target_pairs={{0,15},{1,2},{2,1},{3,4},{4,3},{5,6},{6,5},{7,8},{8,7},{9,10},{10,... | collective-permute-start | bytes 1179656 | tf_op jit(solution)/shard_map/ppermute | solution.py:580
  32.8 0.8 %edge.2.refs_1_ = f32[6,64,256]{2,1,0:T(8,128)S(1)} custom-call(s32[2]{0:T(128)S(1)} %pad_add_fusion.place_ref, f32[72,128]{1,0:T(8,128)S(1)} %get-tuple-element.28.top_links, f32[72,128]{1,0:T(8,128)S(1)} %collective-permute-done.low_links, f32[6,64,256]{2,1,0:T(8,128)S(1)} %collective-permute-done.1.beyond, f32[6,64,512]{2,1,0:T(8,128)S(1)} %get-tuple-element.33.sums, ...), custom_call_target="tpu_custom_call" | custom-call | tf_op jit(solution)/shard_map/edge/pallas_call | solution.py:557
  33.6 0.1 collective-permute-start.5
  33.7 0.0 collective-permute-done.6.partner
  33.7 8.6 %inner_pairs.1.refs_2_.before = f32[1280,128]{1,0:T(8,128)S(1)} custom-call(s32[2]{0:T(128)S(1)} %pad_add_fusion.place_ref, f32[72,128]{1,0:T(8,128)S(1)} %get-tuple-element.28.top_links, f32[72,128]{1,0:T(8,128)S(1)} %get-tuple-element.30.cross_links, f32[6,72,512]{2,1,0:T(8,128)S(1)} %collective-permute-done.2.partner.linked, ...), custom_call_target="tpu_custom_call" | custom-call | flops 8000000000 | bytes 1572864 | tf_op jit(solution)/shard_map/inner_pairs/pallas_call | solution.py:557
  42.3 2.2 %outer_hop.1.partial = f32[6,64,512]{2,1,0:T(8,128)S(1)} custom-call(f32[288,128]{1,0:T(8,128)S(1)} %get-tuple-element.29.plane_links, f32[72,128]{1,0:T(8,128)S(1)} %get-tuple-element.30.cross_links, f32[6,64,512]{2,1,0:T(8,128)S(1)} %get-tuple-element.37.inner, f32[6,64,256]{2,1,0:T(8,128)S(1)} %get-tuple-element.38.refs_0_, ...), custom_call_target="tpu_custom_call" | custom-call | flops 2000000000 | bytes 1572864 | tf_op jit(solution)/shard_map/outer_hop/pallas_call | solution.py:557
  44.5 0.0 copy-start.2
  44.5 0.0 collective-permute-done.7.far
  44.5 4.2 %outer_pairs.1.before = f32[1280,128]{1,0:T(8,128)S(1)} custom-call(s32[2]{0:T(128)S(1)} %pad_add_fusion.place_ref, f32[72,128]{1,0:T(8,128)S(1)} %get-tuple-element.28.top_links, f32[72,128]{1,0:T(8,128)S(1)} %collective-permute-done.low_links, f32[6,64,256]{2,1,0:T(8,128)S(1)} %collective-permute-done.7.far, f32[6,64,512]{2,1,0:T(8,128)S(1)} %outer_hop.1.partial, ...), custom_call_target="tpu_custom_call" | custom-call | flops 4000000000 | bytes 2359296 | tf_op jit(solution)/shard_map/outer_pairs/pallas_call | solution.py:632
  48.7 0.0 collective-permute-done.5.far
  48.7 0.0 copy-done.2
  48.7 7.2 %last_pairs.1 = (f32[8,4,32,128]{3,2,1,0:T(8,128)S(1)}, f32[8,4,32,128]{3,2,1,0:T(8,128)S(1)}) custom-call(s32[63]{0:T(128)S(1)} %copy-done.2, s32[2]{0:T(128)S(1)} %pad_add_fusion.place_ref, f32[72,128]{1,0:T(8,128)S(1)} %get-tuple-element.28.top_links, f32[72,128]{1,0:T(8,128)S(1)} %collective-permute-done.low_links, ...), custom_call_target="tpu_custom_call" | custom-call | flops 4000000000 | bytes 2359296 | tf_op jit(solution)/shard_map/last_pairs/pallas_call | solution.py:646
  55.9 0.1 collective-permute-start.8
  56.0 1.9 %collective-permute-done.8.received = f32[8,4,32,128]{3,2,1,0:T(8,128)S(1)} collective-permute-done((f32[8,4,32,128]{3,2,1,0:T(8,128)S(1)}, f32[8,4,32,128]{3,2,1,0:T(8,128)S(1)}, u32[]{:S(2)}, u32[]{:S(2)}) %collective-permute-start.8) | collective-permute-done | bytes 524320 | tf_op jit(solution)/shard_map/ppermute | solution.py:665
  57.9 0.1 combine.1
  57.9 3.7 %collective-permute-start.10 = (f32[4,32,128]{2,1,0:T(8,128)S(1)}, f32[4,32,128]{2,1,0:T(8,128)S(1)}, u32[]{:S(2)}, u32[]{:S(2)}) collective-permute-start(f32[4,32,128]{2,1,0:T(8,128)S(1)} %get-tuple-element.43), channel_id=1, source_target_pairs={{0,12},{1,13},{2,14},{3,15},{4,8},{5,9},{6,10},{7,11},{8,4},{9,5},... | collective-permute-start | bytes 196616 | tf_op jit(solution)/shard_map/ppermute | solution.py:669
  61.6 0.0 collective-permute-start.11
  61.6 3.7 %collective-permute-start.12 = (f32[4,32,128]{2,1,0:T(8,128)S(1)}, f32[4,32,128]{2,1,0:T(8,128)S(1)}, u32[]{:S(2)}, u32[]{:S(2)}) collective-permute-start(f32[4,32,128]{2,1,0:T(8,128)S(1)} %get-tuple-element.45), channel_id=1, source_target_pairs={{0,8},{1,9},{2,10},{3,11},{4,12},{5,13},{6,14},{7,15},{8,0},{9,1},... | collective-permute-start | bytes 196616 | tf_op jit(solution)/shard_map/ppermute | solution.py:669
  65.3 0.0 collective-permute-start.13
  65.3 2.2 %collective-permute-start.14 = (f32[4,32,128]{2,1,0:T(8,128)S(1)}, f32[4,32,128]{2,1,0:T(8,128)S(1)}, u32[]{:S(2)}, u32[]{:S(2)}) collective-permute-start(f32[4,32,128]{2,1,0:T(8,128)S(1)} %get-tuple-element.47), channel_id=1, source_target_pairs={{0,4},{1,5},{2,6},{3,7},{4,0},{5,1},{6,2},{7,3},{8,12},{9,13},{10,... | collective-permute-start | bytes 196616 | tf_op jit(solution)/shard_map/ppermute | solution.py:669
  67.5 0.0 collective-permute-done.10.refs_2_
  67.5 1.3 %collective-permute-start.15 = (f32[4,32,128]{2,1,0:T(8,128)S(1)}, f32[4,32,128]{2,1,0:T(8,128)S(1)}, u32[]{:S(2)}, u32[]{:S(2)}) collective-permute-start(f32[4,32,128]{2,1,0:T(8,128)S(1)} %get-tuple-element.48), channel_id=1, source_target_pairs={{0,2},{1,3},{2,0},{3,1},{4,6},{5,7},{6,4},{7,5},{8,10},{9,11},{10,... | collective-permute-start | bytes 196616 | tf_op jit(solution)/shard_map/ppermute | solution.py:669
  68.8 0.8 %collective-permute-done.11.refs_3_ = f32[4,32,128]{2,1,0:T(8,128)S(1)} collective-permute-done((f32[4,32,128]{2,1,0:T(8,128)S(1)}, f32[4,32,128]{2,1,0:T(8,128)S(1)}, u32[]{:S(2)}, u32[]{:S(2)}) %collective-permute-start.11) | collective-permute-done | bytes 65568 | tf_op jit(solution)/shard_map/ppermute | solution.py:669
  69.6 3.3 %collective-permute-start.9 = (f32[4,32,128]{2,1,0:T(8,128)S(1)}, f32[4,32,128]{2,1,0:T(8,128)S(1)}, u32[]{:S(2)}, u32[]{:S(2)}) collective-permute-start(f32[4,32,128]{2,1,0:T(8,128)S(1)} %get-tuple-element.42), channel_id=1, source_target_pairs={{0,14},{1,15},{2,12},{3,13},{4,10},{5,11},{6,8},{7,9},{8,6},{9,7},... | collective-permute-start | bytes 196616 | tf_op jit(solution)/shard_map/ppermute | solution.py:669
  73.0 0.0 collective-permute-done.12.refs_4_
  73.0 0.0 collective-permute-done.13.refs_5_
  73.0 0.1 collective-permute-done.14.refs_6_
  73.1 0.0 collective-permute-done.15.refs_7_
  73.1 3.6 %collective-permute-done.9.refs_1_ = f32[4,32,128]{2,1,0:T(8,128)S(1)} collective-permute-done((f32[4,32,128]{2,1,0:T(8,128)S(1)}, f32[4,32,128]{2,1,0:T(8,128)S(1)}, u32[]{:S(2)}, u32[]{:S(2)}) %collective-permute-start.9) | collective-permute-done | bytes 65568 | tf_op jit(solution)/shard_map/ppermute | solution.py:669
  76.6 0.7 total.1
  (1 shorter events, 0.0 us)
Async XLA Ops:
  0.1 1.4 %copy-start = (f32[64,2,3,2,512]{4,3,2,1,0:T(2,128)S(1)}, f32[64,2,3,2,512]{4,3,2,1,0:T(2,128)}, u32[]{:S(2)}) copy-start(f32[64,2,3,2,512]{4,3,2,1,0:T(2,128)} %param.3) | copy-start | bytes 4718596
  1.5 1.0 %copy-start.1 = (f32[3,2,3,3,2,512]{5,4,3,2,1,0:T(2,128)S(1)}, f32[3,2,3,3,2,512]{5,4,3,2,1,0:T(2,128)}, u32[]{:S(2)}) copy-start(f32[3,2,3,3,2,512]{5,4,3,2,1,0:T(2,128)} %param.4) | copy-start | bytes 663556
  3.7 10.1 %collective-permute-start.2 = (f32[6,72,512]{2,1,0:T(8,128)S(1)}, f32[6,72,512]{2,1,0:T(8,128)S(1)}, u32[]{:S(2)}, u32[]{:S(2)}) collective-permute-start(f32[6,72,512]{2,1,0:T(8,128)S(1)} %get-tuple-element.31.inner.own), channel_id=1, source_target_pairs={{0,1},{1,0},{2,3},{3,2},{4,5},{5,4},{6,7},{7,6},{8,9},{9,8},{10,11... | collective-permute-start | bytes 2654216 | tf_op jit(solution)/shard_map/ppermute | solution.py:583
  4.2 12.6 %collective-permute-start.1 = (f32[6,64,256]{2,1,0:T(8,128)S(1)}, f32[6,64,256]{2,1,0:T(8,128)S(1)}, u32[]{:S(2)}, u32[]{:S(2)}) collective-permute-start(f32[6,64,256]{2,1,0:T(8,128)S(1)} %get-tuple-element.27.after.refs_1_.own), channel_id=1, source_target_pairs={{0,15},{1,2},{2,1},{3,4},{4,3},{5,6},{6,5},{7,8},{8,7},{9,10},{10,... | collective-permute-start | bytes 1179656 | tf_op jit(solution)/shard_map/ppermute | solution.py:580
  9.9 10.0 %collective-permute-start.3 = (f32[6,64,256]{2,1,0:T(8,128)S(1)}, f32[6,64,256]{2,1,0:T(8,128)S(1)}, u32[]{:S(2)}, u32[]{:S(2)}) collective-permute-start(f32[6,64,256]{2,1,0:T(8,128)S(1)} %get-tuple-element.32.refs_0_.own), channel_id=1, source_target_pairs={{0,15},{1,2},{2,1},{3,4},{4,3},{5,6},{6,5},{7,8},{8,7},{9,10},{10,... | collective-permute-start | bytes 1179656 | tf_op jit(solution)/shard_map/ppermute | solution.py:580
  9.9 11.4 %collective-permute-start = (f32[72,128]{1,0:T(8,128)S(1)}, f32[72,128]{1,0:T(8,128)S(1)}, u32[]{:S(2)}, u32[]{:S(2)}) collective-permute-start(f32[72,128]{1,0:T(8,128)S(1)} %get-tuple-element.28.top_links), channel_id=1, source_target_pairs={{0,1},{1,2},{2,3},{3,4},{4,5},{5,6},{6,7},{7,8},{8,9},{9,10},{10,1... | collective-permute-start | bytes 110600 | tf_op jit(solution)/shard_map/ppermute | solution.py:584
  19.8 7.5 %collective-permute-start.4 = (f32[8,128]{1,0:T(8,128)S(1)}, f32[8,128]{1,0:T(8,128)S(1)}, u32[]{:S(2)}, u32[]{:S(2)}) collective-permute-start(f32[8,128]{1,0:T(8,128)S(1)} %fusion), channel_id=1, source_target_pairs={{1,0},{2,3},{5,4},{6,7},{9,8},{10,11},{13,12},{14,15},{17,16},{18,... | collective-permute-start | bytes 12296 | tf_op jit(solution)/shard_map/ppermute | solution.py:594
  28.1 5.5 %collective-permute-start.6 = (f32[6,64,512]{2,1,0:T(8,128)S(1)}, f32[6,64,512]{2,1,0:T(8,128)S(1)}, u32[]{:S(2)}, u32[]{:S(2)}) collective-permute-start(f32[6,64,512]{2,1,0:T(8,128)S(1)} %get-tuple-element.37.inner), channel_id=1, source_target_pairs={{0,1},{1,0},{2,3},{3,2},{4,5},{5,4},{6,7},{7,6},{8,9},{9,8},{10,11... | collective-permute-start | bytes 2359304 | tf_op jit(solution)/shard_map/ppermute | solution.py:613
  28.4 16.1 %collective-permute-start.7 = (f32[6,64,256]{2,1,0:T(8,128)S(1)}, f32[6,64,256]{2,1,0:T(8,128)S(1)}, u32[]{:S(2)}, u32[]{:S(2)}) collective-permute-start(f32[6,64,256]{2,1,0:T(8,128)S(1)} %get-tuple-element.38.refs_0_), channel_id=1, source_target_pairs={{0,15},{1,2},{2,1},{3,4},{4,3},{5,6},{6,5},{7,8},{8,7},{9,10},{10,... | collective-permute-start | bytes 1179656 | tf_op jit(solution)/shard_map/ppermute | solution.py:580
  33.6 15.1 %collective-permute-start.5 = (f32[6,64,256]{2,1,0:T(8,128)S(1)}, f32[6,64,256]{2,1,0:T(8,128)S(1)}, u32[]{:S(2)}, u32[]{:S(2)}) collective-permute-start(f32[6,64,256]{2,1,0:T(8,128)S(1)} %edge.2.refs_1_), channel_id=1, source_target_pairs={{0,15},{1,2},{2,1},{3,4},{4,3},{5,6},{6,5},{7,8},{8,7},{9,10},{10,... | collective-permute-start | bytes 1179656 | tf_op jit(solution)/shard_map/ppermute | solution.py:580
  44.5 4.2 %copy-start.2 = (s32[63]{0:T(128)S(1)}, s32[63]{0:T(128)}, u32[]{:S(2)}) copy-start(s32[63]{0:T(128)} %slot_ref.1) | copy-start | bytes 760
  55.9 2.0 %collective-permute-start.8 = (f32[8,4,32,128]{3,2,1,0:T(8,128)S(1)}, f32[8,4,32,128]{3,2,1,0:T(8,128)S(1)}, u32[]{:S(2)}, u32[]{:S(2)}) collective-permute-start(f32[8,4,32,128]{3,2,1,0:T(8,128)S(1)} %get-tuple-element.40), channel_id=1, source_target_pairs={{0,1},{1,0},{2,3},{3,2},{4,5},{5,4},{6,7},{7,6},{8,9},{9,8},{10,11... | collective-permute-start | bytes 1572872 | tf_op jit(solution)/shard_map/ppermute | solution.py:665
  57.9 9.6 %collective-permute-start.10 = (f32[4,32,128]{2,1,0:T(8,128)S(1)}, f32[4,32,128]{2,1,0:T(8,128)S(1)}, u32[]{:S(2)}, u32[]{:S(2)}) collective-permute-start(f32[4,32,128]{2,1,0:T(8,128)S(1)} %get-tuple-element.43), channel_id=1, source_target_pairs={{0,12},{1,13},{2,14},{3,15},{4,8},{5,9},{6,10},{7,11},{8,4},{9,5},... | collective-permute-start | bytes 196616 | tf_op jit(solution)/shard_map/ppermute | solution.py:669
  61.6 8.0 %collective-permute-start.11 = (f32[4,32,128]{2,1,0:T(8,128)S(1)}, f32[4,32,128]{2,1,0:T(8,128)S(1)}, u32[]{:S(2)}, u32[]{:S(2)}) collective-permute-start(f32[4,32,128]{2,1,0:T(8,128)S(1)} %get-tuple-element.44), channel_id=1, source_target_pairs={{0,10},{1,11},{2,8},{3,9},{4,14},{5,15},{6,12},{7,13},{8,2},{9,3},... | collective-permute-start | bytes 196616 | tf_op jit(solution)/shard_map/ppermute | solution.py:669
  61.6 11.3 %collective-permute-start.12 = (f32[4,32,128]{2,1,0:T(8,128)S(1)}, f32[4,32,128]{2,1,0:T(8,128)S(1)}, u32[]{:S(2)}, u32[]{:S(2)}) collective-permute-start(f32[4,32,128]{2,1,0:T(8,128)S(1)} %get-tuple-element.45), channel_id=1, source_target_pairs={{0,8},{1,9},{2,10},{3,11},{4,12},{5,13},{6,14},{7,15},{8,0},{9,1},... | collective-permute-start | bytes 196616 | tf_op jit(solution)/shard_map/ppermute | solution.py:669
  65.3 7.7 %collective-permute-start.13 = (f32[4,32,128]{2,1,0:T(8,128)S(1)}, f32[4,32,128]{2,1,0:T(8,128)S(1)}, u32[]{:S(2)}, u32[]{:S(2)}) collective-permute-start(f32[4,32,128]{2,1,0:T(8,128)S(1)} %get-tuple-element.46), channel_id=1, source_target_pairs={{0,6},{1,7},{2,4},{3,5},{4,2},{5,3},{6,0},{7,1},{8,14},{9,15},{10,... | collective-permute-start | bytes 196616 | tf_op jit(solution)/shard_map/ppermute | solution.py:669
  65.3 7.7 %collective-permute-start.14 = (f32[4,32,128]{2,1,0:T(8,128)S(1)}, f32[4,32,128]{2,1,0:T(8,128)S(1)}, u32[]{:S(2)}, u32[]{:S(2)}) collective-permute-start(f32[4,32,128]{2,1,0:T(8,128)S(1)} %get-tuple-element.47), channel_id=1, source_target_pairs={{0,4},{1,5},{2,6},{3,7},{4,0},{5,1},{6,2},{7,3},{8,12},{9,13},{10,... | collective-permute-start | bytes 196616 | tf_op jit(solution)/shard_map/ppermute | solution.py:669
  67.5 5.6 %collective-permute-start.15 = (f32[4,32,128]{2,1,0:T(8,128)S(1)}, f32[4,32,128]{2,1,0:T(8,128)S(1)}, u32[]{:S(2)}, u32[]{:S(2)}) collective-permute-start(f32[4,32,128]{2,1,0:T(8,128)S(1)} %get-tuple-element.48), channel_id=1, source_target_pairs={{0,2},{1,3},{2,0},{3,1},{4,6},{5,7},{6,4},{7,5},{8,10},{9,11},{10,... | collective-permute-start | bytes 196616 | tf_op jit(solution)/shard_map/ppermute | solution.py:669
  69.6 7.0 %collective-permute-start.9 = (f32[4,32,128]{2,1,0:T(8,128)S(1)}, f32[4,32,128]{2,1,0:T(8,128)S(1)}, u32[]{:S(2)}, u32[]{:S(2)}) collective-permute-start(f32[4,32,128]{2,1,0:T(8,128)S(1)} %get-tuple-element.42), channel_id=1, source_target_pairs={{0,14},{1,15},{2,12},{3,13},{4,10},{5,11},{6,8},{7,9},{8,6},{9,7},... | collective-permute-start | bytes 196616 | tf_op jit(solution)/shard_map/ppermute | solution.py:669

commit v3 on v2

--- a/solution.py
+++ b/solution.py
@@ -333,9 +333,6 @@
     combos = pair_tiles(vectors)
     block = ROWS * ROWS
     lefts = sorted({left for left, _ in combos})
-    half = len(lefts) // 2
-    steps = [lefts[:1], lefts[1:half], lefts[half : half + 1], lefts[half + 1 :]]
-
     def form(left):
         numbers = [number for number, combo in enumerate(combos) if combo[0] == left]
         for tile in range(width // LANES):
@@ -373,22 +370,11 @@
                             part * width + at : part * width + at + LANES,
                         ] = jnp.concatenate(made[part], 0).astype(jnp.bfloat16)
 
-    def multiply(step):
-        numbers = [number for number, combo in enumerate(combos) if combo[0] in step]
-        rows = slice(numbers[0] * block, (numbers[-1] + 1) * block)
-        sums[rows, :] += lax.dot_general(
-            quarks[rows, :],
-            low[...],
-            (((1,), (1,)), ((), ())),
-            preferred_element_type=jnp.float32,
-        )
-
-    for left in steps[0]:
+    for left in lefts:
         form(left)
-    for now, later in zip(steps, steps[1:] + [[]]):
-        for left in later:
-            form(left)
-        multiply(now)
+    sums[...] += lax.dot_general(
+        quarks[...], low[...], (((1,), (1,)), ((), ())), preferred_element_type=jnp.float32
+    )
 
 
 def inner_pairs_kernel(
@@ -518,9 +504,18 @@
     lax.fori_loop(0, slot_ref.shape[0], place, 0)
 
 
-def combine_kernel(kept, received, *outs):
-    for away, out in enumerate(outs):
+def combine_kernel(kept, received, far_sent, far_kept, *near):
+    for away, out in enumerate(near):
         out[...] = kept[away] + received[away]
+    for index in range(far_sent.shape[0]):
+        away = len(near) + 2 * index
+        far_kept[index] = kept[away] + received[away]
+        far_sent[index] = kept[away + 1] + received[away + 1]
+
+
+def far_kernel(kept, received, *outs):
+    for index, out in enumerate(outs):
+        out[...] = kept[index] + received[index]
 
 
 def total_kernel(*refs):
@@ -664,10 +659,20 @@
     )(block_slot, place, top_links, low_links, far[-1], sums, outer[-1], before)
     received = lax.ppermute(send, "brick", on_chip)
     share = jax.ShapeDtypeStruct((CAP, PB, 2 * vectors), jnp.float32)
-    shares = call(combine_kernel, [share] * chips, "combine", 0, keep, received)
-    arrived = [
-        lax.ppermute(shares[away], "brick", [(i, i ^ (2 * away)) for i in range(count)])
-        for away in reversed(range(1, chips))
+    near = chips // 2
+    stack = jax.ShapeDtypeStruct((near // 2, CAP, PB, 2 * vectors), jnp.float32)
+    far_sent, far_kept, *shares = call(
+        combine_kernel, [stack] * 2 + [share] * near, "combine", 0, keep, received
+    )
+
+    def to_chip(array, away):
+        return lax.ppermute(array, "brick", [(i, i ^ (2 * away)) for i in range(count)])
+
+    far_received = to_chip(far_sent, 1)
+    far_shares = call(far_kernel, [share] * (near // 2), "far", 0, far_kept, far_received)
+    arrived = [to_chip(shares[away], away) for away in range(1, near)]
+    arrived += [
+        to_chip(far_shares[index], near + 2 * index) for index in reversed(range(near // 2))
     ]
     return call(total_kernel, share, "total", 0, shares[0], *arrived)
 

time: 77.4 us -> 75.7 us (0.978)
  starting transfers between devices: 26.7 us -> 23.9 us
  waiting for transfers between devices: 15.4 us -> 16.6 us
    ppermute x7 -> x6, starting transfers between devices: 14.2 us -> 11.2 us  [to_chip(): lax.ppermute(array, 'brick', [(i, i ^ 2 * away) for i in range(count)])]
    ppermute x7 -> x6, waiting for transfers between devices: 4.45 us -> 5.83 us  [to_chip(): lax.ppermute(array, 'brick', [(i, i ^ 2 * away) for i in range(count)])]
    pallas_call x9 -> x10, Pallas kernels: 21.3 us -> 20.9 us  [call(): pl.pallas_call(kernel, out_shape=shapes, in_specs=[SMEM] * smem + [VMEM]...]
  transfers between devices with their start and end apart: 16 -> 15, of which waited for: 6 -> 6; matrix products, arithmetic and copies ran while one was open for 0% -> 0% of each run, Pallas kernels for 29% -> 29%
where the time goes in v3:
time: 75.7 us; the launch traced here: 75.5 us
  Pallas kernels  33.4 us (44%)
  starting transfers between devices  23.9 us (32%)
  waiting for transfers between devices  16.6 us (22%)
  local copies, waits for them, and re-layouts  1.42 us (2%)
    pallas_call x10, Pallas kernels, call(): pl.pallas_call(kernel, out_shape=shapes, in_specs=[SMEM] * smem + [VMEM]...  20.9 us
    ppermute x6, starting transfers between devices, to_chip(): lax.ppermute(array, 'brick', [(i, i ^ 2 * away) for i in range(count)])  11.2 us
    ppermute x4, starting transfers between devices, off(): return [lax.ppermute(field, 'brick', off_chip) for field in fields]  10.2 us
    pallas_call x1, Pallas kernels, on_device(): pl.pallas_call(functools.partial(last_pairs_kernel, tiles, chunk_tiles[-1...  7.43 us
    ppermute x1, waiting for transfers between devices, on_device(): lax.ppermute(token, 'brick', [(i, i ^ 1) for i in range(count) if i % 4 i...  6.03 us
    ppermute x6, waiting for transfers between devices, to_chip(): lax.ppermute(array, 'brick', [(i, i ^ 2 * away) for i in range(count)])  5.83 us
    pallas_call x1, Pallas kernels, on_device(): pl.pallas_call(functools.partial(outer_pairs_kernel, tiles, chunk), out_s...  4.24 us
    ppermute x4, waiting for transfers between devices, off(): return [lax.ppermute(field, 'brick', off_chip) for field in fields]  3.04 us
  transfers between devices with their start and end apart: 15, of which 6 were waited for; matrix products, arithmetic and copies ran while one was open for 0% of the time, Pallas kernels for 29%

profile of v3, /device:TPU:0, one launch (start us, length us, event | category | flops | bytes accessed | tf_op | source)
XLA Modules:
  0.0 75.5 jit_solution(299160856549049493)
XLA Ops:
  0.0 0.1 pad_add_fusion.place_ref
  0.1 0.0 copy-start
  0.1 1.4 %copy-done = f32[64,2,3,2,512]{4,3,2,1,0:T(2,128)S(1)} copy-done((f32[64,2,3,2,512]{4,3,2,1,0:T(2,128)S(1)}, f32[64,2,3,2,512]{4,3,2,1,0:T(2,128)}, u32[]{:S(2)}) %copy-start) | copy-done | bytes 1572888
  1.5 0.0 copy-start.1
  1.5 1.0 %outer.1 = (f32[6,64,256]{2,1,0:T(8,128)S(1)}, f32[6,64,256]{2,1,0:T(8,128)S(1)}) custom-call(s32[2]{0:T(128)S(1)} %pad_add_fusion.place_ref, f32[3072,128]{1,0:T(8,128)S(1)} %bitcast.14), custom_call_target="tpu_custom_call" | custom-call | tf_op jit(solution)/shard_map/outer/pallas_call | solution.py:552
  2.5 0.0 copy-done.1
  2.5 1.2 %inner.1 = (f32[6,72,512]{2,1,0:T(8,128)S(1)}, f32[288,128]{1,0:T(8,128)S(1)}, f32[72,128]{1,0:T(8,128)S(1)}, f32[72,128]{1,0:T(8,128)S(1)}) custom-call(s32[2]{0:T(128)S(1)} %pad_add_fusion.place_ref, f32[3072,128]{1,0:T(8,128)S(1)} %bitcast.15, f32[432,128]{1,0:T(8,128)S(1)} %bitcast.16, f32[6,64,256]{2,1,0:T(8,128)S(1)} %get-tuple-element.27.after.refs_1_.own), custom_call_target="tpu_custom_call" | custom-call | tf_op jit(solution)/shard_map/inner/pallas_call | solution.py:552
  3.7 0.5 collective-permute-start.2
  4.2 5.7 %collective-permute-start.1 = (f32[6,64,256]{2,1,0:T(8,128)S(1)}, f32[6,64,256]{2,1,0:T(8,128)S(1)}, u32[]{:S(2)}, u32[]{:S(2)}) collective-permute-start(f32[6,64,256]{2,1,0:T(8,128)S(1)} %get-tuple-element.27.after.refs_1_.own), channel_id=1, source_target_pairs={{0,15},{1,2},{2,1},{3,4},{4,3},{5,6},{6,5},{7,8},{8,7},{9,10},{10,... | collective-permute-start | bytes 1179656 | tf_op jit(solution)/shard_map/ppermute | solution.py:575
  9.9 0.0 collective-permute-start.3
  9.9 0.0 collective-permute-start
  9.9 3.8 %local.1 = (f32[6,64,512]{2,1,0:T(8,128)S(1)}, f32[6,64,512]{2,1,0:T(8,128)S(1)}) custom-call(f32[288,128]{1,0:T(8,128)S(1)} %get-tuple-element.29.plane_links, f32[72,128]{1,0:T(8,128)S(1)} %get-tuple-element.30.cross_links, f32[6,72,512]{2,1,0:T(8,128)S(1)} %get-tuple-element.31.inner.own, f32[6,64,256]{2,1,0:T(8,128)S(1)} %get-tuple-element.32.refs_0_.own, ...), custom_call_target="tpu_custom_call" | custom-call | flops 4000000000 | bytes 1572864 | tf_op jit(solution)/shard_map/local/pallas_call | solution.py:552
  13.7 0.0 collective-permute-done.2.partner.linked
  13.7 3.0 %inner_step.1 = (f32[6,64,512]{2,1,0:T(8,128)S(1)}, f32[6,64,512]{2,1,0:T(8,128)S(1)}) custom-call(s32[2]{0:T(128)S(1)} %pad_add_fusion.place_ref, f32[72,128]{1,0:T(8,128)S(1)} %get-tuple-element.28.top_links, f32[288,128]{1,0:T(8,128)S(1)} %get-tuple-element.29.plane_links, f32[6,72,512]{2,1,0:T(8,128)S(1)} %collective-permute-done.2.partner.linked, ...), custom_call_target="tpu_custom_call" | custom-call | tf_op jit(solution)/shard_map/inner_step/pallas_call | solution.py:552
  16.8 0.0 collective-permute-done.1.beyond
  16.8 3.0 %collective-permute-done.3.beyond = f32[6,64,256]{2,1,0:T(8,128)S(1)} collective-permute-done((f32[6,64,256]{2,1,0:T(8,128)S(1)}, f32[6,64,256]{2,1,0:T(8,128)S(1)}, u32[]{:S(2)}, u32[]{:S(2)}) %collective-permute-start.3) | collective-permute-done | bytes 393248 | tf_op jit(solution)/shard_map/ppermute | solution.py:575
  19.8 1.5 %collective-permute-start.4 = (f32[8,128]{1,0:T(8,128)S(1)}, f32[8,128]{1,0:T(8,128)S(1)}, u32[]{:S(2)}, u32[]{:S(2)}) collective-permute-start(f32[8,128]{1,0:T(8,128)S(1)} %fusion), channel_id=1, source_target_pairs={{1,0},{2,3},{5,4},{6,7},{9,8},{10,11},{13,12},{14,15},{17,16},{18,... | collective-permute-start | bytes 12296 | tf_op jit(solution)/shard_map/ppermute | solution.py:589
  21.3 0.0 collective-permute-done.low_links
  21.3 6.0 %collective-permute-done.4.token = f32[8,128]{1,0:T(8,128)S(1)} collective-permute-done((f32[8,128]{1,0:T(8,128)S(1)}, f32[8,128]{1,0:T(8,128)S(1)}, u32[]{:S(2)}, u32[]{:S(2)}) %collective-permute-start.4) | collective-permute-done | bytes 4128 | tf_op jit(solution)/shard_map/ppermute | solution.py:589
  27.3 0.8 %edge.3 = (f32[6,64,256]{2,1,0:T(8,128)S(1)}, f32[6,64,512]{2,1,0:T(8,128)S(1)}) custom-call(s32[2]{0:T(128)S(1)} %pad_add_fusion.place_ref, f32[72,128]{1,0:T(8,128)S(1)} %get-tuple-element.28.top_links, f32[72,128]{1,0:T(8,128)S(1)} %collective-permute-done.low_links, ...), custom_call_target="tpu_custom_call", output_to_operand_aliasing={{1}: (6, {})} | custom-call | tf_op jit(solution)/shard_map/edge/pallas_call | solution.py:598
  28.1 0.2 collective-permute-start.6
  28.4 4.4 %collective-permute-start.7 = (f32[6,64,256]{2,1,0:T(8,128)S(1)}, f32[6,64,256]{2,1,0:T(8,128)S(1)}, u32[]{:S(2)}, u32[]{:S(2)}) collective-permute-start(f32[6,64,256]{2,1,0:T(8,128)S(1)} %get-tuple-element.38.refs_0_), channel_id=1, source_target_pairs={{0,15},{1,2},{2,1},{3,4},{4,3},{5,6},{6,5},{7,8},{8,7},{9,10},{10,... | collective-permute-start | bytes 1179656 | tf_op jit(solution)/shard_map/ppermute | solution.py:575
  32.8 0.8 %edge.2.refs_1_ = f32[6,64,256]{2,1,0:T(8,128)S(1)} custom-call(s32[2]{0:T(128)S(1)} %pad_add_fusion.place_ref, f32[72,128]{1,0:T(8,128)S(1)} %get-tuple-element.28.top_links, f32[72,128]{1,0:T(8,128)S(1)} %collective-permute-done.low_links, f32[6,64,256]{2,1,0:T(8,128)S(1)} %collective-permute-done.1.beyond, f32[6,64,512]{2,1,0:T(8,128)S(1)} %get-tuple-element.33.sums, ...), custom_call_target="tpu_custom_call" | custom-call | tf_op jit(solution)/shard_map/edge/pallas_call | solution.py:552
  33.6 0.1 collective-permute-start.5
  33.7 0.0 collective-permute-done.6.partner
  33.7 8.2 %inner_pairs.1.refs_2_.before = f32[1280,128]{1,0:T(8,128)S(1)} custom-call(s32[2]{0:T(128)S(1)} %pad_add_fusion.place_ref, f32[72,128]{1,0:T(8,128)S(1)} %get-tuple-element.28.top_links, f32[72,128]{1,0:T(8,128)S(1)} %get-tuple-element.30.cross_links, f32[6,72,512]{2,1,0:T(8,128)S(1)} %collective-permute-done.2.partner.linked, ...), custom_call_target="tpu_custom_call" | custom-call | flops 8000000000 | bytes 1572864 | tf_op jit(solution)/shard_map/inner_pairs/pallas_call | solution.py:552
  41.9 2.2 %outer_hop.1.partial = f32[6,64,512]{2,1,0:T(8,128)S(1)} custom-call(f32[288,128]{1,0:T(8,128)S(1)} %get-tuple-element.29.plane_links, f32[72,128]{1,0:T(8,128)S(1)} %get-tuple-element.30.cross_links, f32[6,64,512]{2,1,0:T(8,128)S(1)} %get-tuple-element.37.inner, f32[6,64,256]{2,1,0:T(8,128)S(1)} %get-tuple-element.38.refs_0_, ...), custom_call_target="tpu_custom_call" | custom-call | flops 2000000000 | bytes 1572864 | tf_op jit(solution)/shard_map/outer_hop/pallas_call | solution.py:552
  44.1 0.0 copy-start.2
  44.1 0.0 collective-permute-done.7.far
  44.1 4.2 %outer_pairs.1.before = f32[1280,128]{1,0:T(8,128)S(1)} custom-call(s32[2]{0:T(128)S(1)} %pad_add_fusion.place_ref, f32[72,128]{1,0:T(8,128)S(1)} %get-tuple-element.28.top_links, f32[72,128]{1,0:T(8,128)S(1)} %collective-permute-done.low_links, f32[6,64,256]{2,1,0:T(8,128)S(1)} %collective-permute-done.7.far, f32[6,64,512]{2,1,0:T(8,128)S(1)} %outer_hop.1.partial, ...), custom_call_target="tpu_custom_call" | custom-call | flops 4000000000 | bytes 2359296 | tf_op jit(solution)/shard_map/outer_pairs/pallas_call | solution.py:627
  48.3 0.0 collective-permute-done.5.far
  48.4 0.0 copy-done.2
  48.4 7.4 %last_pairs.1 = (f32[8,4,32,128]{3,2,1,0:T(8,128)S(1)}, f32[8,4,32,128]{3,2,1,0:T(8,128)S(1)}) custom-call(s32[63]{0:T(128)S(1)} %copy-done.2, s32[2]{0:T(128)S(1)} %pad_add_fusion.place_ref, f32[72,128]{1,0:T(8,128)S(1)} %get-tuple-element.28.top_links, f32[72,128]{1,0:T(8,128)S(1)} %collective-permute-done.low_links, ...), custom_call_target="tpu_custom_call" | custom-call | flops 4000000000 | bytes 2359296 | tf_op jit(solution)/shard_map/last_pairs/pallas_call | solution.py:641
  55.8 0.3 collective-permute-start.8
  56.1 1.7 %collective-permute-done.8.received = f32[8,4,32,128]{3,2,1,0:T(8,128)S(1)} collective-permute-done((f32[8,4,32,128]{3,2,1,0:T(8,128)S(1)}, f32[8,4,32,128]{3,2,1,0:T(8,128)S(1)}, u32[]{:S(2)}, u32[]{:S(2)}) %collective-permute-start.8) | collective-permute-done | bytes 524320 | tf_op jit(solution)/shard_map/ppermute | solution.py:660
  57.8 0.1 combine.1
  57.8 1.5 %collective-permute-start.12 = (f32[2,4,32,128]{3,2,1,0:T(8,128)S(1)}, f32[2,4,32,128]{3,2,1,0:T(8,128)S(1)}, u32[]{:S(2)}, u32[]{:S(2)}) collective-permute-start(f32[2,4,32,128]{3,2,1,0:T(8,128)S(1)} %get-tuple-element.46), channel_id=1, source_target_pairs={{0,2},{1,3},{2,0},{3,1},{4,6},{5,7},{6,4},{7,5},{8,10},{9,11},{10,... | collective-permute-start | bytes 393224 | tf_op jit(solution)/shard_map/ppermute | solution.py:669
  59.4 1.6 %collective-permute-start.10 = (f32[4,32,128]{2,1,0:T(8,128)S(1)}, f32[4,32,128]{2,1,0:T(8,128)S(1)}, u32[]{:S(2)}, u32[]{:S(2)}) collective-permute-start(f32[4,32,128]{2,1,0:T(8,128)S(1)} %get-tuple-element.43), channel_id=1, source_target_pairs={{0,4},{1,5},{2,6},{3,7},{4,0},{5,1},{6,2},{7,3},{8,12},{9,13},{10,... | collective-permute-start | bytes 196616 | tf_op jit(solution)/shard_map/ppermute | solution.py:669
  61.0 0.4 collective-permute-start.11
  61.4 1.5 %collective-permute-start.9 = (f32[4,32,128]{2,1,0:T(8,128)S(1)}, f32[4,32,128]{2,1,0:T(8,128)S(1)}, u32[]{:S(2)}, u32[]{:S(2)}) collective-permute-start(f32[4,32,128]{2,1,0:T(8,128)S(1)} %get-tuple-element.42), channel_id=1, source_target_pairs={{0,2},{1,3},{2,0},{3,1},{4,6},{5,7},{6,4},{7,5},{8,10},{9,11},{10,... | collective-permute-start | bytes 196616 | tf_op jit(solution)/shard_map/ppermute | solution.py:669
  62.9 0.7 collective-permute-done.12.received
  63.6 6.2 %collective-permute-start.13 = (f32[4,32,128]{2,1,0:T(8,128)S(1)}, f32[4,32,128]{2,1,0:T(8,128)S(1)}, u32[]{:S(2)}, u32[]{:S(2)}) collective-permute-start(f32[4,32,128]{2,1,0:T(8,128)S(1)} %get-tuple-element.47), channel_id=1, source_target_pairs={{0,12},{1,13},{2,14},{3,15},{4,8},{5,9},{6,10},{7,11},{8,4},{9,5},... | collective-permute-start | bytes 196616 | tf_op jit(solution)/shard_map/ppermute | solution.py:669
  69.7 0.0 collective-permute-start.14
  69.7 0.0 collective-permute-done.10.refs_2_
  69.7 0.0 collective-permute-done.11.refs_3_
  69.7 0.0 collective-permute-done.9.refs_1_
  69.8 2.3 %collective-permute-done.13.refs_4_ = f32[4,32,128]{2,1,0:T(8,128)S(1)} collective-permute-done((f32[4,32,128]{2,1,0:T(8,128)S(1)}, f32[4,32,128]{2,1,0:T(8,128)S(1)}, u32[]{:S(2)}, u32[]{:S(2)}) %collective-permute-start.13) | collective-permute-done | bytes 65568 | tf_op jit(solution)/shard_map/ppermute | solution.py:669
  72.1 2.8 %collective-permute-done.14.refs_5_ = f32[4,32,128]{2,1,0:T(8,128)S(1)} collective-permute-done((f32[4,32,128]{2,1,0:T(8,128)S(1)}, f32[4,32,128]{2,1,0:T(8,128)S(1)}, u32[]{:S(2)}, u32[]{:S(2)}) %collective-permute-start.14) | collective-permute-done | bytes 65568 | tf_op jit(solution)/shard_map/ppermute | solution.py:669
  74.9 0.7 total.1
  (2 shorter events, 0.0 us)
Async XLA Ops:
  0.1 1.4 %copy-start = (f32[64,2,3,2,512]{4,3,2,1,0:T(2,128)S(1)}, f32[64,2,3,2,512]{4,3,2,1,0:T(2,128)}, u32[]{:S(2)}) copy-start(f32[64,2,3,2,512]{4,3,2,1,0:T(2,128)} %param.3) | copy-start | bytes 4718596
  1.5 1.0 %copy-start.1 = (f32[3,2,3,3,2,512]{5,4,3,2,1,0:T(2,128)S(1)}, f32[3,2,3,3,2,512]{5,4,3,2,1,0:T(2,128)}, u32[]{:S(2)}) copy-start(f32[3,2,3,3,2,512]{5,4,3,2,1,0:T(2,128)} %param.4) | copy-start | bytes 663556
  3.7 10.1 %collective-permute-start.2 = (f32[6,72,512]{2,1,0:T(8,128)S(1)}, f32[6,72,512]{2,1,0:T(8,128)S(1)}, u32[]{:S(2)}, u32[]{:S(2)}) collective-permute-start(f32[6,72,512]{2,1,0:T(8,128)S(1)} %get-tuple-element.31.inner.own), channel_id=1, source_target_pairs={{0,1},{1,0},{2,3},{3,2},{4,5},{5,4},{6,7},{7,6},{8,9},{9,8},{10,11... | collective-permute-start | bytes 2654216 | tf_op jit(solution)/shard_map/ppermute | solution.py:578
  4.2 12.6 %collective-permute-start.1 = (f32[6,64,256]{2,1,0:T(8,128)S(1)}, f32[6,64,256]{2,1,0:T(8,128)S(1)}, u32[]{:S(2)}, u32[]{:S(2)}) collective-permute-start(f32[6,64,256]{2,1,0:T(8,128)S(1)} %get-tuple-element.27.after.refs_1_.own), channel_id=1, source_target_pairs={{0,15},{1,2},{2,1},{3,4},{4,3},{5,6},{6,5},{7,8},{8,7},{9,10},{10,... | collective-permute-start | bytes 1179656 | tf_op jit(solution)/shard_map/ppermute | solution.py:575
  9.9 10.0 %collective-permute-start.3 = (f32[6,64,256]{2,1,0:T(8,128)S(1)}, f32[6,64,256]{2,1,0:T(8,128)S(1)}, u32[]{:S(2)}, u32[]{:S(2)}) collective-permute-start(f32[6,64,256]{2,1,0:T(8,128)S(1)} %get-tuple-element.32.refs_0_.own), channel_id=1, source_target_pairs={{0,15},{1,2},{2,1},{3,4},{4,3},{5,6},{6,5},{7,8},{8,7},{9,10},{10,... | collective-permute-start | bytes 1179656 | tf_op jit(solution)/shard_map/ppermute | solution.py:575
  9.9 11.4 %collective-permute-start = (f32[72,128]{1,0:T(8,128)S(1)}, f32[72,128]{1,0:T(8,128)S(1)}, u32[]{:S(2)}, u32[]{:S(2)}) collective-permute-start(f32[72,128]{1,0:T(8,128)S(1)} %get-tuple-element.28.top_links), channel_id=1, source_target_pairs={{0,1},{1,2},{2,3},{3,4},{4,5},{5,6},{6,7},{7,8},{8,9},{9,10},{10,1... | collective-permute-start | bytes 110600 | tf_op jit(solution)/shard_map/ppermute | solution.py:579
  19.8 7.5 %collective-permute-start.4 = (f32[8,128]{1,0:T(8,128)S(1)}, f32[8,128]{1,0:T(8,128)S(1)}, u32[]{:S(2)}, u32[]{:S(2)}) collective-permute-start(f32[8,128]{1,0:T(8,128)S(1)} %fusion), channel_id=1, source_target_pairs={{1,0},{2,3},{5,4},{6,7},{9,8},{10,11},{13,12},{14,15},{17,16},{18,... | collective-permute-start | bytes 12296 | tf_op jit(solution)/shard_map/ppermute | solution.py:589
  28.1 5.5 %collective-permute-start.6 = (f32[6,64,512]{2,1,0:T(8,128)S(1)}, f32[6,64,512]{2,1,0:T(8,128)S(1)}, u32[]{:S(2)}, u32[]{:S(2)}) collective-permute-start(f32[6,64,512]{2,1,0:T(8,128)S(1)} %get-tuple-element.37.inner), channel_id=1, source_target_pairs={{0,1},{1,0},{2,3},{3,2},{4,5},{5,4},{6,7},{7,6},{8,9},{9,8},{10,11... | collective-permute-start | bytes 2359304 | tf_op jit(solution)/shard_map/ppermute | solution.py:608
  28.4 15.7 %collective-permute-start.7 = (f32[6,64,256]{2,1,0:T(8,128)S(1)}, f32[6,64,256]{2,1,0:T(8,128)S(1)}, u32[]{:S(2)}, u32[]{:S(2)}) collective-permute-start(f32[6,64,256]{2,1,0:T(8,128)S(1)} %get-tuple-element.38.refs_0_), channel_id=1, source_target_pairs={{0,15},{1,2},{2,1},{3,4},{4,3},{5,6},{6,5},{7,8},{8,7},{9,10},{10,... | collective-permute-start | bytes 1179656 | tf_op jit(solution)/shard_map/ppermute | solution.py:575
  33.6 14.8 %collective-permute-start.5 = (f32[6,64,256]{2,1,0:T(8,128)S(1)}, f32[6,64,256]{2,1,0:T(8,128)S(1)}, u32[]{:S(2)}, u32[]{:S(2)}) collective-permute-start(f32[6,64,256]{2,1,0:T(8,128)S(1)} %edge.2.refs_1_), channel_id=1, source_target_pairs={{0,15},{1,2},{2,1},{3,4},{4,3},{5,6},{6,5},{7,8},{8,7},{9,10},{10,... | collective-permute-start | bytes 1179656 | tf_op jit(solution)/shard_map/ppermute | solution.py:575
  44.1 4.3 %copy-start.2 = (s32[63]{0:T(128)S(1)}, s32[63]{0:T(128)}, u32[]{:S(2)}) copy-start(s32[63]{0:T(128)} %slot_ref.1) | copy-start | bytes 760
  55.8 2.0 %collective-permute-start.8 = (f32[8,4,32,128]{3,2,1,0:T(8,128)S(1)}, f32[8,4,32,128]{3,2,1,0:T(8,128)S(1)}, u32[]{:S(2)}, u32[]{:S(2)}) collective-permute-start(f32[8,4,32,128]{3,2,1,0:T(8,128)S(1)} %get-tuple-element.40), channel_id=1, source_target_pairs={{0,1},{1,0},{2,3},{3,2},{4,5},{5,4},{6,7},{7,6},{8,9},{9,8},{10,11... | collective-permute-start | bytes 1572872 | tf_op jit(solution)/shard_map/ppermute | solution.py:660
  57.8 5.7 %collective-permute-start.12 = (f32[2,4,32,128]{3,2,1,0:T(8,128)S(1)}, f32[2,4,32,128]{3,2,1,0:T(8,128)S(1)}, u32[]{:S(2)}, u32[]{:S(2)}) collective-permute-start(f32[2,4,32,128]{3,2,1,0:T(8,128)S(1)} %get-tuple-element.46), channel_id=1, source_target_pairs={{0,2},{1,3},{2,0},{3,1},{4,6},{5,7},{6,4},{7,5},{8,10},{9,11},{10,... | collective-permute-start | bytes 393224 | tf_op jit(solution)/shard_map/ppermute | solution.py:669
  59.4 10.4 %collective-permute-start.10 = (f32[4,32,128]{2,1,0:T(8,128)S(1)}, f32[4,32,128]{2,1,0:T(8,128)S(1)}, u32[]{:S(2)}, u32[]{:S(2)}) collective-permute-start(f32[4,32,128]{2,1,0:T(8,128)S(1)} %get-tuple-element.43), channel_id=1, source_target_pairs={{0,4},{1,5},{2,6},{3,7},{4,0},{5,1},{6,2},{7,3},{8,12},{9,13},{10,... | collective-permute-start | bytes 196616 | tf_op jit(solution)/shard_map/ppermute | solution.py:669
  61.0 8.8 %collective-permute-start.11 = (f32[4,32,128]{2,1,0:T(8,128)S(1)}, f32[4,32,128]{2,1,0:T(8,128)S(1)}, u32[]{:S(2)}, u32[]{:S(2)}) collective-permute-start(f32[4,32,128]{2,1,0:T(8,128)S(1)} %get-tuple-element.44), channel_id=1, source_target_pairs={{0,6},{1,7},{2,4},{3,5},{4,2},{5,3},{6,0},{7,1},{8,14},{9,15},{10,... | collective-permute-start | bytes 196616 | tf_op jit(solution)/shard_map/ppermute | solution.py:669
  61.4 8.4 %collective-permute-start.9 = (f32[4,32,128]{2,1,0:T(8,128)S(1)}, f32[4,32,128]{2,1,0:T(8,128)S(1)}, u32[]{:S(2)}, u32[]{:S(2)}) collective-permute-start(f32[4,32,128]{2,1,0:T(8,128)S(1)} %get-tuple-element.42), channel_id=1, source_target_pairs={{0,2},{1,3},{2,0},{3,1},{4,6},{5,7},{6,4},{7,5},{8,10},{9,11},{10,... | collective-permute-start | bytes 196616 | tf_op jit(solution)/shard_map/ppermute | solution.py:669
  63.6 8.5 %collective-permute-start.13 = (f32[4,32,128]{2,1,0:T(8,128)S(1)}, f32[4,32,128]{2,1,0:T(8,128)S(1)}, u32[]{:S(2)}, u32[]{:S(2)}) collective-permute-start(f32[4,32,128]{2,1,0:T(8,128)S(1)} %get-tuple-element.47), channel_id=1, source_target_pairs={{0,12},{1,13},{2,14},{3,15},{4,8},{5,9},{6,10},{7,11},{8,4},{9,5},... | collective-permute-start | bytes 196616 | tf_op jit(solution)/shard_map/ppermute | solution.py:669
  69.7 5.2 %collective-permute-start.14 = (f32[4,32,128]{2,1,0:T(8,128)S(1)}, f32[4,32,128]{2,1,0:T(8,128)S(1)}, u32[]{:S(2)}, u32[]{:S(2)}) collective-permute-start(f32[4,32,128]{2,1,0:T(8,128)S(1)} %get-tuple-element.48), channel_id=1, source_target_pairs={{0,8},{1,9},{2,10},{3,11},{4,12},{5,13},{6,14},{7,15},{8,0},{9,1},... | collective-permute-start | bytes 196616 | tf_op jit(solution)/shard_map/ppermute | solution.py:669

commit v4 on v3

--- a/solution.py
+++ b/solution.py
@@ -474,34 +474,26 @@
 
 def last_pairs_kernel(
     tiles, chunk, factor, slot_ref, place_ref, top_links, low_links, far, partial, own, before,
-    keep, send, sums, field, low, quarks, grid, crossed, ordered,
+    keep, send, sums, field, low, quarks, grid, crossed, ordered, both,
 ):
     outer_pairs_kernel(
         tiles, chunk, place_ref, top_links, low_links, far, partial, own, before, sums, field, low,
         quarks,
     )
     arrange(sums, grid, crossed, ordered, factor)
-    keep[...] = jnp.zeros_like(keep)
-    send[...] = jnp.zeros_like(send)
-    my_core = place_ref[1]
+    both[...] = jnp.zeros_like(both)
 
     def place(block, carry):
         slot = slot_ref[block]
         owner = slot // CAP
+        other = jnp.bitwise_xor(owner % 2, place_ref[1])
         away = jnp.bitwise_xor(owner // 2, place_ref[0])
-        value = ordered[pl.ds(pl.multiple_of(block * PB, PB), PB), :]
-
-        @pl.when(owner % 2 == my_core)
-        def _():
-            keep[away, slot % CAP] = value
-
-        @pl.when(owner % 2 != my_core)
-        def _():
-            send[away, slot % CAP] = value
-
+        both[other, away, slot % CAP] = ordered[pl.ds(pl.multiple_of(block * PB, PB), PB), :]
         return carry
 
-    lax.fori_loop(0, slot_ref.shape[0], place, 0)
+    lax.fori_loop(0, slot_ref.shape[0], place, 0, unroll=7 if slot_ref.shape[0] % 7 == 0 else 1)
+    keep[...] = both[0]
+    send[...] = both[1]
 
 
 def combine_kernel(kept, received, far_sent, far_kept, *near):
@@ -652,6 +644,7 @@
             pltpu.VMEM((vectors * vectors // 2, 2 * vectors), jnp.float32),
             pltpu.VMEM((vectors * vectors // 4, 2 * vectors), jnp.float32),
             pltpu.VMEM((blocks, 2 * vectors), jnp.float32),
+            pltpu.VMEM((2,) + half.shape, jnp.float32),
         ],
         compiler_params=params(48),
         cost_estimate=cost(4e9, 3 * plane_bytes),
@@ -672,7 +665,7 @@
     far_shares = call(far_kernel, [share] * (near // 2), "far", 0, far_kept, far_received)
     arrived = [to_chip(shares[away], away) for away in range(1, near)]
     arrived += [
-        to_chip(far_shares[index], near + 2 * index) for index in reversed(range(near // 2))
+        to_chip(far_shares[index], near + 2 * index) for index in range(near // 2)
     ]
     return call(total_kernel, share, "total", 0, shares[0], *arrived)
 

time: 75.7 us -> 72.8 us (0.962)
  waiting for transfers between devices: 16.6 us -> 14.4 us
  Pallas kernels: 33.4 us -> 32.4 us
    ppermute x6, waiting for transfers between devices: 5.83 us -> 3.61 us  [to_chip(): lax.ppermute(array, 'brick', [(i, i ^ 2 * away) for i in range(count)])]
    pallas_call x1, Pallas kernels: 7.43 us -> 6.41 us  [on_device(): pl.pallas_call(functools.partial(last_pairs_kernel, tiles, chunk_tiles[-1...]
  transfers between devices with their start and end apart: 15 -> 15, of which waited for: 6 -> 5; matrix products, arithmetic and copies ran while one was open for 0% -> 0% of each run, Pallas kernels for 29% -> 31%
where the time goes in v4:
time: 72.8 us; the launch traced here: 72.6 us
  Pallas kernels  32.4 us (45%)
  starting transfers between devices  24.3 us (33%)
  waiting for transfers between devices  14.4 us (20%)
  local copies, waits for them, and re-layouts  1.42 us (2%)
    pallas_call x10, Pallas kernels, call(): pl.pallas_call(kernel, out_shape=shapes, in_specs=[SMEM] * smem + [VMEM]...  20.9 us
    ppermute x6, starting transfers between devices, to_chip(): lax.ppermute(array, 'brick', [(i, i ^ 2 * away) for i in range(count)])  11.5 us
    ppermute x4, starting transfers between devices, off(): return [lax.ppermute(field, 'brick', off_chip) for field in fields]  10.2 us
    pallas_call x1, Pallas kernels, on_device(): pl.pallas_call(functools.partial(last_pairs_kernel, tiles, chunk_tiles[-1...  6.41 us
    ppermute x1, waiting for transfers between devices, on_device(): lax.ppermute(token, 'brick', [(i, i ^ 1) for i in range(count) if i % 4 i...  6.03 us
    pallas_call x1, Pallas kernels, on_device(): pl.pallas_call(functools.partial(outer_pairs_kernel, tiles, chunk), out_s...  4.24 us
    ppermute x6, waiting for transfers between devices, to_chip(): lax.ppermute(array, 'brick', [(i, i ^ 2 * away) for i in range(count)])  3.61 us
    ppermute x4, waiting for transfers between devices, off(): return [lax.ppermute(field, 'brick', off_chip) for field in fields]  3.04 us
  transfers between devices with their start and end apart: 15, of which 5 were waited for; matrix products, arithmetic and copies ran while one was open for 0% of the time, Pallas kernels for 31%

profile of v4, /device:TPU:0, one launch (start us, length us, event | category | flops | bytes accessed | tf_op | source)
XLA Modules:
  0.0 72.6 jit_solution(4705365215019003136)
XLA Ops:
  0.0 0.1 pad_add_fusion.place_ref
  0.1 0.0 copy-start
  0.1 1.4 %copy-done = f32[64,2,3,2,512]{4,3,2,1,0:T(2,128)S(1)} copy-done((f32[64,2,3,2,512]{4,3,2,1,0:T(2,128)S(1)}, f32[64,2,3,2,512]{4,3,2,1,0:T(2,128)}, u32[]{:S(2)}) %copy-start) | copy-done | bytes 1572888
  1.5 0.0 copy-start.1
  1.5 1.0 %outer.1 = (f32[6,64,256]{2,1,0:T(8,128)S(1)}, f32[6,64,256]{2,1,0:T(8,128)S(1)}) custom-call(s32[2]{0:T(128)S(1)} %pad_add_fusion.place_ref, f32[3072,128]{1,0:T(8,128)S(1)} %bitcast.14), custom_call_target="tpu_custom_call" | custom-call | tf_op jit(solution)/shard_map/outer/pallas_call | solution.py:544
  2.5 0.0 copy-done.1
  2.5 1.2 %inner.1 = (f32[6,72,512]{2,1,0:T(8,128)S(1)}, f32[288,128]{1,0:T(8,128)S(1)}, f32[72,128]{1,0:T(8,128)S(1)}, f32[72,128]{1,0:T(8,128)S(1)}) custom-call(s32[2]{0:T(128)S(1)} %pad_add_fusion.place_ref, f32[3072,128]{1,0:T(8,128)S(1)} %bitcast.15, f32[432,128]{1,0:T(8,128)S(1)} %bitcast.16, f32[6,64,256]{2,1,0:T(8,128)S(1)} %get-tuple-element.27.after.refs_1_.own), custom_call_target="tpu_custom_call" | custom-call | tf_op jit(solution)/shard_map/inner/pallas_call | solution.py:544
  3.7 0.5 collective-permute-start.2
  4.2 5.7 %collective-permute-start.1 = (f32[6,64,256]{2,1,0:T(8,128)S(1)}, f32[6,64,256]{2,1,0:T(8,128)S(1)}, u32[]{:S(2)}, u32[]{:S(2)}) collective-permute-start(f32[6,64,256]{2,1,0:T(8,128)S(1)} %get-tuple-element.27.after.refs_1_.own), channel_id=1, source_target_pairs={{0,15},{1,2},{2,1},{3,4},{4,3},{5,6},{6,5},{7,8},{8,7},{9,10},{10,... | collective-permute-start | bytes 1179656 | tf_op jit(solution)/shard_map/ppermute | solution.py:567
  9.9 0.0 collective-permute-start.3
  9.9 0.0 collective-permute-start
  9.9 3.8 %local.1 = (f32[6,64,512]{2,1,0:T(8,128)S(1)}, f32[6,64,512]{2,1,0:T(8,128)S(1)}) custom-call(f32[288,128]{1,0:T(8,128)S(1)} %get-tuple-element.29.plane_links, f32[72,128]{1,0:T(8,128)S(1)} %get-tuple-element.30.cross_links, f32[6,72,512]{2,1,0:T(8,128)S(1)} %get-tuple-element.31.inner.own, f32[6,64,256]{2,1,0:T(8,128)S(1)} %get-tuple-element.32.refs_0_.own, ...), custom_call_target="tpu_custom_call" | custom-call | flops 4000000000 | bytes 1572864 | tf_op jit(solution)/shard_map/local/pallas_call | solution.py:544
  13.7 0.0 collective-permute-done.2.partner.linked
  13.7 3.0 %inner_step.1 = (f32[6,64,512]{2,1,0:T(8,128)S(1)}, f32[6,64,512]{2,1,0:T(8,128)S(1)}) custom-call(s32[2]{0:T(128)S(1)} %pad_add_fusion.place_ref, f32[72,128]{1,0:T(8,128)S(1)} %get-tuple-element.28.top_links, f32[288,128]{1,0:T(8,128)S(1)} %get-tuple-element.29.plane_links, f32[6,72,512]{2,1,0:T(8,128)S(1)} %collective-permute-done.2.partner.linked, ...), custom_call_target="tpu_custom_call" | custom-call | tf_op jit(solution)/shard_map/inner_step/pallas_call | solution.py:544
  16.8 0.0 collective-permute-done.1.beyond
  16.8 3.0 %collective-permute-done.3.beyond = f32[6,64,256]{2,1,0:T(8,128)S(1)} collective-permute-done((f32[6,64,256]{2,1,0:T(8,128)S(1)}, f32[6,64,256]{2,1,0:T(8,128)S(1)}, u32[]{:S(2)}, u32[]{:S(2)}) %collective-permute-start.3) | collective-permute-done | bytes 393248 | tf_op jit(solution)/shard_map/ppermute | solution.py:567
  19.8 1.5 %collective-permute-start.4 = (f32[8,128]{1,0:T(8,128)S(1)}, f32[8,128]{1,0:T(8,128)S(1)}, u32[]{:S(2)}, u32[]{:S(2)}) collective-permute-start(f32[8,128]{1,0:T(8,128)S(1)} %fusion), channel_id=1, source_target_pairs={{1,0},{2,3},{5,4},{6,7},{9,8},{10,11},{13,12},{14,15},{17,16},{18,... | collective-permute-start | bytes 12296 | tf_op jit(solution)/shard_map/ppermute | solution.py:581
  21.3 0.0 collective-permute-done.low_links
  21.3 6.0 %collective-permute-done.4.token = f32[8,128]{1,0:T(8,128)S(1)} collective-permute-done((f32[8,128]{1,0:T(8,128)S(1)}, f32[8,128]{1,0:T(8,128)S(1)}, u32[]{:S(2)}, u32[]{:S(2)}) %collective-permute-start.4) | collective-permute-done | bytes 4128 | tf_op jit(solution)/shard_map/ppermute | solution.py:581
  27.3 0.8 %edge.3 = (f32[6,64,256]{2,1,0:T(8,128)S(1)}, f32[6,64,512]{2,1,0:T(8,128)S(1)}) custom-call(s32[2]{0:T(128)S(1)} %pad_add_fusion.place_ref, f32[72,128]{1,0:T(8,128)S(1)} %get-tuple-element.28.top_links, f32[72,128]{1,0:T(8,128)S(1)} %collective-permute-done.low_links, ...), custom_call_target="tpu_custom_call", output_to_operand_aliasing={{1}: (6, {})} | custom-call | tf_op jit(solution)/shard_map/edge/pallas_call | solution.py:590
  28.1 0.2 collective-permute-start.6
  28.4 4.4 %collective-permute-start.7 = (f32[6,64,256]{2,1,0:T(8,128)S(1)}, f32[6,64,256]{2,1,0:T(8,128)S(1)}, u32[]{:S(2)}, u32[]{:S(2)}) collective-permute-start(f32[6,64,256]{2,1,0:T(8,128)S(1)} %get-tuple-element.38.refs_0_), channel_id=1, source_target_pairs={{0,15},{1,2},{2,1},{3,4},{4,3},{5,6},{6,5},{7,8},{8,7},{9,10},{10,... | collective-permute-start | bytes 1179656 | tf_op jit(solution)/shard_map/ppermute | solution.py:567
  32.8 0.8 %edge.2.refs_1_ = f32[6,64,256]{2,1,0:T(8,128)S(1)} custom-call(s32[2]{0:T(128)S(1)} %pad_add_fusion.place_ref, f32[72,128]{1,0:T(8,128)S(1)} %get-tuple-element.28.top_links, f32[72,128]{1,0:T(8,128)S(1)} %collective-permute-done.low_links, f32[6,64,256]{2,1,0:T(8,128)S(1)} %collective-permute-done.1.beyond, f32[6,64,512]{2,1,0:T(8,128)S(1)} %get-tuple-element.33.sums, ...), custom_call_target="tpu_custom_call" | custom-call | tf_op jit(solution)/shard_map/edge/pallas_call | solution.py:544
  33.6 0.1 collective-permute-start.5
  33.7 0.0 collective-permute-done.6.partner
  33.7 8.2 %inner_pairs.1.refs_2_.before = f32[1280,128]{1,0:T(8,128)S(1)} custom-call(s32[2]{0:T(128)S(1)} %pad_add_fusion.place_ref, f32[72,128]{1,0:T(8,128)S(1)} %get-tuple-element.28.top_links, f32[72,128]{1,0:T(8,128)S(1)} %get-tuple-element.30.cross_links, f32[6,72,512]{2,1,0:T(8,128)S(1)} %collective-permute-done.2.partner.linked, ...), custom_call_target="tpu_custom_call" | custom-call | flops 8000000000 | bytes 1572864 | tf_op jit(solution)/shard_map/inner_pairs/pallas_call | solution.py:544
  41.9 2.2 %outer_hop.1.partial = f32[6,64,512]{2,1,0:T(8,128)S(1)} custom-call(f32[288,128]{1,0:T(8,128)S(1)} %get-tuple-element.29.plane_links, f32[72,128]{1,0:T(8,128)S(1)} %get-tuple-element.30.cross_links, f32[6,64,512]{2,1,0:T(8,128)S(1)} %get-tuple-element.37.inner, f32[6,64,256]{2,1,0:T(8,128)S(1)} %get-tuple-element.38.refs_0_, ...), custom_call_target="tpu_custom_call" | custom-call | flops 2000000000 | bytes 1572864 | tf_op jit(solution)/shard_map/outer_hop/pallas_call | solution.py:544
  44.1 0.0 copy-start.2
  44.1 0.0 collective-permute-done.7.far
  44.1 4.2 %outer_pairs.1.before = f32[1280,128]{1,0:T(8,128)S(1)} custom-call(s32[2]{0:T(128)S(1)} %pad_add_fusion.place_ref, f32[72,128]{1,0:T(8,128)S(1)} %get-tuple-element.28.top_links, f32[72,128]{1,0:T(8,128)S(1)} %collective-permute-done.low_links, f32[6,64,256]{2,1,0:T(8,128)S(1)} %collective-permute-done.7.far, f32[6,64,512]{2,1,0:T(8,128)S(1)} %outer_hop.1.partial, ...), custom_call_target="tpu_custom_call" | custom-call | flops 4000000000 | bytes 2359296 | tf_op jit(solution)/shard_map/outer_pairs/pallas_call | solution.py:619
  48.3 0.0 collective-permute-done.5.far
  48.4 0.0 copy-done.2
  48.4 6.4 %last_pairs.1 = (f32[8,4,32,128]{3,2,1,0:T(8,128)S(1)}, f32[8,4,32,128]{3,2,1,0:T(8,128)S(1)}) custom-call(s32[63]{0:T(128)S(1)} %copy-done.2, s32[2]{0:T(128)S(1)} %pad_add_fusion.place_ref, f32[72,128]{1,0:T(8,128)S(1)} %get-tuple-element.28.top_links, f32[72,128]{1,0:T(8,128)S(1)} %collective-permute-done.low_links, ...), custom_call_target="tpu_custom_call" | custom-call | flops 4000000000 | bytes 2359296 | tf_op jit(solution)/shard_map/last_pairs/pallas_call | solution.py:633
  54.8 0.3 collective-permute-start.8
  55.1 1.7 %collective-permute-done.8.received = f32[8,4,32,128]{3,2,1,0:T(8,128)S(1)} collective-permute-done((f32[8,4,32,128]{3,2,1,0:T(8,128)S(1)}, f32[8,4,32,128]{3,2,1,0:T(8,128)S(1)}, u32[]{:S(2)}, u32[]{:S(2)}) %collective-permute-start.8) | collective-permute-done | bytes 524320 | tf_op jit(solution)/shard_map/ppermute | solution.py:653
  56.8 0.1 combine.1
  56.8 1.5 %collective-permute-start.12 = (f32[2,4,32,128]{3,2,1,0:T(8,128)S(1)}, f32[2,4,32,128]{3,2,1,0:T(8,128)S(1)}, u32[]{:S(2)}, u32[]{:S(2)}) collective-permute-start(f32[2,4,32,128]{3,2,1,0:T(8,128)S(1)} %get-tuple-element.46), channel_id=1, source_target_pairs={{0,2},{1,3},{2,0},{3,1},{4,6},{5,7},{6,4},{7,5},{8,10},{9,11},{10,... | collective-permute-start | bytes 393224 | tf_op jit(solution)/shard_map/ppermute | solution.py:662
  58.4 1.6 %collective-permute-start.10 = (f32[4,32,128]{2,1,0:T(8,128)S(1)}, f32[4,32,128]{2,1,0:T(8,128)S(1)}, u32[]{:S(2)}, u32[]{:S(2)}) collective-permute-start(f32[4,32,128]{2,1,0:T(8,128)S(1)} %get-tuple-element.43), channel_id=1, source_target_pairs={{0,4},{1,5},{2,6},{3,7},{4,0},{5,1},{6,2},{7,3},{8,12},{9,13},{10,... | collective-permute-start | bytes 196616 | tf_op jit(solution)/shard_map/ppermute | solution.py:662
  59.9 0.4 collective-permute-start.11
  60.4 1.5 %collective-permute-start.9 = (f32[4,32,128]{2,1,0:T(8,128)S(1)}, f32[4,32,128]{2,1,0:T(8,128)S(1)}, u32[]{:S(2)}, u32[]{:S(2)}) collective-permute-start(f32[4,32,128]{2,1,0:T(8,128)S(1)} %get-tuple-element.42), channel_id=1, source_target_pairs={{0,2},{1,3},{2,0},{3,1},{4,6},{5,7},{6,4},{7,5},{8,10},{9,11},{10,... | collective-permute-start | bytes 196616 | tf_op jit(solution)/shard_map/ppermute | solution.py:662
  61.8 0.7 collective-permute-done.12.received
  62.5 3.3 %collective-permute-start.13 = (f32[4,32,128]{2,1,0:T(8,128)S(1)}, f32[4,32,128]{2,1,0:T(8,128)S(1)}, u32[]{:S(2)}, u32[]{:S(2)}) collective-permute-start(f32[4,32,128]{2,1,0:T(8,128)S(1)} %get-tuple-element.47), channel_id=1, source_target_pairs={{0,8},{1,9},{2,10},{3,11},{4,12},{5,13},{6,14},{7,15},{8,0},{9,1},... | collective-permute-start | bytes 196616 | tf_op jit(solution)/shard_map/ppermute | solution.py:662
  65.8 3.2 %collective-permute-start.14 = (f32[4,32,128]{2,1,0:T(8,128)S(1)}, f32[4,32,128]{2,1,0:T(8,128)S(1)}, u32[]{:S(2)}, u32[]{:S(2)}) collective-permute-start(f32[4,32,128]{2,1,0:T(8,128)S(1)} %get-tuple-element.48), channel_id=1, source_target_pairs={{0,12},{1,13},{2,14},{3,15},{4,8},{5,9},{6,10},{7,11},{8,4},{9,5},... | collective-permute-start | bytes 196616 | tf_op jit(solution)/shard_map/ppermute | solution.py:662
  69.0 0.0 collective-permute-done.10.refs_2_
  69.0 0.0 collective-permute-done.11.refs_3_
  69.1 0.0 collective-permute-done.9.refs_1_
  69.1 0.0 collective-permute-done.13.refs_4_
  69.1 2.9 %collective-permute-done.14.refs_5_ = f32[4,32,128]{2,1,0:T(8,128)S(1)} collective-permute-done((f32[4,32,128]{2,1,0:T(8,128)S(1)}, f32[4,32,128]{2,1,0:T(8,128)S(1)}, u32[]{:S(2)}, u32[]{:S(2)}) %collective-permute-start.14) | collective-permute-done | bytes 65568 | tf_op jit(solution)/shard_map/ppermute | solution.py:662
  72.0 0.7 total.1
  (2 shorter events, 0.0 us)
Async XLA Ops:
  0.1 1.4 %copy-start = (f32[64,2,3,2,512]{4,3,2,1,0:T(2,128)S(1)}, f32[64,2,3,2,512]{4,3,2,1,0:T(2,128)}, u32[]{:S(2)}) copy-start(f32[64,2,3,2,512]{4,3,2,1,0:T(2,128)} %param.3) | copy-start | bytes 4718596
  1.5 1.0 %copy-start.1 = (f32[3,2,3,3,2,512]{5,4,3,2,1,0:T(2,128)S(1)}, f32[3,2,3,3,2,512]{5,4,3,2,1,0:T(2,128)}, u32[]{:S(2)}) copy-start(f32[3,2,3,3,2,512]{5,4,3,2,1,0:T(2,128)} %param.4) | copy-start | bytes 663556
  3.7 10.1 %collective-permute-start.2 = (f32[6,72,512]{2,1,0:T(8,128)S(1)}, f32[6,72,512]{2,1,0:T(8,128)S(1)}, u32[]{:S(2)}, u32[]{:S(2)}) collective-permute-start(f32[6,72,512]{2,1,0:T(8,128)S(1)} %get-tuple-element.31.inner.own), channel_id=1, source_target_pairs={{0,1},{1,0},{2,3},{3,2},{4,5},{5,4},{6,7},{7,6},{8,9},{9,8},{10,11... | collective-permute-start | bytes 2654216 | tf_op jit(solution)/shard_map/ppermute | solution.py:570
  4.2 12.6 %collective-permute-start.1 = (f32[6,64,256]{2,1,0:T(8,128)S(1)}, f32[6,64,256]{2,1,0:T(8,128)S(1)}, u32[]{:S(2)}, u32[]{:S(2)}) collective-permute-start(f32[6,64,256]{2,1,0:T(8,128)S(1)} %get-tuple-element.27.after.refs_1_.own), channel_id=1, source_target_pairs={{0,15},{1,2},{2,1},{3,4},{4,3},{5,6},{6,5},{7,8},{8,7},{9,10},{10,... | collective-permute-start | bytes 1179656 | tf_op jit(solution)/shard_map/ppermute | solution.py:567
  9.9 10.0 %collective-permute-start.3 = (f32[6,64,256]{2,1,0:T(8,128)S(1)}, f32[6,64,256]{2,1,0:T(8,128)S(1)}, u32[]{:S(2)}, u32[]{:S(2)}) collective-permute-start(f32[6,64,256]{2,1,0:T(8,128)S(1)} %get-tuple-element.32.refs_0_.own), channel_id=1, source_target_pairs={{0,15},{1,2},{2,1},{3,4},{4,3},{5,6},{6,5},{7,8},{8,7},{9,10},{10,... | collective-permute-start | bytes 1179656 | tf_op jit(solution)/shard_map/ppermute | solution.py:567
  9.9 11.4 %collective-permute-start = (f32[72,128]{1,0:T(8,128)S(1)}, f32[72,128]{1,0:T(8,128)S(1)}, u32[]{:S(2)}, u32[]{:S(2)}) collective-permute-start(f32[72,128]{1,0:T(8,128)S(1)} %get-tuple-element.28.top_links), channel_id=1, source_target_pairs={{0,1},{1,2},{2,3},{3,4},{4,5},{5,6},{6,7},{7,8},{8,9},{9,10},{10,1... | collective-permute-start | bytes 110600 | tf_op jit(solution)/shard_map/ppermute | solution.py:571
  19.8 7.5 %collective-permute-start.4 = (f32[8,128]{1,0:T(8,128)S(1)}, f32[8,128]{1,0:T(8,128)S(1)}, u32[]{:S(2)}, u32[]{:S(2)}) collective-permute-start(f32[8,128]{1,0:T(8,128)S(1)} %fusion), channel_id=1, source_target_pairs={{1,0},{2,3},{5,4},{6,7},{9,8},{10,11},{13,12},{14,15},{17,16},{18,... | collective-permute-start | bytes 12296 | tf_op jit(solution)/shard_map/ppermute | solution.py:581
  28.1 5.5 %collective-permute-start.6 = (f32[6,64,512]{2,1,0:T(8,128)S(1)}, f32[6,64,512]{2,1,0:T(8,128)S(1)}, u32[]{:S(2)}, u32[]{:S(2)}) collective-permute-start(f32[6,64,512]{2,1,0:T(8,128)S(1)} %get-tuple-element.37.inner), channel_id=1, source_target_pairs={{0,1},{1,0},{2,3},{3,2},{4,5},{5,4},{6,7},{7,6},{8,9},{9,8},{10,11... | collective-permute-start | bytes 2359304 | tf_op jit(solution)/shard_map/ppermute | solution.py:600
  28.4 15.7 %collective-permute-start.7 = (f32[6,64,256]{2,1,0:T(8,128)S(1)}, f32[6,64,256]{2,1,0:T(8,128)S(1)}, u32[]{:S(2)}, u32[]{:S(2)}) collective-permute-start(f32[6,64,256]{2,1,0:T(8,128)S(1)} %get-tuple-element.38.refs_0_), channel_id=1, source_target_pairs={{0,15},{1,2},{2,1},{3,4},{4,3},{5,6},{6,5},{7,8},{8,7},{9,10},{10,... | collective-permute-start | bytes 1179656 | tf_op jit(solution)/shard_map/ppermute | solution.py:567
  33.6 14.8 %collective-permute-start.5 = (f32[6,64,256]{2,1,0:T(8,128)S(1)}, f32[6,64,256]{2,1,0:T(8,128)S(1)}, u32[]{:S(2)}, u32[]{:S(2)}) collective-permute-start(f32[6,64,256]{2,1,0:T(8,128)S(1)} %edge.2.refs_1_), channel_id=1, source_target_pairs={{0,15},{1,2},{2,1},{3,4},{4,3},{5,6},{6,5},{7,8},{8,7},{9,10},{10,... | collective-permute-start | bytes 1179656 | tf_op jit(solution)/shard_map/ppermute | solution.py:567
  44.1 4.3 %copy-start.2 = (s32[63]{0:T(128)S(1)}, s32[63]{0:T(128)}, u32[]{:S(2)}) copy-start(s32[63]{0:T(128)} %slot_ref.1) | copy-start | bytes 760
  54.8 2.0 %collective-permute-start.8 = (f32[8,4,32,128]{3,2,1,0:T(8,128)S(1)}, f32[8,4,32,128]{3,2,1,0:T(8,128)S(1)}, u32[]{:S(2)}, u32[]{:S(2)}) collective-permute-start(f32[8,4,32,128]{3,2,1,0:T(8,128)S(1)} %get-tuple-element.40), channel_id=1, source_target_pairs={{0,1},{1,0},{2,3},{3,2},{4,5},{5,4},{6,7},{7,6},{8,9},{9,8},{10,11... | collective-permute-start | bytes 1572872 | tf_op jit(solution)/shard_map/ppermute | solution.py:653
  56.8 5.7 %collective-permute-start.12 = (f32[2,4,32,128]{3,2,1,0:T(8,128)S(1)}, f32[2,4,32,128]{3,2,1,0:T(8,128)S(1)}, u32[]{:S(2)}, u32[]{:S(2)}) collective-permute-start(f32[2,4,32,128]{3,2,1,0:T(8,128)S(1)} %get-tuple-element.46), channel_id=1, source_target_pairs={{0,2},{1,3},{2,0},{3,1},{4,6},{5,7},{6,4},{7,5},{8,10},{9,11},{10,... | collective-permute-start | bytes 393224 | tf_op jit(solution)/shard_map/ppermute | solution.py:662
  58.4 10.7 %collective-permute-start.10 = (f32[4,32,128]{2,1,0:T(8,128)S(1)}, f32[4,32,128]{2,1,0:T(8,128)S(1)}, u32[]{:S(2)}, u32[]{:S(2)}) collective-permute-start(f32[4,32,128]{2,1,0:T(8,128)S(1)} %get-tuple-element.43), channel_id=1, source_target_pairs={{0,4},{1,5},{2,6},{3,7},{4,0},{5,1},{6,2},{7,3},{8,12},{9,13},{10,... | collective-permute-start | bytes 196616 | tf_op jit(solution)/shard_map/ppermute | solution.py:662
  59.9 9.1 %collective-permute-start.11 = (f32[4,32,128]{2,1,0:T(8,128)S(1)}, f32[4,32,128]{2,1,0:T(8,128)S(1)}, u32[]{:S(2)}, u32[]{:S(2)}) collective-permute-start(f32[4,32,128]{2,1,0:T(8,128)S(1)} %get-tuple-element.44), channel_id=1, source_target_pairs={{0,6},{1,7},{2,4},{3,5},{4,2},{5,3},{6,0},{7,1},{8,14},{9,15},{10,... | collective-permute-start | bytes 196616 | tf_op jit(solution)/shard_map/ppermute | solution.py:662
  60.4 8.7 %collective-permute-start.9 = (f32[4,32,128]{2,1,0:T(8,128)S(1)}, f32[4,32,128]{2,1,0:T(8,128)S(1)}, u32[]{:S(2)}, u32[]{:S(2)}) collective-permute-start(f32[4,32,128]{2,1,0:T(8,128)S(1)} %get-tuple-element.42), channel_id=1, source_target_pairs={{0,2},{1,3},{2,0},{3,1},{4,6},{5,7},{6,4},{7,5},{8,10},{9,11},{10,... | collective-permute-start | bytes 196616 | tf_op jit(solution)/shard_map/ppermute | solution.py:662
  62.5 6.5 %collective-permute-start.13 = (f32[4,32,128]{2,1,0:T(8,128)S(1)}, f32[4,32,128]{2,1,0:T(8,128)S(1)}, u32[]{:S(2)}, u32[]{:S(2)}) collective-permute-start(f32[4,32,128]{2,1,0:T(8,128)S(1)} %get-tuple-element.47), channel_id=1, source_target_pairs={{0,8},{1,9},{2,10},{3,11},{4,12},{5,13},{6,14},{7,15},{8,0},{9,1},... | collective-permute-start | bytes 196616 | tf_op jit(solution)/shard_map/ppermute | solution.py:662
  65.8 6.1 %collective-permute-start.14 = (f32[4,32,128]{2,1,0:T(8,128)S(1)}, f32[4,32,128]{2,1,0:T(8,128)S(1)}, u32[]{:S(2)}, u32[]{:S(2)}) collective-permute-start(f32[4,32,128]{2,1,0:T(8,128)S(1)} %get-tuple-element.48), channel_id=1, source_target_pairs={{0,12},{1,13},{2,14},{3,15},{4,8},{5,9},{6,10},{7,11},{8,4},{9,5},... | collective-permute-start | bytes 196616 | tf_op jit(solution)/shard_map/ppermute | solution.py:662

commit v5 on v4

--- a/solution.py
+++ b/solution.py
@@ -271,7 +271,7 @@
             for part in range(6):
                 out[part, rows, lanes] = finish(total[part], (part, rows, lanes))
 
-        groups_loop(out.shape[1], step, 2)
+        groups_loop(out.shape[1], step, 4)
 
 
 def inner_step_kernel(tiles, place_ref, top_links, plane_links, partner, sums, first, out):
@@ -397,7 +397,7 @@
             for part in range(6):
                 field[part, rows, lanes] = total[part] * (2.0 / 6.0) - own[part, rows, lanes]
 
-        groups_loop(vectors, step, 2)
+        groups_loop(vectors, step, 4)
     sums[...] = jnp.zeros_like(sums)
     width = low.shape[1] // 6
     for start in range(0, field.shape[2], width):

time: 72.8 us -> 73.4 us (level)
  transfers between devices with their start and end apart: 15 -> 15, of which waited for: 5 -> 6; matrix products, arithmetic and copies ran while one was open for 0% -> 0% of each run, Pallas kernels for 31% -> 30%
where the time goes in v5:
time: 73.4 us; the launch traced here: 73.2 us
  Pallas kernels  32.1 us (44%)
  starting transfers between devices  24.5 us (33%)
  waiting for transfers between devices  15 us (20%)
  local copies, waits for them, and re-layouts  1.42 us (2%)
    pallas_call x10, Pallas kernels, call(): pl.pallas_call(kernel, out_shape=shapes, in_specs=[SMEM] * smem + [VMEM]...  20.7 us
    ppermute x6, starting transfers between devices, to_chip(): lax.ppermute(array, 'brick', [(i, i ^ 2 * away) for i in range(count)])  11.6 us
    ppermute x4, starting transfers between devices, off(): return [lax.ppermute(field, 'brick', off_chip) for field in fields]  10.2 us
    pallas_call x1, Pallas kernels, on_device(): pl.pallas_call(functools.partial(last_pairs_kernel, tiles, chunk_tiles[-1...  6.4 us
    ppermute x1, waiting for transfers between devices, on_device(): lax.ppermute(token, 'brick', [(i, i ^ 1) for i in range(count) if i % 4 i...  6.03 us
    ppermute x6, waiting for transfers between devices, to_chip(): lax.ppermute(array, 'brick', [(i, i ^ 2 * away) for i in range(count)])  4.26 us
    pallas_call x1, Pallas kernels, on_device(): pl.pallas_call(functools.partial(outer_pairs_kernel, tiles, chunk), out_s...  4.21 us
    ppermute x4, waiting for transfers between devices, off(): return [lax.ppermute(field, 'brick', off_chip) for field in fields]  3.11 us
  transfers between devices with their start and end apart: 15, of which 6 were waited for; matrix products, arithmetic and copies ran while one was open for 0% of the time, Pallas kernels for 30%

profile of v5, /device:TPU:0, one launch (start us, length us, event | category | flops | bytes accessed | tf_op | source)
XLA Modules:
  0.0 73.2 jit_solution(1620008157594650649)
XLA Ops:
  0.0 0.1 pad_add_fusion.place_ref
  0.1 0.0 copy-start
  0.1 1.4 %copy-done = f32[64,2,3,2,512]{4,3,2,1,0:T(2,128)S(1)} copy-done((f32[64,2,3,2,512]{4,3,2,1,0:T(2,128)S(1)}, f32[64,2,3,2,512]{4,3,2,1,0:T(2,128)}, u32[]{:S(2)}) %copy-start) | copy-done | bytes 1572888
  1.5 0.0 copy-start.1
  1.5 1.0 %outer.1 = (f32[6,64,256]{2,1,0:T(8,128)S(1)}, f32[6,64,256]{2,1,0:T(8,128)S(1)}) custom-call(s32[2]{0:T(128)S(1)} %pad_add_fusion.place_ref, f32[3072,128]{1,0:T(8,128)S(1)} %bitcast.14), custom_call_target="tpu_custom_call" | custom-call | tf_op jit(solution)/shard_map/outer/pallas_call | solution.py:544
  2.5 0.0 copy-done.1
  2.5 1.2 %inner.1 = (f32[6,72,512]{2,1,0:T(8,128)S(1)}, f32[288,128]{1,0:T(8,128)S(1)}, f32[72,128]{1,0:T(8,128)S(1)}, f32[72,128]{1,0:T(8,128)S(1)}) custom-call(s32[2]{0:T(128)S(1)} %pad_add_fusion.place_ref, f32[3072,128]{1,0:T(8,128)S(1)} %bitcast.15, f32[432,128]{1,0:T(8,128)S(1)} %bitcast.16, f32[6,64,256]{2,1,0:T(8,128)S(1)} %get-tuple-element.27.after.refs_1_.own), custom_call_target="tpu_custom_call" | custom-call | tf_op jit(solution)/shard_map/inner/pallas_call | solution.py:544
  3.7 0.5 collective-permute-start.2
  4.2 5.7 %collective-permute-start.1 = (f32[6,64,256]{2,1,0:T(8,128)S(1)}, f32[6,64,256]{2,1,0:T(8,128)S(1)}, u32[]{:S(2)}, u32[]{:S(2)}) collective-permute-start(f32[6,64,256]{2,1,0:T(8,128)S(1)} %get-tuple-element.27.after.refs_1_.own), channel_id=1, source_target_pairs={{0,15},{1,2},{2,1},{3,4},{4,3},{5,6},{6,5},{7,8},{8,7},{9,10},{10,... | collective-permute-start | bytes 1179656 | tf_op jit(solution)/shard_map/ppermute | solution.py:567
  9.9 0.0 collective-permute-start.3
  9.9 0.0 collective-permute-start
  9.9 3.8 %local.1 = (f32[6,64,512]{2,1,0:T(8,128)S(1)}, f32[6,64,512]{2,1,0:T(8,128)S(1)}) custom-call(f32[288,128]{1,0:T(8,128)S(1)} %get-tuple-element.29.plane_links, f32[72,128]{1,0:T(8,128)S(1)} %get-tuple-element.30.cross_links, f32[6,72,512]{2,1,0:T(8,128)S(1)} %get-tuple-element.31.inner.own, f32[6,64,256]{2,1,0:T(8,128)S(1)} %get-tuple-element.32.refs_0_.own, ...), custom_call_target="tpu_custom_call" | custom-call | flops 4000000000 | bytes 1572864 | tf_op jit(solution)/shard_map/local/pallas_call | solution.py:544
  13.7 0.0 collective-permute-done.2.partner.linked
  13.7 3.0 %inner_step.1 = (f32[6,64,512]{2,1,0:T(8,128)S(1)}, f32[6,64,512]{2,1,0:T(8,128)S(1)}) custom-call(s32[2]{0:T(128)S(1)} %pad_add_fusion.place_ref, f32[72,128]{1,0:T(8,128)S(1)} %get-tuple-element.28.top_links, f32[288,128]{1,0:T(8,128)S(1)} %get-tuple-element.29.plane_links, f32[6,72,512]{2,1,0:T(8,128)S(1)} %collective-permute-done.2.partner.linked, ...), custom_call_target="tpu_custom_call" | custom-call | tf_op jit(solution)/shard_map/inner_step/pallas_call | solution.py:544
  16.7 0.0 collective-permute-done.1.beyond
  16.7 3.1 %collective-permute-done.3.beyond = f32[6,64,256]{2,1,0:T(8,128)S(1)} collective-permute-done((f32[6,64,256]{2,1,0:T(8,128)S(1)}, f32[6,64,256]{2,1,0:T(8,128)S(1)}, u32[]{:S(2)}, u32[]{:S(2)}) %collective-permute-start.3) | collective-permute-done | bytes 393248 | tf_op jit(solution)/shard_map/ppermute | solution.py:567
  19.8 1.5 %collective-permute-start.4 = (f32[8,128]{1,0:T(8,128)S(1)}, f32[8,128]{1,0:T(8,128)S(1)}, u32[]{:S(2)}, u32[]{:S(2)}) collective-permute-start(f32[8,128]{1,0:T(8,128)S(1)} %fusion), channel_id=1, source_target_pairs={{1,0},{2,3},{5,4},{6,7},{9,8},{10,11},{13,12},{14,15},{17,16},{18,... | collective-permute-start | bytes 12296 | tf_op jit(solution)/shard_map/ppermute | solution.py:581
  21.3 0.0 collective-permute-done.low_links
  21.3 6.0 %collective-permute-done.4.token = f32[8,128]{1,0:T(8,128)S(1)} collective-permute-done((f32[8,128]{1,0:T(8,128)S(1)}, f32[8,128]{1,0:T(8,128)S(1)}, u32[]{:S(2)}, u32[]{:S(2)}) %collective-permute-start.4) | collective-permute-done | bytes 4128 | tf_op jit(solution)/shard_map/ppermute | solution.py:581
  27.3 0.8 %edge.3 = (f32[6,64,256]{2,1,0:T(8,128)S(1)}, f32[6,64,512]{2,1,0:T(8,128)S(1)}) custom-call(s32[2]{0:T(128)S(1)} %pad_add_fusion.place_ref, f32[72,128]{1,0:T(8,128)S(1)} %get-tuple-element.28.top_links, f32[72,128]{1,0:T(8,128)S(1)} %collective-permute-done.low_links, ...), custom_call_target="tpu_custom_call", output_to_operand_aliasing={{1}: (6, {})} | custom-call | tf_op jit(solution)/shard_map/edge/pallas_call | solution.py:590
  28.1 0.2 collective-permute-start.6
  28.3 4.4 %collective-permute-start.7 = (f32[6,64,256]{2,1,0:T(8,128)S(1)}, f32[6,64,256]{2,1,0:T(8,128)S(1)}, u32[]{:S(2)}, u32[]{:S(2)}) collective-permute-start(f32[6,64,256]{2,1,0:T(8,128)S(1)} %get-tuple-element.38.refs_0_), channel_id=1, source_target_pairs={{0,15},{1,2},{2,1},{3,4},{4,3},{5,6},{6,5},{7,8},{8,7},{9,10},{10,... | collective-permute-start | bytes 1179656 | tf_op jit(solution)/shard_map/ppermute | solution.py:567
  32.7 0.8 %edge.2.refs_1_ = f32[6,64,256]{2,1,0:T(8,128)S(1)} custom-call(s32[2]{0:T(128)S(1)} %pad_add_fusion.place_ref, f32[72,128]{1,0:T(8,128)S(1)} %get-tuple-element.28.top_links, f32[72,128]{1,0:T(8,128)S(1)} %collective-permute-done.low_links, f32[6,64,256]{2,1,0:T(8,128)S(1)} %collective-permute-done.1.beyond, f32[6,64,512]{2,1,0:T(8,128)S(1)} %get-tuple-element.33.sums, ...), custom_call_target="tpu_custom_call" | custom-call | tf_op jit(solution)/shard_map/edge/pallas_call | solution.py:544
  33.5 0.1 collective-permute-start.5
  33.6 0.0 collective-permute-done.6.partner
  33.6 8.1 %inner_pairs.1.refs_2_.before = f32[1280,128]{1,0:T(8,128)S(1)} custom-call(s32[2]{0:T(128)S(1)} %pad_add_fusion.place_ref, f32[72,128]{1,0:T(8,128)S(1)} %get-tuple-element.28.top_links, f32[72,128]{1,0:T(8,128)S(1)} %get-tuple-element.30.cross_links, f32[6,72,512]{2,1,0:T(8,128)S(1)} %collective-permute-done.2.partner.linked, ...), custom_call_target="tpu_custom_call" | custom-call | flops 8000000000 | bytes 1572864 | tf_op jit(solution)/shard_map/inner_pairs/pallas_call | solution.py:544
  41.8 2.2 %outer_hop.1.partial = f32[6,64,512]{2,1,0:T(8,128)S(1)} custom-call(f32[288,128]{1,0:T(8,128)S(1)} %get-tuple-element.29.plane_links, f32[72,128]{1,0:T(8,128)S(1)} %get-tuple-element.30.cross_links, f32[6,64,512]{2,1,0:T(8,128)S(1)} %get-tuple-element.37.inner, f32[6,64,256]{2,1,0:T(8,128)S(1)} %get-tuple-element.38.refs_0_, ...), custom_call_target="tpu_custom_call" | custom-call | flops 2000000000 | bytes 1572864 | tf_op jit(solution)/shard_map/outer_hop/pallas_call | solution.py:544
  43.9 0.0 copy-start.2
  43.9 0.0 collective-permute-done.7.far
  44.0 4.2 %outer_pairs.1.before = f32[1280,128]{1,0:T(8,128)S(1)} custom-call(s32[2]{0:T(128)S(1)} %pad_add_fusion.place_ref, f32[72,128]{1,0:T(8,128)S(1)} %get-tuple-element.28.top_links, f32[72,128]{1,0:T(8,128)S(1)} %collective-permute-done.low_links, f32[6,64,256]{2,1,0:T(8,128)S(1)} %collective-permute-done.7.far, f32[6,64,512]{2,1,0:T(8,128)S(1)} %outer_hop.1.partial, ...), custom_call_target="tpu_custom_call" | custom-call | flops 4000000000 | bytes 2359296 | tf_op jit(solution)/shard_map/outer_pairs/pallas_call | solution.py:619
  48.2 0.0 collective-permute-done.5.far
  48.2 0.0 copy-done.2
  48.2 6.4 %last_pairs.1 = (f32[8,4,32,128]{3,2,1,0:T(8,128)S(1)}, f32[8,4,32,128]{3,2,1,0:T(8,128)S(1)}) custom-call(s32[63]{0:T(128)S(1)} %copy-done.2, s32[2]{0:T(128)S(1)} %pad_add_fusion.place_ref, f32[72,128]{1,0:T(8,128)S(1)} %get-tuple-element.28.top_links, f32[72,128]{1,0:T(8,128)S(1)} %collective-permute-done.low_links, ...), custom_call_target="tpu_custom_call" | custom-call | flops 4000000000 | bytes 2359296 | tf_op jit(solution)/shard_map/last_pairs/pallas_call | solution.py:633
  54.6 0.4 collective-permute-start.8
  55.0 1.6 %collective-permute-done.8.received = f32[8,4,32,128]{3,2,1,0:T(8,128)S(1)} collective-permute-done((f32[8,4,32,128]{3,2,1,0:T(8,128)S(1)}, f32[8,4,32,128]{3,2,1,0:T(8,128)S(1)}, u32[]{:S(2)}, u32[]{:S(2)}) %collective-permute-start.8) | collective-permute-done | bytes 524320 | tf_op jit(solution)/shard_map/ppermute | solution.py:653
  56.6 0.1 combine.1
  56.6 1.6 %collective-permute-start.12 = (f32[2,4,32,128]{3,2,1,0:T(8,128)S(1)}, f32[2,4,32,128]{3,2,1,0:T(8,128)S(1)}, u32[]{:S(2)}, u32[]{:S(2)}) collective-permute-start(f32[2,4,32,128]{3,2,1,0:T(8,128)S(1)} %get-tuple-element.46), channel_id=1, source_target_pairs={{0,2},{1,3},{2,0},{3,1},{4,6},{5,7},{6,4},{7,5},{8,10},{9,11},{10,... | collective-permute-start | bytes 393224 | tf_op jit(solution)/shard_map/ppermute | solution.py:662
  58.3 1.6 %collective-permute-start.10 = (f32[4,32,128]{2,1,0:T(8,128)S(1)}, f32[4,32,128]{2,1,0:T(8,128)S(1)}, u32[]{:S(2)}, u32[]{:S(2)}) collective-permute-start(f32[4,32,128]{2,1,0:T(8,128)S(1)} %get-tuple-element.43), channel_id=1, source_target_pairs={{0,4},{1,5},{2,6},{3,7},{4,0},{5,1},{6,2},{7,3},{8,12},{9,13},{10,... | collective-permute-start | bytes 196616 | tf_op jit(solution)/shard_map/ppermute | solution.py:662
  59.9 0.4 collective-permute-start.11
  60.3 1.5 %collective-permute-start.9 = (f32[4,32,128]{2,1,0:T(8,128)S(1)}, f32[4,32,128]{2,1,0:T(8,128)S(1)}, u32[]{:S(2)}, u32[]{:S(2)}) collective-permute-start(f32[4,32,128]{2,1,0:T(8,128)S(1)} %get-tuple-element.42), channel_id=1, source_target_pairs={{0,2},{1,3},{2,0},{3,1},{4,6},{5,7},{6,4},{7,5},{8,10},{9,11},{10,... | collective-permute-start | bytes 196616 | tf_op jit(solution)/shard_map/ppermute | solution.py:662
  61.8 0.7 collective-permute-done.12.received
  62.5 4.0 %collective-permute-start.13 = (f32[4,32,128]{2,1,0:T(8,128)S(1)}, f32[4,32,128]{2,1,0:T(8,128)S(1)}, u32[]{:S(2)}, u32[]{:S(2)}) collective-permute-start(f32[4,32,128]{2,1,0:T(8,128)S(1)} %get-tuple-element.47), channel_id=1, source_target_pairs={{0,8},{1,9},{2,10},{3,11},{4,12},{5,13},{6,14},{7,15},{8,0},{9,1},... | collective-permute-start | bytes 196616 | tf_op jit(solution)/shard_map/ppermute | solution.py:662
  66.5 2.5 %collective-permute-start.14 = (f32[4,32,128]{2,1,0:T(8,128)S(1)}, f32[4,32,128]{2,1,0:T(8,128)S(1)}, u32[]{:S(2)}, u32[]{:S(2)}) collective-permute-start(f32[4,32,128]{2,1,0:T(8,128)S(1)} %get-tuple-element.48), channel_id=1, source_target_pairs={{0,12},{1,13},{2,14},{3,15},{4,8},{5,9},{6,10},{7,11},{8,4},{9,5},... | collective-permute-start | bytes 196616 | tf_op jit(solution)/shard_map/ppermute | solution.py:662
  69.0 0.0 collective-permute-done.10.refs_2_
  69.0 0.0 collective-permute-done.11.refs_3_
  69.0 0.0 collective-permute-done.9.refs_1_
  69.0 0.1 collective-permute-done.13.refs_4_
  69.1 3.5 %collective-permute-done.14.refs_5_ = f32[4,32,128]{2,1,0:T(8,128)S(1)} collective-permute-done((f32[4,32,128]{2,1,0:T(8,128)S(1)}, f32[4,32,128]{2,1,0:T(8,128)S(1)}, u32[]{:S(2)}, u32[]{:S(2)}) %collective-permute-start.14) | collective-permute-done | bytes 65568 | tf_op jit(solution)/shard_map/ppermute | solution.py:662
  72.5 0.7 total.1
  (2 shorter events, 0.0 us)
Async XLA Ops:
  0.1 1.4 %copy-start = (f32[64,2,3,2,512]{4,3,2,1,0:T(2,128)S(1)}, f32[64,2,3,2,512]{4,3,2,1,0:T(2,128)}, u32[]{:S(2)}) copy-start(f32[64,2,3,2,512]{4,3,2,1,0:T(2,128)} %param.3) | copy-start | bytes 4718596
  1.5 1.0 %copy-start.1 = (f32[3,2,3,3,2,512]{5,4,3,2,1,0:T(2,128)S(1)}, f32[3,2,3,3,2,512]{5,4,3,2,1,0:T(2,128)}, u32[]{:S(2)}) copy-start(f32[3,2,3,3,2,512]{5,4,3,2,1,0:T(2,128)} %param.4) | copy-start | bytes 663556
  3.7 10.1 %collective-permute-start.2 = (f32[6,72,512]{2,1,0:T(8,128)S(1)}, f32[6,72,512]{2,1,0:T(8,128)S(1)}, u32[]{:S(2)}, u32[]{:S(2)}) collective-permute-start(f32[6,72,512]{2,1,0:T(8,128)S(1)} %get-tuple-element.31.inner.own), channel_id=1, source_target_pairs={{0,1},{1,0},{2,3},{3,2},{4,5},{5,4},{6,7},{7,6},{8,9},{9,8},{10,11... | collective-permute-start | bytes 2654216 | tf_op jit(solution)/shard_map/ppermute | solution.py:570
  4.2 12.5 %collective-permute-start.1 = (f32[6,64,256]{2,1,0:T(8,128)S(1)}, f32[6,64,256]{2,1,0:T(8,128)S(1)}, u32[]{:S(2)}, u32[]{:S(2)}) collective-permute-start(f32[6,64,256]{2,1,0:T(8,128)S(1)} %get-tuple-element.27.after.refs_1_.own), channel_id=1, source_target_pairs={{0,15},{1,2},{2,1},{3,4},{4,3},{5,6},{6,5},{7,8},{8,7},{9,10},{10,... | collective-permute-start | bytes 1179656 | tf_op jit(solution)/shard_map/ppermute | solution.py:567
  9.9 10.0 %collective-permute-start.3 = (f32[6,64,256]{2,1,0:T(8,128)S(1)}, f32[6,64,256]{2,1,0:T(8,128)S(1)}, u32[]{:S(2)}, u32[]{:S(2)}) collective-permute-start(f32[6,64,256]{2,1,0:T(8,128)S(1)} %get-tuple-element.32.refs_0_.own), channel_id=1, source_target_pairs={{0,15},{1,2},{2,1},{3,4},{4,3},{5,6},{6,5},{7,8},{8,7},{9,10},{10,... | collective-permute-start | bytes 1179656 | tf_op jit(solution)/shard_map/ppermute | solution.py:567
  9.9 11.4 %collective-permute-start = (f32[72,128]{1,0:T(8,128)S(1)}, f32[72,128]{1,0:T(8,128)S(1)}, u32[]{:S(2)}, u32[]{:S(2)}) collective-permute-start(f32[72,128]{1,0:T(8,128)S(1)} %get-tuple-element.28.top_links), channel_id=1, source_target_pairs={{0,1},{1,2},{2,3},{3,4},{4,5},{5,6},{6,7},{7,8},{8,9},{9,10},{10,1... | collective-permute-start | bytes 110600 | tf_op jit(solution)/shard_map/ppermute | solution.py:571
  19.8 7.5 %collective-permute-start.4 = (f32[8,128]{1,0:T(8,128)S(1)}, f32[8,128]{1,0:T(8,128)S(1)}, u32[]{:S(2)}, u32[]{:S(2)}) collective-permute-start(f32[8,128]{1,0:T(8,128)S(1)} %fusion), channel_id=1, source_target_pairs={{1,0},{2,3},{5,4},{6,7},{9,8},{10,11},{13,12},{14,15},{17,16},{18,... | collective-permute-start | bytes 12296 | tf_op jit(solution)/shard_map/ppermute | solution.py:581
  28.1 5.5 %collective-permute-start.6 = (f32[6,64,512]{2,1,0:T(8,128)S(1)}, f32[6,64,512]{2,1,0:T(8,128)S(1)}, u32[]{:S(2)}, u32[]{:S(2)}) collective-permute-start(f32[6,64,512]{2,1,0:T(8,128)S(1)} %get-tuple-element.37.inner), channel_id=1, source_target_pairs={{0,1},{1,0},{2,3},{3,2},{4,5},{5,4},{6,7},{7,6},{8,9},{9,8},{10,11... | collective-permute-start | bytes 2359304 | tf_op jit(solution)/shard_map/ppermute | solution.py:600
  28.3 15.6 %collective-permute-start.7 = (f32[6,64,256]{2,1,0:T(8,128)S(1)}, f32[6,64,256]{2,1,0:T(8,128)S(1)}, u32[]{:S(2)}, u32[]{:S(2)}) collective-permute-start(f32[6,64,256]{2,1,0:T(8,128)S(1)} %get-tuple-element.38.refs_0_), channel_id=1, source_target_pairs={{0,15},{1,2},{2,1},{3,4},{4,3},{5,6},{6,5},{7,8},{8,7},{9,10},{10,... | collective-permute-start | bytes 1179656 | tf_op jit(solution)/shard_map/ppermute | solution.py:567
  33.5 14.7 %collective-permute-start.5 = (f32[6,64,256]{2,1,0:T(8,128)S(1)}, f32[6,64,256]{2,1,0:T(8,128)S(1)}, u32[]{:S(2)}, u32[]{:S(2)}) collective-permute-start(f32[6,64,256]{2,1,0:T(8,128)S(1)} %edge.2.refs_1_), channel_id=1, source_target_pairs={{0,15},{1,2},{2,1},{3,4},{4,3},{5,6},{6,5},{7,8},{8,7},{9,10},{10,... | collective-permute-start | bytes 1179656 | tf_op jit(solution)/shard_map/ppermute | solution.py:567
  43.9 4.2 %copy-start.2 = (s32[63]{0:T(128)S(1)}, s32[63]{0:T(128)}, u32[]{:S(2)}) copy-start(s32[63]{0:T(128)} %slot_ref.1) | copy-start | bytes 760
  54.6 2.0 %collective-permute-start.8 = (f32[8,4,32,128]{3,2,1,0:T(8,128)S(1)}, f32[8,4,32,128]{3,2,1,0:T(8,128)S(1)}, u32[]{:S(2)}, u32[]{:S(2)}) collective-permute-start(f32[8,4,32,128]{3,2,1,0:T(8,128)S(1)} %get-tuple-element.40), channel_id=1, source_target_pairs={{0,1},{1,0},{2,3},{3,2},{4,5},{5,4},{6,7},{7,6},{8,9},{9,8},{10,11... | collective-permute-start | bytes 1572872 | tf_op jit(solution)/shard_map/ppermute | solution.py:653
  56.6 5.8 %collective-permute-start.12 = (f32[2,4,32,128]{3,2,1,0:T(8,128)S(1)}, f32[2,4,32,128]{3,2,1,0:T(8,128)S(1)}, u32[]{:S(2)}, u32[]{:S(2)}) collective-permute-start(f32[2,4,32,128]{3,2,1,0:T(8,128)S(1)} %get-tuple-element.46), channel_id=1, source_target_pairs={{0,2},{1,3},{2,0},{3,1},{4,6},{5,7},{6,4},{7,5},{8,10},{9,11},{10,... | collective-permute-start | bytes 393224 | tf_op jit(solution)/shard_map/ppermute | solution.py:662
  58.3 10.7 %collective-permute-start.10 = (f32[4,32,128]{2,1,0:T(8,128)S(1)}, f32[4,32,128]{2,1,0:T(8,128)S(1)}, u32[]{:S(2)}, u32[]{:S(2)}) collective-permute-start(f32[4,32,128]{2,1,0:T(8,128)S(1)} %get-tuple-element.43), channel_id=1, source_target_pairs={{0,4},{1,5},{2,6},{3,7},{4,0},{5,1},{6,2},{7,3},{8,12},{9,13},{10,... | collective-permute-start | bytes 196616 | tf_op jit(solution)/shard_map/ppermute | solution.py:662
  59.9 9.1 %collective-permute-start.11 = (f32[4,32,128]{2,1,0:T(8,128)S(1)}, f32[4,32,128]{2,1,0:T(8,128)S(1)}, u32[]{:S(2)}, u32[]{:S(2)}) collective-permute-start(f32[4,32,128]{2,1,0:T(8,128)S(1)} %get-tuple-element.44), channel_id=1, source_target_pairs={{0,6},{1,7},{2,4},{3,5},{4,2},{5,3},{6,0},{7,1},{8,14},{9,15},{10,... | collective-permute-start | bytes 196616 | tf_op jit(solution)/shard_map/ppermute | solution.py:662
  60.3 8.7 %collective-permute-start.9 = (f32[4,32,128]{2,1,0:T(8,128)S(1)}, f32[4,32,128]{2,1,0:T(8,128)S(1)}, u32[]{:S(2)}, u32[]{:S(2)}) collective-permute-start(f32[4,32,128]{2,1,0:T(8,128)S(1)} %get-tuple-element.42), channel_id=1, source_target_pairs={{0,2},{1,3},{2,0},{3,1},{4,6},{5,7},{6,4},{7,5},{8,10},{9,11},{10,... | collective-permute-start | bytes 196616 | tf_op jit(solution)/shard_map/ppermute | solution.py:662
  62.5 6.6 %collective-permute-start.13 = (f32[4,32,128]{2,1,0:T(8,128)S(1)}, f32[4,32,128]{2,1,0:T(8,128)S(1)}, u32[]{:S(2)}, u32[]{:S(2)}) collective-permute-start(f32[4,32,128]{2,1,0:T(8,128)S(1)} %get-tuple-element.47), channel_id=1, source_target_pairs={{0,8},{1,9},{2,10},{3,11},{4,12},{5,13},{6,14},{7,15},{8,0},{9,1},... | collective-permute-start | bytes 196616 | tf_op jit(solution)/shard_map/ppermute | solution.py:662
  66.5 6.1 %collective-permute-start.14 = (f32[4,32,128]{2,1,0:T(8,128)S(1)}, f32[4,32,128]{2,1,0:T(8,128)S(1)}, u32[]{:S(2)}, u32[]{:S(2)}) collective-permute-start(f32[4,32,128]{2,1,0:T(8,128)S(1)} %get-tuple-element.48), channel_id=1, source_target_pairs={{0,12},{1,13},{2,14},{3,15},{4,8},{5,9},{6,10},{7,11},{8,4},{9,5},... | collective-permute-start | bytes 196616 | tf_op jit(solution)/shard_map/ppermute | solution.py:662
